TPU v7x, 256 devices: a whole 4x4x8 slice. The times are simulated.
256 devices in a mesh: band: 128 (over y_lo, z, x, core), grid: 2 (over y_hi).
Axes of the slice: x: 4, y: 4 (y_hi: 2, y_lo: 2; y = y_hi * 2 + y_lo), z: 8, core: 2. Of those that a mesh axis runs over, the one named last changes fastest.
Arguments:
- orbitals: float32 [128, 80, 80, 80], P('band', 'grid'), may hold values from -6 to 6
Outputs:
- exchange_field: float32 [128, 80, 80, 80], P('band', 'grid')
All inputs are finite; a program needn't handle non-finite values.
Results may differ from a plain program's by a relative error of at most 0.0003.
Values sent between devices are 32-bit elements; how exact they have to be, the bound alone decides.
No kernel may reach another device: no remote copies, remote signals or barrier semaphores. Data moves between devices by JAX's collectives and lax.ppermute only.
A program may use at most 64 MiB of HBM per device.

v0:
```python
import functools
import math

import jax
import jax.numpy as jnp
import numpy as np
from jax import lax
from jax.experimental import pallas as pl
from jax.experimental.pallas import tpu as pltpu
from jax.sharding import PartitionSpec as P

CELL_LENGTH = 37.2
SCREENING = 0.106
BF16 = jnp.bfloat16
F32 = jnp.float32
N = 80
HALF = N // 2
GROUP = 8
GROUPS = HALF // GROUP
PLANES = 5
PACKED = (GROUPS * PLANES, N, 128)
LANES = 128
LOW, HIGH = 64, 16

FOLD = np.concatenate([np.arange(HALF), [HALF], np.arange(N - 1, HALF, -1)])


def cas(rows, columns):
    angles = (rows[:, None] * columns[None, :] % N) * (2.0 * math.pi / N)
    return np.cos(angles) + np.sin(angles)


def three_terms(table):
    high = table.astype(np.float32).astype(jnp.bfloat16)
    low = (table - high.astype(np.float64)).astype(np.float32).astype(jnp.bfloat16)
    return np.concatenate([high, high, low], axis=1)


def tables():
    places = np.arange(N)
    return (
        three_terms(cas(places, places)),
        three_terms(cas(FOLD, places)),
        three_terms(cas(places, FOLD)),
    )


def screened_kernel():
    line = np.arange(N)
    freq_y = np.pad(np.where(2 * line >= N, line - N, line), (0, LANES - N))[None, None, None, :]
    freq_x = np.arange(HALF + 1)[None, :, None, None]
    freq_z = np.concatenate([np.arange(HALF + 1), np.arange(1, GROUP)]).reshape(6, 1, GROUP, 1)
    squares = freq_x * freq_x + freq_y * freq_y + freq_z * freq_z
    wave_square = np.where(squares == 0, 1, squares) * (2.0 * math.pi / CELL_LENGTH) ** 2
    shaped = 4.0 * math.pi / wave_square * (1.0 - np.exp(-wave_square / (4.0 * SCREENING**2)))
    return (np.where(squares == 0, math.pi / SCREENING**2, shaped) * (1.0 / N**3)).astype(np.float32)


def point(n1, n2):
    return (5 * n1 + 16 * n2) % N


def frequency(k1, k2):
    k = next(k for k in range(N) if k % 16 == k1 and k % 5 == k2)
    return min(k, N - k)


def turn(re, im, k, n, sign):
    if k == 0:
        return re, im
    if 4 * k == n:
        return (-im, re) if sign > 0 else (im, -re)
    c, s = math.cos(2 * math.pi * k / n), sign * math.sin(2 * math.pi * k / n)
    if 8 * k == n:
        return c * (re - sign * im), c * (im + sign * re)
    if 8 * k == 3 * n:
        return c * (re + sign * im), c * (im - sign * re)
    return c * re - s * im, c * im + s * re


def real_transform(x):
    n = len(x)
    if n == 2:
        return [(x[0] + x[1], None), (x[0] - x[1], None)]
    even, odd = real_transform(x[0::2]), real_transform(x[1::2])
    out = [None] * (n // 2 + 1)
    out[0] = (even[0][0] + odd[0][0], None)
    out[n // 2] = (even[0][0] - odd[0][0], None)
    out[n // 4] = (even[n // 4][0], -odd[n // 4][0])
    for k in range(1, n // 4):
        re, im = turn(*odd[k], k, n, -1)
        out[k] = (even[k][0] + re, even[k][1] + im)
        out[n // 2 - k] = (even[k][0] - re, im - even[k][1])
    return out


def real_inverse(spectrum):
    n = 2 * (len(spectrum) - 1)
    if n == 2:
        return [spectrum[0][0] + spectrum[1][0], spectrum[0][0] - spectrum[1][0]]
    even, odd = [None] * (n // 4 + 1), [None] * (n // 4 + 1)
    even[0] = (spectrum[0][0] + spectrum[n // 2][0], None)
    odd[0] = (spectrum[0][0] - spectrum[n // 2][0], None)
    even[n // 4] = (2.0 * spectrum[n // 4][0], None)
    odd[n // 4] = (-2.0 * spectrum[n // 4][1], None)
    for k in range(1, n // 4):
        (re, im), (re_far, im_far) = spectrum[k], spectrum[n // 2 - k]
        even[k] = (re + re_far, im - im_far)
        odd[k] = turn(re - re_far, im + im_far, k, n, 1)
    out = [None] * n
    out[0::2], out[1::2] = real_inverse(even), real_inverse(odd)
    return out


C1, C2 = math.cos(2 * math.pi / 5), math.cos(4 * math.pi / 5)
S1, S2 = math.sin(2 * math.pi / 5), math.sin(4 * math.pi / 5)


def five_parts(x):
    t1, t2, t3, t4 = x[1] + x[4], x[2] + x[3], x[1] - x[4], x[2] - x[3]
    return (
        x[0] + t1 + t2,
        x[0] + C1 * t1 + C2 * t2,
        x[0] + C2 * t1 + C1 * t2,
        S1 * t3 + S2 * t4,
        S2 * t3 - S1 * t4,
    )


def five_real(x, kernel):
    zero, a1, a2, b1, b2 = five_parts(x)
    zero, a1, a2, b1, b2 = kernel[0] * zero, 2.0 * kernel[1] * a1, 2.0 * kernel[2] * a2, 2.0 * kernel[1] * b1, 2.0 * kernel[2] * b2
    m1, m2 = zero + C1 * a1 + C2 * a2, zero + C2 * a1 + C1 * a2
    n1, n2 = S1 * b1 + S2 * b2, S2 * b1 - S1 * b2
    return [zero + a1 + a2, m1 + n1, m2 + n2, m2 - n2, m1 - n1]


def five_complex(re, im, kernel):
    r0, ra1, ra2, rb1, rb2 = five_parts(re)
    i0, ia1, ia2, ib1, ib2 = five_parts(im)
    r = [kernel[0] * r0, kernel[1] * (ra1 + ib1), kernel[2] * (ra2 + ib2), kernel[3] * (ra2 - ib2), kernel[4] * (ra1 - ib1)]
    i = [kernel[0] * i0, kernel[1] * (ia1 - rb1), kernel[2] * (ia2 - rb2), kernel[3] * (ia2 + rb2), kernel[4] * (ia1 + rb1)]
    r0, ra1, ra2, rb1, rb2 = five_parts(r)
    i0, ia1, ia2, ib1, ib2 = five_parts(i)
    return (
        [r0, ra1 - ib1, ra2 - ib2, ra2 + ib2, ra1 + ib1],
        [i0, ia1 + rb1, ia2 + rb2, ia2 - rb2, ia1 - rb1],
    )


def times(table, data):
    high = data.astype(BF16)
    low = (data - high.astype(F32)).astype(BF16)
    stacked = jnp.concatenate([high, low, high], axis=0)
    return lax.dot_general(table, stacked, (((1,), (0,)), ((), ())), preferred_element_type=F32)


def piece(data, index):
    return data[:, LANES * index : LANES * (index + 1)]


def unit_body(near_a, near_b, far_a, far_b, table_y, table_to, table_from, kernel, total, out, there, back, mid, turned):
    fill = jnp.zeros((LANES - N, LANES), F32)

    def forward_y(a, b, first, group):
        start = group * PLANES
        density = jnp.concatenate([a[start + i] * b[start + i] for i in range(PLANES)], axis=1)
        along_y = times(table_y[...], density)
        for i in range(PLANES):
            turned[first + start + i] = jnp.concatenate([piece(along_y, i), fill], axis=0).T

    def forward_z(group):
        start = group * PLANES
        rows = [
            jnp.concatenate(
                [
                    turned[start + j // 2, LOW * (j % 2) : LOW * (j % 2) + LOW],
                    turned[start + 4, HIGH * j : HIGH * (j + 1)],
                ],
                axis=0,
            )
            for j in range(GROUP)
        ]
        along_z = times(table_to[...], jnp.concatenate(rows, axis=1))
        for j in range(GROUP):
            there[group * GROUP + j] = piece(along_z, j)

    def middle(group, kernel_group):
        rows = pl.ds(pl.multiple_of(group * GROUP, GROUP), GROUP)
        for n2 in range(5):
            for k1, (re, im) in enumerate(real_transform([there[point(n1, n2), rows, :] for n1 in range(16)])):
                mid[2 * k1, n2] = re
                if im is not None:
                    mid[2 * k1 + 1, n2] = im
        for k1 in range(9):
            scale = [kernel[kernel_group, frequency(k1, k2)] for k2 in range(5)]
            re = [mid[2 * k1, n2] for n2 in range(5)]
            if k1 in (0, 8):
                re = five_real(re, scale)
            else:
                re, im = five_complex(re, [mid[2 * k1 + 1, n2] for n2 in range(5)], scale)
                for n2 in range(5):
                    mid[2 * k1 + 1, n2] = im[n2]
            for n2 in range(5):
                mid[2 * k1, n2] = re[n2]
        for n2 in range(5):
            spectrum = [(mid[2 * k1, n2], None if k1 in (0, 8) else mid[2 * k1 + 1, n2]) for k1 in range(9)]
            for n1, value in enumerate(real_inverse(spectrum)):
                if point(n1, n2) < HALF:
                    back[point(n1, n2), rows, :] = value

    def backward_z(group):
        rows = [back[group * GROUP + j] for j in range(GROUP)]
        along_z = times(table_from[...], jnp.concatenate(rows, axis=1))
        parts = [piece(along_z, j) for j in range(GROUP)]
        packed = [jnp.concatenate([parts[2 * i][:LOW], parts[2 * i + 1][:LOW]], axis=0) for i in range(4)]
        packed.append(jnp.concatenate([part[LOW:] for part in parts], axis=0))
        for i, plane in enumerate(packed):
            turned[group * PLANES + i] = plane.T

    def backward_y(group):
        start = group * PLANES
        planes = jnp.concatenate([turned[start + i, :N] for i in range(PLANES)], axis=1)
        potential = times(table_y[...], planes)
        for i in range(PLANES):
            term = piece(potential, i) * near_b[start + i]
            out[start + i] = term if total is None else total[start + i] + term

    for group in range(GROUPS):
        forward_y(near_a, near_b, 0, group)
        forward_y(far_a, far_b, GROUPS * PLANES, group)
    for group in range(2 * GROUPS):
        forward_z(group)

    @pl.loop(0, 2 * GROUPS)
    def _(group):
        middle(group, jnp.where(group > GROUPS, group - GROUPS, group))

    for group in range(GROUPS):
        backward_z(group)
    for group in range(GROUPS):
        backward_y(group)


def unit(a, b, constants, total=None):
    operands = [a[0], b[0], a[1], b[1], *constants]

    def body(*refs):
        ins, rest = refs[: len(operands)], refs[len(operands) :]
        if total is None:
            unit_body(*ins, None, *rest)
        else:
            unit_body(*ins, *rest)

    return pl.pallas_call(
        body,
        out_shape=jax.ShapeDtypeStruct(PACKED, F32),
        scratch_shapes=[pltpu.VMEM((N, N, LANES), F32), pltpu.VMEM((HALF, N, LANES), F32), pltpu.VMEM((17, 5, GROUP, LANES), F32), pltpu.VMEM((2 * GROUPS * PLANES, LANES, LANES), F32)],
        compiler_params=pltpu.CompilerParams(vmem_limit_bytes=20 * 2**20),
        cost_estimate=pl.CostEstimate(flops=10**9, bytes_accessed=2**20, transcendentals=0),
        name="unit",
    )(*operands, *(() if total is None else (total,)))


def pack_body(data, out):
    lane = lax.broadcasted_iota(jnp.int32, (N, LANES), 1)
    pad = jnp.zeros((N, LANES - N), F32)

    @pl.loop(0, GROUPS)
    def _(group):
        last = None
        for i in range(4):
            pair = [jnp.concatenate([data[group * GROUP + 2 * i + h], pad], axis=1) for h in range(2)]
            out[group * PLANES + i] = jnp.where(lane < LOW, pair[0], pltpu.roll(pair[1], LOW, 1))
            for h in range(2):
                place = HIGH * (2 * i + h)
                moved = pltpu.roll(pair[h], (place - LOW) % LANES, 1) if place != LOW else pair[h]
                last = moved if last is None else jnp.where(lane >= place, moved, last)
        out[group * PLANES + 4] = last


def pack(data):
    return pl.pallas_call(
        pack_body,
        out_shape=jax.ShapeDtypeStruct(PACKED, F32),
        compiler_params=pltpu.CompilerParams(vmem_limit_bytes=16 * 2**20),
        name="pack",
    )(data)


def unpack_body(total, returned, theirs, out):
    lane = lax.broadcasted_iota(jnp.int32, (N, LANES), 1)

    @pl.loop(0, GROUPS)
    def _(group):
        start = group * PLANES
        planes = [total[start + i] + returned[start + i] + theirs[start + i] for i in range(PLANES)]
        for j in range(GROUP):
            low = planes[j // 2] if j % 2 == 0 else pltpu.roll(planes[j // 2], LOW, 1)
            place = HIGH * j
            high = pltpu.roll(planes[4], (LOW - place) % LANES, 1) if place != LOW else planes[4]
            out[group * GROUP + j] = jnp.where(lane < LOW, low, high)[:, :N]


def unpack_sum(total, returned, theirs):
    return pl.pallas_call(
        unpack_body,
        out_shape=jax.ShapeDtypeStruct((HALF, N, N), F32),
        compiler_params=pltpu.CompilerParams(vmem_limit_bytes=16 * 2**20),
        name="unpack_sum",
    )(total, returned, theirs)


def shards(orbitals):
    bands = lax.axis_size("band")
    half = bands // 2
    place = lax.axis_index("band")
    sides = [1 if b % 2 else -1 for b in range(bands)]

    def sources(distance):
        return [(b + distance * sides[b]) % bands for b in range(bands)]

    def crosses(b, source):
        return b // half != source // half

    def holds(places):
        return functools.reduce(jnp.logical_or, [place == p for p in places])

    def from_place(data, distance):
        return lax.ppermute(data, "band", [(source, b) for b, source in enumerate(sources(distance))])

    def near_inside(data, distance):
        return lax.ppermute(
            data, "band", [(source, b) for b, source in enumerate(sources(distance)) if not crosses(b, source)]
        )

    def near_across(data, distance):
        route = [(source, b) for b, source in enumerate(sources(distance)) if crosses(b, source)]
        return lax.ppermute(data, "band", route), holds([b for _, b in route])

    def far_route(distance):
        route, across = [], []
        for b, source in enumerate(sources(distance)):
            cross = crosses(b, source)
            if cross:
                across.append(source)
            for slab in range(2):
                route.append((2 * source + (1 - slab if cross else slab), 2 * b + slab))
        return route, holds(across)

    def other_core(data):
        return from_place(data, -1)

    constants = tuple(jnp.asarray(t) for t in (*tables(), screened_kernel()))
    near = pack(orbitals[0])
    far = lax.ppermute(near, "grid", [(0, 1), (1, 0)])
    m2_inside = near_inside(near, -2)
    p2_inside = near_inside(near, 2)
    near_later, far, m2_inside, p2_inside = lax.optimization_barrier((near, far, m2_inside, p2_inside))
    own = (near, far)
    m2_route, m2_across = far_route(-2)
    p2_route, p2_across = far_route(2)
    m2_sent = jnp.where(m2_across, near, far)
    p2_sent = jnp.where(p2_across, near, far)
    m2_far = lax.ppermute(m2_sent, ("band", "grid"), m2_route)
    m2_crossed, m2_takes = near_across(near_later, -2)
    m1 = (other_core(near), other_core(far))
    total = unit(own, m1, constants)
    p2_sent, m2_inside, total = lax.optimization_barrier((p2_sent, m2_inside, total))
    p2_far = lax.ppermute(p2_sent, ("band", "grid"), p2_route)
    p2_crossed, p2_takes = near_across(near_later, 2)
    m2_near = jnp.where(m2_takes, m2_crossed, m2_inside)
    p1_near = other_core(m2_near)
    m2_far, p1_near, total = lax.optimization_barrier((m2_far, p1_near, total))
    m2 = (m2_near, m2_far)
    p1_far = other_core(m2_far)
    total = unit(own, m2, constants, total)
    p1_near, total = lax.optimization_barrier((p1_near, total))
    lent = unit(m2, (p1_near, p1_far), constants)
    returned = from_place(lent, 2)
    m2_near, lent = lax.optimization_barrier((m2_near, lent))
    partner = unit(m1, (m2_near, m2_far), constants)
    p2_far, p2_inside, partner, total = lax.optimization_barrier((p2_far, p2_inside, partner, total))
    p2 = (jnp.where(p2_takes, p2_crossed, p2_inside), p2_far)
    partner = unit(m1, p2, constants, partner)
    theirs = other_core(partner)
    total, partner = lax.optimization_barrier((total, partner))
    total = unit(own, p2, constants, total)
    return unpack_sum(total, returned, theirs)[None]


def solution(mesh):
    spec = P("band", "grid", None, None)
    return jax.shard_map(shards, mesh=mesh, in_specs=(spec,), out_specs=spec, check_vma=False)
```

profile of v0, /device:TPU:1, one launch (start us, length us, event | category | flops | bytes accessed | tf_op | source)
XLA Modules:
  0.0 127.0 jit_solution(15879902668925940017)
XLA Ops:
  0.0 1.4 %copy-done.6 = f32[1,40,80,80]{3,2,1,0:T(8,128)S(1)} copy-done((f32[1,40,80,80]{3,2,1,0:T(8,128)S(1)}, f32[1,40,80,80]{3,2,1,0:T(8,128)}, u32[]{:S(2)}) %copy-start.6) | copy-done | bytes 1024024
  1.4 0.9 pack.1.refs_0_
  2.4 3.8 %collective-permute-start = (f32[25,80,128]{2,1,0:T(8,128)S(1)}, f32[25,80,128]{2,1,0:T(8,128)S(1)}, u32[]{:S(2)}, u32[]{:S(2)}) collective-permute-start(f32[25,80,128]{2,1,0:T(8,128)S(1)} %pack.1.refs_0_), channel_id=1, source_target_pairs={{0,1},{1,0},{2,3},{3,2},{4,5},{5,4},{6,7},{7,6},{8,9},{9,8},{10,11... | collective-permute-start | bytes 3072008 | tf_op jit(solution)/shard_map/ppermute | solution.py:356
  6.2 3.2 %collective-permute-start.1 = (f32[25,80,128]{2,1,0:T(8,128)S(1)}, f32[25,80,128]{2,1,0:T(8,128)S(1)}, u32[]{:S(2)}, u32[]{:S(2)}) collective-permute-start(f32[25,80,128]{2,1,0:T(8,128)S(1)} %pack.1.refs_0_), channel_id=1, source_target_pairs={{4,0},{8,4},{2,6},{12,8},{6,10},{16,12},{10,14},{20,16},{14,18},{2... | collective-permute-start | bytes 3072008 | tf_op jit(solution)/shard_map/ppermute | solution.py:333
  9.4 1.3 %collective-permute-start.2 = (f32[25,80,128]{2,1,0:T(8,128)S(1)}, f32[25,80,128]{2,1,0:T(8,128)S(1)}, u32[]{:S(2)}, u32[]{:S(2)}) collective-permute-start(f32[25,80,128]{2,1,0:T(8,128)S(1)} %pack.1.refs_0_), channel_id=1, source_target_pairs={{6,2},{0,4},{10,6},{4,8},{14,10},{8,12},{18,14},{12,16},{22,18},{1... | collective-permute-start | bytes 3072008 | tf_op jit(solution)/shard_map/ppermute | solution.py:333
  10.7 2.5 %collective-permute-start.4 = (f32[25,80,128]{2,1,0:T(8,128)S(1)}, f32[25,80,128]{2,1,0:T(8,128)}, u32[]{:S(2)}, u32[]{:S(2)}) collective-permute-start(f32[25,80,128]{2,1,0:T(8,128)S(1)} %pack.1.refs_0_), channel_id=1, source_target_pairs={{2,0},{0,2},{6,4},{4,6},{10,8},{8,10},{14,12},{12,14},{18,16},{16,... | collective-permute-start | bytes 3072008 | tf_op jit(solution)/shard_map/ppermute | solution.py:330
  13.1 14.4 %collective-permute-done.refs_2_ = f32[25,80,128]{2,1,0:T(8,128)S(1)} collective-permute-done((f32[25,80,128]{2,1,0:T(8,128)S(1)}, f32[25,80,128]{2,1,0:T(8,128)S(1)}, u32[]{:S(2)}, u32[]{:S(2)}) %collective-permute-start) | collective-permute-done | bytes 1024032 | tf_op jit(solution)/shard_map/ppermute | solution.py:356
  27.5 0.3 collective-permute-done.1
  27.8 6.0 %collective-permute-done.2 = f32[25,80,128]{2,1,0:T(8,128)S(1)} collective-permute-done((f32[25,80,128]{2,1,0:T(8,128)S(1)}, f32[25,80,128]{2,1,0:T(8,128)S(1)}, u32[]{:S(2)}, u32[]{:S(2)}) %collective-permute-start.2) | collective-permute-done | bytes 1024032 | tf_op jit(solution)/shard_map/ppermute | solution.py:333
  33.8 1.0 copy-done.12
  34.8 0.0 collective-permute-start.5
  34.8 1.3 %collective-permute-start.7 = (f32[25,80,128]{2,1,0:T(8,128)S(1)}, f32[25,80,128]{2,1,0:T(8,128)}, u32[]{:S(2)}, u32[]{:S(2)}) collective-permute-start(f32[25,80,128]{2,1,0:T(8,128)S(1)} %pack.1.refs_0_), channel_id=1, source_target_pairs={{254,2},{128,124},{126,130},{0,252},{255,3},{129,125},{127,131},{1... | collective-permute-start | bytes 3072008 | tf_op jit(solution)/shard_map/ppermute | solution.py:339
  36.1 0.0 copy-start
  36.1 0.0 copy-start.7
  36.2 0.0 copy-start.8
  36.2 0.0 copy-start.9
  36.2 1.1 broadcast_select_fusion
  37.3 1.5 %collective-permute-start.8 = (f32[25,80,128]{2,1,0:T(8,128)S(1)}, f32[25,80,128]{2,1,0:T(8,128)}, u32[]{:S(2)}, u32[]{:S(2)}) collective-permute-start(f32[25,80,128]{2,1,0:T(8,128)S(1)} %get-tuple-element.41), channel_id=1, source_target_pairs={{4,0},{5,1},{255,2},{254,3},{8,4},{9,5},{2,6},{3,7},{12,8},{13,9},... | collective-permute-start | bytes 3072008 | tf_op jit(solution)/shard_map/ppermute | solution.py:365
  38.8 0.0 collective-permute-done.4.refs_1_.refs_0_
  38.8 0.0 collective-permute-done.5.refs_3_.refs_2_
  38.8 0.0 copy-done
  38.8 6.5 %unit.6.refs_8_ = f32[25,80,128]{2,1,0:T(8,128)S(1)} custom-call(f32[25,80,128]{2,1,0:T(8,128)S(1)} %pack.1.refs_0_, f32[25,80,128]{2,1,0:T(8,128)} %collective-permute-done.4.refs_1_.refs_0_, f32[25,80,128]{2,1,0:T(8,128)S(1)} %collective-permute-done.refs_2_, f32[25,80,128]{2,1,0:T(8,128)} %collective-permute-done.5.refs_3_.refs_2_, ...), custom_call_target="tpu_custom_call" | custom-call | flops 1000000000 | bytes 1048576 | tf_op jit(solution)/shard_map/unit/pallas_call | solution.py:255
  45.3 10.0 %collective-permute-done.7 = f32[25,80,128]{2,1,0:T(8,128)} collective-permute-done((f32[25,80,128]{2,1,0:T(8,128)S(1)}, f32[25,80,128]{2,1,0:T(8,128)}, u32[]{:S(2)}, u32[]{:S(2)}) %collective-permute-start.7) | collective-permute-done | bytes 1024032 | tf_op jit(solution)/shard_map/ppermute | solution.py:339
  55.3 1.3 %broadcast_select_fusion.1.refs_1_.refs_0_ = f32[25,80,128]{2,1,0:T(8,128)S(1)} fusion(f32[25,80,128]{2,1,0:T(8,128)} %collective-permute-done.7, f32[25,80,128]{2,1,0:T(8,128)S(1)} %copy-done.15, pred[]{:T(512)S(6)} %or.44), kind=kLoop, calls=%fused_computation.1 | loop fusion | flops 256000 | bytes 3072001 | tf_op jit(solution)/shard_map/jit(_where)/select_n | solution.py:372
  56.6 0.1 collective-permute-start.9
  56.7 1.0 copy-done.1
  57.7 8.9 %collective-permute-done.8.refs_3_.refs_2_ = f32[25,80,128]{2,1,0:T(8,128)} collective-permute-done((f32[25,80,128]{2,1,0:T(8,128)S(1)}, f32[25,80,128]{2,1,0:T(8,128)}, u32[]{:S(2)}, u32[]{:S(2)}) %collective-permute-start.8) | collective-permute-done | bytes 1024032 | tf_op jit(solution)/shard_map/ppermute | solution.py:365
  66.7 0.0 collective-permute-done.9.refs_1_
  66.7 1.1 copy-done.10
  67.7 0.5 collective-permute-start.10
  68.2 7.7 %collective-permute-start.6 = (f32[25,80,128]{2,1,0:T(8,128)}, f32[25,80,128]{2,1,0:T(8,128)}, u32[]{:S(2)}, u32[]{:S(2)}) collective-permute-start(f32[25,80,128]{2,1,0:T(8,128)} %get-tuple-element.26), channel_id=1, source_target_pairs={{253,0},{252,1},{6,2},{7,3},{0,4},{1,5},{10,6},{11,7},{4,8},{5,9},... | collective-permute-start | bytes 3072008 | tf_op jit(solution)/shard_map/ppermute | solution.py:370
  76.0 2.3 %collective-permute-start.3 = (f32[25,80,128]{2,1,0:T(8,128)S(1)}, f32[25,80,128]{2,1,0:T(8,128)}, u32[]{:S(2)}, u32[]{:S(2)}) collective-permute-start(f32[25,80,128]{2,1,0:T(8,128)S(1)} %pack.1.refs_0_), channel_id=1, source_target_pairs={{252,0},{130,126},{124,128},{2,254},{253,1},{131,127},{125,129},{3... | collective-permute-start | bytes 3072008 | tf_op jit(solution)/shard_map/ppermute | solution.py:339
  78.2 1.2 copy-done.2
  79.4 1.2 copy-done.5
  80.7 6.3 %unit.7.refs_8_ = f32[25,80,128]{2,1,0:T(8,128)S(1)} custom-call(f32[25,80,128]{2,1,0:T(8,128)S(1)} %pack.1.refs_0_, f32[25,80,128]{2,1,0:T(8,128)S(1)} %copy-done.2, f32[25,80,128]{2,1,0:T(8,128)S(1)} %collective-permute-done.refs_2_, f32[25,80,128]{2,1,0:T(8,128)} %collective-permute-done.8.refs_3_.refs_2_, bf16[80,240]{1,0:T(8,128)(2,1)S(1)} %copy-done.7, ...), custom_call_target="tpu_custom_call" | custom-call | flops 1000000000 | bytes 1048576 | tf_op jit(solution)/shard_map/unit/pallas_call | solution.py:255
  87.0 0.0 collective-permute-done.10.refs_3_
  87.0 6.5 %unit.8 = f32[25,80,128]{2,1,0:T(8,128)S(1)} custom-call(f32[25,80,128]{2,1,0:T(8,128)S(1)} %copy-done.3, f32[25,80,128]{2,1,0:T(8,128)S(1)} %copy-done.11, f32[25,80,128]{2,1,0:T(8,128)} %collective-permute-done.8.refs_3_.refs_2_, f32[25,80,128]{2,1,0:T(8,128)} %collective-permute-done.10.refs_3_, bf16[80,240]{1,0:T(8,128)(2,1)S(1)} %copy-done.7, ...), custom_call_target="tpu_custom_call" | custom-call | flops 1000000000 | bytes 1048576 | tf_op jit(solution)/shard_map/unit/pallas_call | solution.py:255
  93.5 6.9 %unit.9.refs_8_ = f32[25,80,128]{2,1,0:T(8,128)S(1)} custom-call(f32[25,80,128]{2,1,0:T(8,128)} %collective-permute-done.4.refs_1_.refs_0_, f32[25,80,128]{2,1,0:T(8,128)S(1)} %copy-done.3, f32[25,80,128]{2,1,0:T(8,128)} %collective-permute-done.5.refs_3_.refs_2_, f32[25,80,128]{2,1,0:T(8,128)} %collective-permute-done.8.refs_3_.refs_2_, ...), custom_call_target="tpu_custom_call" | custom-call | flops 1000000000 | bytes 1048576 | tf_op jit(solution)/shard_map/unit/pallas_call | solution.py:255
  100.4 0.0 collective-permute-done.6.refs_3_
  100.4 0.0 collective-permute-done.3
  100.4 0.1 broadcast_select_fusion.3.refs_1_
  100.5 6.8 %unit.10 = f32[25,80,128]{2,1,0:T(8,128)S(1)} custom-call(f32[25,80,128]{2,1,0:T(8,128)} %collective-permute-done.4.refs_1_.refs_0_, f32[25,80,128]{2,1,0:T(8,128)S(1)} %broadcast_select_fusion.3.refs_1_, f32[25,80,128]{2,1,0:T(8,128)} %collective-permute-done.5.refs_3_.refs_2_, f32[25,80,128]{2,1,0:T(8,128)} %collective-permute-done.6.refs_3_, ...), custom_call_target="tpu_custom_call" | custom-call | flops 1000000000 | bytes 1048576 | tf_op jit(solution)/shard_map/unit/pallas_call | solution.py:255
  107.3 0.1 collective-permute-start.12
  107.4 6.0 %collective-permute-start.11 = (f32[25,80,128]{2,1,0:T(8,128)S(1)}, f32[25,80,128]{2,1,0:T(8,128)S(1)}, u32[]{:S(2)}, u32[]{:S(2)}) collective-permute-start(f32[25,80,128]{2,1,0:T(8,128)S(1)} %unit.8), channel_id=1, source_target_pairs={{252,0},{6,2},{0,4},{10,6},{4,8},{14,10},{8,12},{18,14},{12,16},{2... | collective-permute-start | bytes 3072008 | tf_op jit(solution)/shard_map/ppermute | solution.py:330
  113.4 6.2 %unit.11.total = f32[25,80,128]{2,1,0:T(8,128)S(1)} custom-call(f32[25,80,128]{2,1,0:T(8,128)S(1)} %pack.1.refs_0_, f32[25,80,128]{2,1,0:T(8,128)S(1)} %broadcast_select_fusion.3.refs_1_, f32[25,80,128]{2,1,0:T(8,128)S(1)} %collective-permute-done.refs_2_, f32[25,80,128]{2,1,0:T(8,128)} %collective-permute-done.6.refs_3_, bf16[80,240]{1,0:T(8,128)(2,1)S(1)} %copy-done.7, ...), custom_call_target="tpu_custom_call" | custom-call | flops 1000000000 | bytes 1048576 | tf_op jit(solution)/shard_map/unit/pallas_call | solution.py:255
  119.6 0.0 collective-permute-done.12.theirs
  119.6 5.3 %collective-permute-done.11.returned = f32[25,80,128]{2,1,0:T(8,128)S(1)} collective-permute-done((f32[25,80,128]{2,1,0:T(8,128)S(1)}, f32[25,80,128]{2,1,0:T(8,128)S(1)}, u32[]{:S(2)}, u32[]{:S(2)}) %collective-permute-start.11) | collective-permute-done | bytes 1024032 | tf_op jit(solution)/shard_map/ppermute | solution.py:330
  124.9 2.1 %unpack_sum.1 = f32[40,80,80]{2,1,0:T(8,128)} custom-call(f32[25,80,128]{2,1,0:T(8,128)S(1)} %unit.11.total, f32[25,80,128]{2,1,0:T(8,128)S(1)} %collective-permute-done.11.returned, f32[25,80,128]{2,1,0:T(8,128)S(1)} %collective-permute-done.12.theirs), custom_call_target="tpu_custom_call" | custom-call | tf_op jit(solution)/shard_map/unpack_sum/pallas_call | solution.py:306
  (21 shorter events, 0.0 us)
Async XLA Ops:
  0.0 1.4 %copy-start.6 = (f32[1,40,80,80]{3,2,1,0:T(8,128)S(1)}, f32[1,40,80,80]{3,2,1,0:T(8,128)}, u32[]{:S(2)}) copy-start(f32[1,40,80,80]{3,2,1,0:T(8,128)} %param.5) | copy-start | bytes 3072004
  2.4 25.1 %collective-permute-start = (f32[25,80,128]{2,1,0:T(8,128)S(1)}, f32[25,80,128]{2,1,0:T(8,128)S(1)}, u32[]{:S(2)}, u32[]{:S(2)}) collective-permute-start(f32[25,80,128]{2,1,0:T(8,128)S(1)} %pack.1.refs_0_), channel_id=1, source_target_pairs={{0,1},{1,0},{2,3},{3,2},{4,5},{5,4},{6,7},{7,6},{8,9},{9,8},{10,11... | collective-permute-start | bytes 3072008 | tf_op jit(solution)/shard_map/ppermute | solution.py:356
  6.2 21.6 %collective-permute-start.1 = (f32[25,80,128]{2,1,0:T(8,128)S(1)}, f32[25,80,128]{2,1,0:T(8,128)S(1)}, u32[]{:S(2)}, u32[]{:S(2)}) collective-permute-start(f32[25,80,128]{2,1,0:T(8,128)S(1)} %pack.1.refs_0_), channel_id=1, source_target_pairs={{4,0},{8,4},{2,6},{12,8},{6,10},{16,12},{10,14},{20,16},{14,18},{2... | collective-permute-start | bytes 3072008 | tf_op jit(solution)/shard_map/ppermute | solution.py:333
  9.4 24.5 %collective-permute-start.2 = (f32[25,80,128]{2,1,0:T(8,128)S(1)}, f32[25,80,128]{2,1,0:T(8,128)S(1)}, u32[]{:S(2)}, u32[]{:S(2)}) collective-permute-start(f32[25,80,128]{2,1,0:T(8,128)S(1)} %pack.1.refs_0_), channel_id=1, source_target_pairs={{6,2},{0,4},{10,6},{4,8},{14,10},{8,12},{18,14},{12,16},{22,18},{1... | collective-permute-start | bytes 3072008 | tf_op jit(solution)/shard_map/ppermute | solution.py:333
  10.7 28.1 %collective-permute-start.4 = (f32[25,80,128]{2,1,0:T(8,128)S(1)}, f32[25,80,128]{2,1,0:T(8,128)}, u32[]{:S(2)}, u32[]{:S(2)}) collective-permute-start(f32[25,80,128]{2,1,0:T(8,128)S(1)} %pack.1.refs_0_), channel_id=1, source_target_pairs={{2,0},{0,2},{6,4},{4,6},{10,8},{8,10},{14,12},{12,14},{18,16},{16,... | collective-permute-start | bytes 3072008 | tf_op jit(solution)/shard_map/ppermute | solution.py:330
  27.8 7.0 %copy-start.14 = (f32[25,80,128]{2,1,0:T(8,128)}, f32[25,80,128]{2,1,0:T(8,128)S(1)}, u32[]{:S(2)}) copy-start(f32[25,80,128]{2,1,0:T(8,128)S(1)} %collective-permute-done.1) | copy-start | bytes 3072004
  33.8 1.0 copy-start.12
  34.8 4.0 %collective-permute-start.5 = (f32[25,80,128]{2,1,0:T(8,128)S(1)}, f32[25,80,128]{2,1,0:T(8,128)}, u32[]{:S(2)}, u32[]{:S(2)}) collective-permute-start(f32[25,80,128]{2,1,0:T(8,128)S(1)} %collective-permute-done.refs_2_), channel_id=1, source_target_pairs={{2,0},{0,2},{6,4},{4,6},{10,8},{8,10},{14,12},{12,14},{18,16},{16,... | collective-permute-start | bytes 3072008 | tf_op jit(solution)/shard_map/ppermute | solution.py:330
  34.8 20.4 %collective-permute-start.7 = (f32[25,80,128]{2,1,0:T(8,128)S(1)}, f32[25,80,128]{2,1,0:T(8,128)}, u32[]{:S(2)}, u32[]{:S(2)}) collective-permute-start(f32[25,80,128]{2,1,0:T(8,128)S(1)} %pack.1.refs_0_), channel_id=1, source_target_pairs={{254,2},{128,124},{126,130},{0,252},{255,3},{129,125},{127,131},{1... | collective-permute-start | bytes 3072008 | tf_op jit(solution)/shard_map/ppermute | solution.py:339
  36.1 2.6 %copy-start = (f32[6,41,8,128]{3,2,1,0:T(8,128)S(1)}, f32[6,41,8,128]{3,2,1,0:T(8,128)}, u32[]{:S(2)}) copy-start(f32[6,41,8,128]{3,2,1,0:T(8,128)} %constant.33.clone.refs_7_) | copy-start | bytes 3022852
  36.1 2.6 %copy-start.7 = (bf16[80,240]{1,0:T(8,128)(2,1)S(1)}, bf16[80,240]{1,0:T(8,128)(2,1)}, u32[]{:S(2)}) copy-start(bf16[80,240]{1,0:T(8,128)(2,1)} %constant.30.clone.refs_4_) | copy-start | bytes 115204
  36.2 2.6 %copy-start.8 = (bf16[80,240]{1,0:T(8,128)(2,1)S(1)}, bf16[80,240]{1,0:T(8,128)(2,1)}, u32[]{:S(2)}) copy-start(bf16[80,240]{1,0:T(8,128)(2,1)} %constant.31.clone.refs_5_) | copy-start | bytes 115204
  36.2 2.6 %copy-start.9 = (bf16[80,240]{1,0:T(8,128)(2,1)S(1)}, bf16[80,240]{1,0:T(8,128)(2,1)}, u32[]{:S(2)}) copy-start(bf16[80,240]{1,0:T(8,128)(2,1)} %constant.32.clone.refs_6_) | copy-start | bytes 115204
  37.3 18.0 %copy-start.15 = (f32[25,80,128]{2,1,0:T(8,128)S(1)}, f32[25,80,128]{2,1,0:T(8,128)}, u32[]{:S(2)}) copy-start(f32[25,80,128]{2,1,0:T(8,128)} %copy-done.14) | copy-start | bytes 3072004
  37.3 29.4 %collective-permute-start.8 = (f32[25,80,128]{2,1,0:T(8,128)S(1)}, f32[25,80,128]{2,1,0:T(8,128)}, u32[]{:S(2)}, u32[]{:S(2)}) collective-permute-start(f32[25,80,128]{2,1,0:T(8,128)S(1)} %get-tuple-element.41), channel_id=1, source_target_pairs={{4,0},{5,1},{255,2},{254,3},{8,4},{9,5},{2,6},{3,7},{12,8},{13,9},... | collective-permute-start | bytes 3072008 | tf_op jit(solution)/shard_map/ppermute | solution.py:365
  45.3 22.9 %copy-start.4 = (f32[25,80,128]{2,1,0:T(8,128)}, f32[25,80,128]{2,1,0:T(8,128)S(1)}, u32[]{:S(2)}) copy-start(f32[25,80,128]{2,1,0:T(8,128)S(1)} %unit.6.refs_8_) | copy-start | bytes 3072004
  56.6 10.1 %collective-permute-start.9 = (f32[25,80,128]{2,1,0:T(8,128)S(1)}, f32[25,80,128]{2,1,0:T(8,128)S(1)}, u32[]{:S(2)}, u32[]{:S(2)}) collective-permute-start(f32[25,80,128]{2,1,0:T(8,128)S(1)} %broadcast_select_fusion.1.refs_1_.refs_0_), channel_id=1, source_target_pairs={{2,0},{0,2},{6,4},{4,6},{10,8},{8,10},{14,12},{12,14},{18,16},{16,... | collective-permute-start | bytes 3072008 | tf_op jit(solution)/shard_map/ppermute | solution.py:330
  56.7 1.1 copy-start.1
  66.7 1.1 copy-start.10
  67.7 19.3 %collective-permute-start.10 = (f32[25,80,128]{2,1,0:T(8,128)}, f32[25,80,128]{2,1,0:T(8,128)}, u32[]{:S(2)}, u32[]{:S(2)}) collective-permute-start(f32[25,80,128]{2,1,0:T(8,128)} %collective-permute-done.8.refs_3_.refs_2_), channel_id=1, source_target_pairs={{2,0},{0,2},{6,4},{4,6},{10,8},{8,10},{14,12},{12,14},{18,16},{16,... | collective-permute-start | bytes 3072008 | tf_op jit(solution)/shard_map/ppermute | solution.py:330
  68.2 32.1 %collective-permute-start.6 = (f32[25,80,128]{2,1,0:T(8,128)}, f32[25,80,128]{2,1,0:T(8,128)}, u32[]{:S(2)}, u32[]{:S(2)}) collective-permute-start(f32[25,80,128]{2,1,0:T(8,128)} %get-tuple-element.26), channel_id=1, source_target_pairs={{253,0},{252,1},{6,2},{7,3},{0,4},{1,5},{10,6},{11,7},{4,8},{5,9},... | collective-permute-start | bytes 3072008 | tf_op jit(solution)/shard_map/ppermute | solution.py:370
  76.0 24.4 %collective-permute-start.3 = (f32[25,80,128]{2,1,0:T(8,128)S(1)}, f32[25,80,128]{2,1,0:T(8,128)}, u32[]{:S(2)}, u32[]{:S(2)}) collective-permute-start(f32[25,80,128]{2,1,0:T(8,128)S(1)} %pack.1.refs_0_), channel_id=1, source_target_pairs={{252,0},{130,126},{124,128},{2,254},{253,1},{131,127},{125,129},{3... | collective-permute-start | bytes 3072008 | tf_op jit(solution)/shard_map/ppermute | solution.py:339
  78.2 1.2 copy-start.2
  79.4 1.2 copy-start.5
  80.7 6.3 %copy-start.3 = (f32[25,80,128]{2,1,0:T(8,128)S(1)}, f32[25,80,128]{2,1,0:T(8,128)}, u32[]{:S(2)}) copy-start(f32[25,80,128]{2,1,0:T(8,128)} %copy-done.1) | copy-start | bytes 3072004
  80.7 6.3 %copy-start.11 = (f32[25,80,128]{2,1,0:T(8,128)S(1)}, f32[25,80,128]{2,1,0:T(8,128)}, u32[]{:S(2)}) copy-start(f32[25,80,128]{2,1,0:T(8,128)} %copy-done.10) | copy-start | bytes 3072004
  93.5 6.9 %copy-start.13 = (f32[25,80,128]{2,1,0:T(8,128)S(1)}, f32[25,80,128]{2,1,0:T(8,128)}, u32[]{:S(2)}) copy-start(f32[25,80,128]{2,1,0:T(8,128)} %copy-done.12) | copy-start | bytes 3072004
  107.3 12.3 %collective-permute-start.12 = (f32[25,80,128]{2,1,0:T(8,128)S(1)}, f32[25,80,128]{2,1,0:T(8,128)S(1)}, u32[]{:S(2)}, u32[]{:S(2)}) collective-permute-start(f32[25,80,128]{2,1,0:T(8,128)S(1)} %unit.10), channel_id=1, source_target_pairs={{2,0},{0,2},{6,4},{4,6},{10,8},{8,10},{14,12},{12,14},{18,16},{16,... | collective-permute-start | bytes 3072008 | tf_op jit(solution)/shard_map/ppermute | solution.py:330
  107.4 17.5 %collective-permute-start.11 = (f32[25,80,128]{2,1,0:T(8,128)S(1)}, f32[25,80,128]{2,1,0:T(8,128)S(1)}, u32[]{:S(2)}, u32[]{:S(2)}) collective-permute-start(f32[25,80,128]{2,1,0:T(8,128)S(1)} %unit.8), channel_id=1, source_target_pairs={{252,0},{6,2},{0,4},{10,6},{4,8},{14,10},{8,12},{18,14},{12,16},{2... | collective-permute-start | bytes 3072008 | tf_op jit(solution)/shard_map/ppermute | solution.py:330
where the time goes:
time: 128 us; the launch traced here: 127 us
  waiting for transfers between devices  44.9 us (35%)
  Pallas kernels  42.2 us (33%)
  starting transfers between devices  30.2 us (24%)
  local copies, waits for them, and re-layouts  6.98 us (5%)
  other arithmetic  2.57 us (2%)
    pallas_call x6, Pallas kernels, unit(): pl.pallas_call(body, out_shape=jax.ShapeDtypeStruct(PACKED, F32), scratch...  39.1 us
    ppermute x1, waiting for transfers between devices, shards(): far = lax.ppermute(near, 'grid', [(0, 1), (1, 0)])  14.4 us
    ppermute x2, waiting for transfers between devices, near_across(): return (lax.ppermute(data, 'band', route), holds([b for _, b in route]))  9.96 us
    ppermute x6, starting transfers between devices, from_place(): lax.ppermute(data, 'band', [(source, b) for b, source in enumerate(source...  9.13 us
    ppermute x1, waiting for transfers between devices, shards(): m2_far = lax.ppermute(m2_sent, ('band', 'grid'), m2_route)  8.92 us
    ppermute x1, starting transfers between devices, shards(): p2_far = lax.ppermute(p2_sent, ('band', 'grid'), p2_route)  7.74 us
    unnamed x32, local copies, waits for them, and re-layouts  6.98 us
    ppermute x2, waiting for transfers between devices, near_inside(): lax.ppermute(data, 'band', [(source, b) for b, source in enumerate(source...  6.35 us
  transfers between devices with their start and end apart: 13, of which 6 were waited for; matrix products, arithmetic and copies ran while one was open for 2% of the time, Pallas kernels for 25%

commit v1 on v0

--- a/solution.py
+++ b/solution.py
@@ -159,7 +159,8 @@
     return data[:, LANES * index : LANES * (index + 1)]
 
 
-def unit_body(near_a, near_b, far_a, far_b, table_y, table_to, table_from, kernel, total, out, there, back, mid, turned):
+def unit_body(near_a, near_b, far_a, far_b, table_y, table_to, table_from, kernel, total, out, done, there, back, mid, turned):
+    done[0, 0] = 0
     fill = jnp.zeros((LANES - N, LANES), F32)
 
     def forward_y(a, b, first, group):
@@ -242,24 +243,55 @@
         backward_y(group)
 
 
-def unit(a, b, constants, total=None):
+def unit(a, b, constants, after, total=None, waits=()):
     operands = [a[0], b[0], a[1], b[1], *constants]
 
-    def body(*refs):
+    def body(order, *refs):
+        refs = refs[len(waits) :]
         ins, rest = refs[: len(operands)], refs[len(operands) :]
         if total is None:
             unit_body(*ins, None, *rest)
         else:
             unit_body(*ins, *rest)
 
+    here = pl.BlockSpec(memory_space=pltpu.VMEM)
+    scalar = pl.BlockSpec(memory_space=pltpu.SMEM)
+    operands_all = (*operands, *(() if total is None else (total,)))
     return pl.pallas_call(
         body,
+        in_specs=[scalar] + [pl.BlockSpec(memory_space=pl.ANY)] * len(waits) + [here] * len(operands_all),
+        out_specs=(here, scalar),
+        out_shape=(jax.ShapeDtypeStruct(PACKED, F32), jax.ShapeDtypeStruct((1, 1), jnp.int32)),
+        scratch_shapes=[
+            pltpu.VMEM((N, N, LANES), F32),
+            pltpu.VMEM((HALF, N, LANES), F32),
+            pltpu.VMEM((17, 5, GROUP, LANES), F32),
+            pltpu.VMEM((2 * GROUPS * PLANES, LANES, LANES), F32),
+        ],
+        compiler_params=pltpu.CompilerParams(vmem_limit_bytes=20 * 2**20),
+        cost_estimate=pl.CostEstimate(flops=1, bytes_accessed=1, transcendentals=0),
+        name="unit",
+    )(after, *waits, *operands_all)
+
+
+def choose_body(order, flag, a, b, out):
+    @pl.loop(0, GROUPS * PLANES)
+    def _(plane):
+        out[plane] = jnp.where(flag[0, 0] != 0, a[plane], b[plane])
+
+
+def choose(flag, a, b, after):
+    here = pl.BlockSpec(memory_space=pltpu.VMEM)
+    scalar = pl.BlockSpec(memory_space=pltpu.SMEM)
+    return pl.pallas_call(
+        choose_body,
+        in_specs=[scalar, scalar, here, here],
+        out_specs=here,
         out_shape=jax.ShapeDtypeStruct(PACKED, F32),
-        scratch_shapes=[pltpu.VMEM((N, N, LANES), F32), pltpu.VMEM((HALF, N, LANES), F32), pltpu.VMEM((17, 5, GROUP, LANES), F32), pltpu.VMEM((2 * GROUPS * PLANES, LANES, LANES), F32)],
-        compiler_params=pltpu.CompilerParams(vmem_limit_bytes=20 * 2**20),
-        cost_estimate=pl.CostEstimate(flops=10**9, bytes_accessed=2**20, transcendentals=0),
-        name="unit",
-    )(*operands, *(() if total is None else (total,)))
+        compiler_params=pltpu.CompilerParams(vmem_limit_bytes=8 * 2**20),
+        cost_estimate=pl.CostEstimate(flops=1, bytes_accessed=1, transcendentals=0),
+        name="choose",
+    )(after, flag.astype(jnp.int32).reshape(1, 1), a, b)
 
 
 def pack_body(data, out):
@@ -356,36 +388,27 @@
     far = lax.ppermute(near, "grid", [(0, 1), (1, 0)])
     m2_inside = near_inside(near, -2)
     p2_inside = near_inside(near, 2)
-    near_later, far, m2_inside, p2_inside = lax.optimization_barrier((near, far, m2_inside, p2_inside))
+    near_later, far = lax.optimization_barrier((near, far))
     own = (near, far)
     m2_route, m2_across = far_route(-2)
     p2_route, p2_across = far_route(2)
-    m2_sent = jnp.where(m2_across, near, far)
-    p2_sent = jnp.where(p2_across, near, far)
-    m2_far = lax.ppermute(m2_sent, ("band", "grid"), m2_route)
+    first = jnp.zeros((1, 1), jnp.int32)
+    m2_far = lax.ppermute(choose(m2_across, near, far, first), ("band", "grid"), m2_route)
     m2_crossed, m2_takes = near_across(near_later, -2)
+    p2_crossed, p2_takes = near_across(near_later, 2)
     m1 = (other_core(near), other_core(far))
-    total = unit(own, m1, constants)
-    p2_sent, m2_inside, total = lax.optimization_barrier((p2_sent, m2_inside, total))
-    p2_far = lax.ppermute(p2_sent, ("band", "grid"), p2_route)
-    p2_crossed, p2_takes = near_across(near_later, 2)
-    m2_near = jnp.where(m2_takes, m2_crossed, m2_inside)
-    p1_near = other_core(m2_near)
-    m2_far, p1_near, total = lax.optimization_barrier((m2_far, p1_near, total))
-    m2 = (m2_near, m2_far)
-    p1_far = other_core(m2_far)
-    total = unit(own, m2, constants, total)
-    p1_near, total = lax.optimization_barrier((p1_near, total))
-    lent = unit(m2, (p1_near, p1_far), constants)
+    total, after = unit(own, m1, constants, first, waits=(m2_inside, p2_inside))
+    p2_far = lax.ppermute(choose(p2_across, near, far, after), ("band", "grid"), p2_route)
+    m2 = (choose(m2_takes, m2_crossed, m2_inside, after), m2_far)
+    p1 = (other_core(m2[0]), other_core(m2_far))
+    total, after = unit(own, m2, constants, after, total)
+    lent, after = unit(m2, p1, constants, after)
     returned = from_place(lent, 2)
-    m2_near, lent = lax.optimization_barrier((m2_near, lent))
-    partner = unit(m1, (m2_near, m2_far), constants)
-    p2_far, p2_inside, partner, total = lax.optimization_barrier((p2_far, p2_inside, partner, total))
-    p2 = (jnp.where(p2_takes, p2_crossed, p2_inside), p2_far)
-    partner = unit(m1, p2, constants, partner)
+    partner, after = unit(m1, m2, constants, after, waits=(p2_far,))
+    p2 = (choose(p2_takes, p2_crossed, p2_inside, after), p2_far)
+    partner, after = unit(m1, p2, constants, after, partner)
     theirs = other_core(partner)
-    total, partner = lax.optimization_barrier((total, partner))
-    total = unit(own, p2, constants, total)
+    total, after = unit(own, p2, constants, after, total, waits=(returned,))
     return unpack_sum(total, returned, theirs)[None]
 
 

time: 128 us -> 120 us (0.938)
  Pallas kernels: 42.2 us -> 55.2 us
  waiting for transfers between devices: 44.9 us -> 33.5 us
  starting transfers between devices: 30.2 us -> 26.4 us
  local copies, waits for them, and re-layouts: 6.98 us -> 3.64 us
  other arithmetic: 2.57 us -> 0 us
    pallas_call x6 -> x10, Pallas kernels: 39.1 us -> 52.2 us  [the longest x6 43.3 us: unit(): pl.pallas_call(body, in_specs=[scalar] + [pl.BlockSpec(memory_space=pl.AN...]
    ppermute x2, waiting for transfers between devices: 6.35 us -> 0.01 us  [near_inside(): lax.ppermute(data, 'band', [(source, b) for b, source in enumerate(source...]
    ppermute x6, waiting for transfers between devices: 5.29 us -> 0.02 us  [from_place(): lax.ppermute(data, 'band', [(source, b) for b, source in enumerate(source...]
    ppermute x6, starting transfers between devices: 9.13 us -> 4.53 us  [from_place(): lax.ppermute(data, 'band', [(source, b) for b, source in enumerate(source...]
    unnamed x32 -> x14, local copies, waits for them, and re-layouts: 6.98 us -> 3.64 us
    select_n x3 -> x0, other arithmetic: 2.57 us -> none  [the longest x1 1.33 us: shards(): m2_near = jnp.where(m2_takes, m2_crossed, m2_inside)]
  transfers between devices with their start and end apart: 13 -> 13, of which waited for: 6 -> 3; matrix products, arithmetic and copies ran while one was open for 2% -> 0% of each run, Pallas kernels for 25% -> 44%
where the time goes in v1:
time: 120 us; the launch traced here: 119 us
  Pallas kernels  55.2 us (46%)
  waiting for transfers between devices  33.5 us (28%)
  starting transfers between devices  26.4 us (22%)
  local copies, waits for them, and re-layouts  3.64 us (3%)
    pallas_call x6, Pallas kernels, unit(): pl.pallas_call(body, in_specs=[scalar] + [pl.BlockSpec(memory_space=pl.AN...  43.3 us
    ppermute x1, waiting for transfers between devices, shards(): far = lax.ppermute(near, 'grid', [(0, 1), (1, 0)])  15 us
    ppermute x2, waiting for transfers between devices, near_across(): return (lax.ppermute(data, 'band', route), holds([b for _, b in route]))  10.4 us
    pallas_call x4, Pallas kernels, choose(): pl.pallas_call(choose_body, in_specs=[scalar, scalar, here, here], out_sp...  8.83 us
    ppermute x1, waiting for transfers between devices, shards(): lax.ppermute(choose(m2_across, near, far, first), ('band', 'grid'), m2_ro...  8.13 us
    ppermute x1, starting transfers between devices, shards(): lax.ppermute(choose(p2_across, near, far, after), ('band', 'grid'), p2_ro...  7.22 us
    ppermute x2, starting transfers between devices, near_inside(): lax.ppermute(data, 'band', [(source, b) for b, source in enumerate(source...  5.35 us
    ppermute x6, starting transfers between devices, from_place(): lax.ppermute(data, 'band', [(source, b) for b, source in enumerate(source...  4.53 us
  transfers between devices with their start and end apart: 13, of which 3 were waited for; matrix products, arithmetic and copies ran while one was open for 0% of the time, Pallas kernels for 44%

profile of v1, /device:TPU:1, one launch (start us, length us, event | category | flops | bytes accessed | tf_op | source)
XLA Modules:
  0.0 119.0 jit_solution(17833393896358080188)
XLA Ops:
  0.0 1.4 %copy-done.1 = f32[1,40,80,80]{3,2,1,0:T(8,128)S(1)} copy-done((f32[1,40,80,80]{3,2,1,0:T(8,128)S(1)}, f32[1,40,80,80]{3,2,1,0:T(8,128)}, u32[]{:S(2)}) %copy-start.1) | copy-done | bytes 1024024
  1.4 0.9 pack.1.refs_2_.a.refs_0_.refs_1_
  2.4 0.0 copy-start
  2.4 0.0 copy-start.2
  2.4 0.0 copy-start.3
  2.4 0.0 copy-start.4
  2.4 3.8 %collective-permute-start.3 = (f32[25,80,128]{2,1,0:T(8,128)S(1)}, f32[25,80,128]{2,1,0:T(8,128)S(1)}, u32[]{:S(2)}, u32[]{:S(2)}) collective-permute-start(f32[25,80,128]{2,1,0:T(8,128)S(1)} %pack.1.refs_2_.a.refs_0_.refs_1_), channel_id=1, source_target_pairs={{0,1},{1,0},{2,3},{3,2},{4,5},{5,4},{6,7},{7,6},{8,9},{9,8},{10,11... | collective-permute-start | bytes 3072008 | tf_op jit(solution)/shard_map/ppermute | solution.py:388
  6.2 1.0 collective-permute-start.2
  7.2 4.1 %collective-permute-start = (f32[25,80,128]{2,1,0:T(8,128)S(1)}, f32[25,80,128]{2,1,0:T(8,128)}, u32[]{:S(2)}, u32[]{:S(2)}) collective-permute-start(f32[25,80,128]{2,1,0:T(8,128)S(1)} %pack.1.refs_2_.a.refs_0_.refs_1_), channel_id=1, source_target_pairs={{4,0},{8,4},{2,6},{12,8},{6,10},{16,12},{10,14},{20,16},{14,18},{2... | collective-permute-start | bytes 3072008 | tf_op jit(solution)/shard_map/ppermute | solution.py:365
  11.3 1.3 %collective-permute-start.1 = (f32[25,80,128]{2,1,0:T(8,128)S(1)}, f32[25,80,128]{2,1,0:T(8,128)}, u32[]{:S(2)}, u32[]{:S(2)}) collective-permute-start(f32[25,80,128]{2,1,0:T(8,128)S(1)} %pack.1.refs_2_.a.refs_0_.refs_1_), channel_id=1, source_target_pairs={{6,2},{0,4},{10,6},{4,8},{14,10},{8,12},{18,14},{12,16},{22,18},{1... | collective-permute-start | bytes 3072008 | tf_op jit(solution)/shard_map/ppermute | solution.py:365
  12.6 15.0 %collective-permute-done.3.refs_4_.b.refs_2_.refs_3_ = f32[25,80,128]{2,1,0:T(8,128)S(1)} collective-permute-done((f32[25,80,128]{2,1,0:T(8,128)S(1)}, f32[25,80,128]{2,1,0:T(8,128)S(1)}, u32[]{:S(2)}, u32[]{:S(2)}) %collective-permute-start.3) | collective-permute-done | bytes 1024032 | tf_op jit(solution)/shard_map/ppermute | solution.py:388
  27.5 2.3 %collective-permute-start.4 = (f32[25,80,128]{2,1,0:T(8,128)S(1)}, f32[25,80,128]{2,1,0:T(8,128)}, u32[]{:S(2)}, u32[]{:S(2)}) collective-permute-start(f32[25,80,128]{2,1,0:T(8,128)S(1)} %collective-permute-done.3.refs_4_.b.refs_2_.refs_3_), channel_id=1, source_target_pairs={{2,0},{0,2},{6,4},{4,6},{10,8},{8,10},{14,12},{12,14},{18,16},{16,... | collective-permute-start | bytes 3072008 | tf_op jit(solution)/shard_map/ppermute | solution.py:362
  29.8 1.3 %collective-permute-start.5 = (f32[25,80,128]{2,1,0:T(8,128)S(1)}, f32[25,80,128]{2,1,0:T(8,128)}, u32[]{:S(2)}, u32[]{:S(2)}) collective-permute-start(f32[25,80,128]{2,1,0:T(8,128)S(1)} %pack.1.refs_2_.a.refs_0_.refs_1_), channel_id=1, source_target_pairs={{254,2},{128,124},{126,130},{0,252},{255,3},{129,125},{127,131},{1... | collective-permute-start | bytes 3072008 | tf_op jit(solution)/shard_map/ppermute | solution.py:371
  31.1 1.3 %choose.5 = f32[25,80,128]{2,1,0:T(8,128)} custom-call(s32[1,1]{1,0:T(1,128)} %constant.6.clone.1.order, s32[1,1]{1,0:T(1,128)} %bitcast.2.flag, f32[25,80,128]{2,1,0:T(8,128)S(1)} %pack.1.refs_2_.a.refs_0_.refs_1_, f32[25,80,128]{2,1,0:T(8,128)S(1)} %collective-permute-done.3.refs_4_.b.refs_2_.refs_3_), custom_call_target="tpu_custom_call" | custom-call | flops 1 | bytes 1 | tf_op jit(solution)/shard_map/choose/pallas_call | solution.py:286
  32.4 0.0 collective-permute-done.2.refs_3_.refs_1_.refs_0_
  32.4 1.7 %collective-permute-start.6 = (f32[25,80,128]{2,1,0:T(8,128)}, f32[25,80,128]{2,1,0:T(8,128)}, u32[]{:S(2)}, u32[]{:S(2)}) collective-permute-start(f32[25,80,128]{2,1,0:T(8,128)} %choose.5), channel_id=1, source_target_pairs={{4,0},{5,1},{255,2},{254,3},{8,4},{9,5},{2,6},{3,7},{12,8},{13,9},... | collective-permute-start | bytes 3072008 | tf_op jit(solution)/shard_map/ppermute | solution.py:396
  34.0 0.0 collective-permute-done.refs_0_.b
  34.0 0.0 collective-permute-done.1.refs_1_.b
  34.0 0.0 collective-permute-done.4.refs_5_.refs_3_.refs_2_
  34.0 0.0 copy-done
  34.1 0.0 copy-done.2
  34.1 0.0 copy-done.3
  34.1 6.5 %unit.6 = (f32[25,80,128]{2,1,0:T(8,128)S(1)}, s32[1,1]{1,0:T(1,128)}) custom-call(s32[1,1]{1,0:T(1,128)} %constant.6.clone.1.order, f32[25,80,128]{2,1,0:T(8,128)} %collective-permute-done.refs_0_.b, f32[25,80,128]{2,1,0:T(8,128)} %collective-permute-done.1.refs_1_.b, f32[25,80,128]{2,1,0:T(8,128)S(1)} %pack.1.refs_2_.a.refs_0_.refs_1_, ...), custom_call_target="tpu_custom_call" | custom-call | flops 1 | bytes 1 | tf_op jit(solution)/shard_map/unit/pallas_call | solution.py:260
  40.6 1.0 copy-done.5
  41.6 10.4 %collective-permute-done.5.a = f32[25,80,128]{2,1,0:T(8,128)} collective-permute-done((f32[25,80,128]{2,1,0:T(8,128)S(1)}, f32[25,80,128]{2,1,0:T(8,128)}, u32[]{:S(2)}, u32[]{:S(2)}) %collective-permute-start.5) | collective-permute-done | bytes 1024032 | tf_op jit(solution)/shard_map/ppermute | solution.py:371
  52.0 3.4 %choose.4.refs_1_.refs_0_.refs_2_ = f32[25,80,128]{2,1,0:T(8,128)} custom-call(s32[1,1]{1,0:T(1,128)} %get-tuple-element.19.order, s32[1,1]{1,0:T(1,128)} %bitcast.1.flag, f32[25,80,128]{2,1,0:T(8,128)} %collective-permute-done.5.a, f32[25,80,128]{2,1,0:T(8,128)} %collective-permute-done.refs_0_.b), custom_call_target="tpu_custom_call" | custom-call | flops 1 | bytes 1 | tf_op jit(solution)/shard_map/choose/pallas_call | solution.py:286
  55.3 0.9 collective-permute-start.7
  56.2 8.1 %collective-permute-done.6.refs_3_.refs_2_.refs_4_ = f32[25,80,128]{2,1,0:T(8,128)} collective-permute-done((f32[25,80,128]{2,1,0:T(8,128)}, f32[25,80,128]{2,1,0:T(8,128)}, u32[]{:S(2)}, u32[]{:S(2)}) %collective-permute-start.6) | collective-permute-done | bytes 1024032 | tf_op jit(solution)/shard_map/ppermute | solution.py:396
  64.4 0.0 collective-permute-start.8
  64.4 1.8 %choose.6 = f32[25,80,128]{2,1,0:T(8,128)} custom-call(s32[1,1]{1,0:T(1,128)} %get-tuple-element.19.order, s32[1,1]{1,0:T(1,128)} %bitcast.3.flag, f32[25,80,128]{2,1,0:T(8,128)S(1)} %pack.1.refs_2_.a.refs_0_.refs_1_, f32[25,80,128]{2,1,0:T(8,128)S(1)} %collective-permute-done.3.refs_4_.b.refs_2_.refs_3_), custom_call_target="tpu_custom_call" | custom-call | flops 1 | bytes 1 | tf_op jit(solution)/shard_map/choose/pallas_call | solution.py:286
  66.2 7.2 %collective-permute-start.9 = (f32[25,80,128]{2,1,0:T(8,128)}, f32[25,80,128]{2,1,0:T(8,128)}, u32[]{:S(2)}, u32[]{:S(2)}) collective-permute-start(f32[25,80,128]{2,1,0:T(8,128)} %choose.6), channel_id=1, source_target_pairs={{253,0},{252,1},{6,2},{7,3},{0,4},{1,5},{10,6},{11,7},{4,8},{5,9},... | collective-permute-start | bytes 3072008 | tf_op jit(solution)/shard_map/ppermute | solution.py:401
  73.4 2.5 %collective-permute-start.10 = (f32[25,80,128]{2,1,0:T(8,128)S(1)}, f32[25,80,128]{2,1,0:T(8,128)}, u32[]{:S(2)}, u32[]{:S(2)}) collective-permute-start(f32[25,80,128]{2,1,0:T(8,128)S(1)} %pack.1.refs_2_.a.refs_0_.refs_1_), channel_id=1, source_target_pairs={{252,0},{130,126},{124,128},{2,254},{253,1},{131,127},{125,129},{3... | collective-permute-start | bytes 3072008 | tf_op jit(solution)/shard_map/ppermute | solution.py:371
  76.0 1.2 %copy-done.6 = f32[25,80,128]{2,1,0:T(8,128)S(1)} copy-done((f32[25,80,128]{2,1,0:T(8,128)S(1)}, f32[25,80,128]{2,1,0:T(8,128)}, u32[]{:S(2)}) %copy-start.6) | copy-done | bytes 1024024
  77.2 7.1 %unit.7 = (f32[25,80,128]{2,1,0:T(8,128)S(1)}, s32[1,1]{1,0:T(1,128)}) custom-call(s32[1,1]{1,0:T(1,128)} %get-tuple-element.19.order, f32[25,80,128]{2,1,0:T(8,128)S(1)} %pack.1.refs_2_.a.refs_0_.refs_1_, f32[25,80,128]{2,1,0:T(8,128)} %choose.4.refs_1_.refs_0_.refs_2_, f32[25,80,128]{2,1,0:T(8,128)S(1)} %collective-permute-done.3.refs_4_.b.refs_2_.refs_3_, ...), custom_call_target="tpu_custom_call" | custom-call | flops 1 | bytes 1 | tf_op jit(solution)/shard_map/unit/pallas_call | solution.py:260
  84.3 0.0 collective-permute-done.7.refs_1_
  84.3 0.0 collective-permute-done.8.refs_3_
  84.3 7.7 %unit.8 = (f32[25,80,128]{2,1,0:T(8,128)S(1)}, s32[1,1]{1,0:T(1,128)}) custom-call(s32[1,1]{1,0:T(1,128)} %get-tuple-element.22.order, f32[25,80,128]{2,1,0:T(8,128)} %choose.4.refs_1_.refs_0_.refs_2_, f32[25,80,128]{2,1,0:T(8,128)} %collective-permute-done.7.refs_1_, f32[25,80,128]{2,1,0:T(8,128)} %collective-permute-done.6.refs_3_.refs_2_.refs_4_, ...), custom_call_target="tpu_custom_call" | custom-call | flops 1 | bytes 1 | tf_op jit(solution)/shard_map/unit/pallas_call | solution.py:260
  92.1 0.3 collective-permute-start.11
  92.4 0.0 collective-permute-done.9.refs_0_.refs_3_.refs_4_
  92.4 7.7 %unit.9 = (f32[25,80,128]{2,1,0:T(8,128)S(1)}, s32[1,1]{1,0:T(1,128)}) custom-call(s32[1,1]{1,0:T(1,128)} %get-tuple-element.23.order, f32[25,80,128]{2,1,0:T(8,128)} %collective-permute-done.9.refs_0_.refs_3_.refs_4_, f32[25,80,128]{2,1,0:T(8,128)} %collective-permute-done.2.refs_3_.refs_1_.refs_0_, f32[25,80,128]{2,1,0:T(8,128)} %choose.4.refs_1_.refs_0_.refs_2_, ...), custom_call_target="tpu_custom_call" | custom-call | flops 1 | bytes 1 | tf_op jit(solution)/shard_map/unit/pallas_call | solution.py:260
  100.1 0.0 collective-permute-done.10.a
  100.1 2.4 %choose.7.refs_1_.refs_2_ = f32[25,80,128]{2,1,0:T(8,128)S(1)} custom-call(s32[1,1]{1,0:T(1,128)} %get-tuple-element.24.order, s32[1,1]{1,0:T(1,128)} %bitcast.4.flag, f32[25,80,128]{2,1,0:T(8,128)} %collective-permute-done.10.a, f32[25,80,128]{2,1,0:T(8,128)} %collective-permute-done.1.refs_1_.b), custom_call_target="tpu_custom_call" | custom-call | flops 1 | bytes 1 | tf_op jit(solution)/shard_map/choose/pallas_call | solution.py:286
  102.5 7.4 %unit.10 = (f32[25,80,128]{2,1,0:T(8,128)S(1)}, s32[1,1]{1,0:T(1,128)}) custom-call(s32[1,1]{1,0:T(1,128)} %get-tuple-element.24.order, f32[25,80,128]{2,1,0:T(8,128)} %collective-permute-done.2.refs_3_.refs_1_.refs_0_, f32[25,80,128]{2,1,0:T(8,128)S(1)} %choose.7.refs_1_.refs_2_, f32[25,80,128]{2,1,0:T(8,128)} %collective-permute-done.4.refs_5_.refs_3_.refs_2_, ...), custom_call_target="tpu_custom_call" | custom-call | flops 1 | bytes 1 | tf_op jit(solution)/shard_map/unit/pallas_call | solution.py:260
  110.0 0.1 collective-permute-start.12
  110.1 0.0 collective-permute-done.11.refs_0_.returned
  110.1 6.8 %unit.11 = (f32[25,80,128]{2,1,0:T(8,128)S(1)}, s32[1,1]{1,0:T(1,128)}) custom-call(s32[1,1]{1,0:T(1,128)} %get-tuple-element.26.order, f32[25,80,128]{2,1,0:T(8,128)S(1)} %collective-permute-done.11.refs_0_.returned, f32[25,80,128]{2,1,0:T(8,128)S(1)} %pack.1.refs_2_.a.refs_0_.refs_1_, f32[25,80,128]{2,1,0:T(8,128)S(1)} %choose.7.refs_1_.refs_2_, ...), custom_call_target="tpu_custom_call" | custom-call | flops 1 | bytes 1 | tf_op jit(solution)/shard_map/unit/pallas_call | solution.py:260
  116.9 0.0 collective-permute-done.12.theirs
  116.9 2.1 %unpack_sum.1 = f32[40,80,80]{2,1,0:T(8,128)} custom-call(f32[25,80,128]{2,1,0:T(8,128)S(1)} %get-tuple-element.29.total, f32[25,80,128]{2,1,0:T(8,128)S(1)} %collective-permute-done.11.refs_0_.returned, f32[25,80,128]{2,1,0:T(8,128)S(1)} %collective-permute-done.12.theirs), custom_call_target="tpu_custom_call" | custom-call | tf_op jit(solution)/shard_map/unpack_sum/pallas_call | solution.py:338
  (4 shorter events, 0.0 us)
Async XLA Ops:
  0.0 1.4 %copy-start.1 = (f32[1,40,80,80]{3,2,1,0:T(8,128)S(1)}, f32[1,40,80,80]{3,2,1,0:T(8,128)}, u32[]{:S(2)}) copy-start(f32[1,40,80,80]{3,2,1,0:T(8,128)} %param.5) | copy-start | bytes 3072004
  2.4 31.7 %copy-start = (f32[6,41,8,128]{3,2,1,0:T(8,128)S(1)}, f32[6,41,8,128]{3,2,1,0:T(8,128)}, u32[]{:S(2)}) copy-start(f32[6,41,8,128]{3,2,1,0:T(8,128)} %constant.35.clone.refs_9_.refs_7_.refs_8_) | copy-start | bytes 3022852
  2.4 31.7 %copy-start.2 = (bf16[80,240]{1,0:T(8,128)(2,1)S(1)}, bf16[80,240]{1,0:T(8,128)(2,1)}, u32[]{:S(2)}) copy-start(bf16[80,240]{1,0:T(8,128)(2,1)} %constant.32.clone.refs_6_.refs_4_.refs_5_) | copy-start | bytes 115204
  2.4 31.7 %copy-start.3 = (bf16[80,240]{1,0:T(8,128)(2,1)S(1)}, bf16[80,240]{1,0:T(8,128)(2,1)}, u32[]{:S(2)}) copy-start(bf16[80,240]{1,0:T(8,128)(2,1)} %constant.33.clone.refs_7_.refs_5_.refs_6_) | copy-start | bytes 115204
  2.4 31.7 %copy-start.4 = (bf16[80,240]{1,0:T(8,128)(2,1)S(1)}, bf16[80,240]{1,0:T(8,128)(2,1)}, u32[]{:S(2)}) copy-start(bf16[80,240]{1,0:T(8,128)(2,1)} %constant.34.clone.refs_8_.refs_6_.refs_7_) | copy-start | bytes 115204
  2.4 25.1 %collective-permute-start.3 = (f32[25,80,128]{2,1,0:T(8,128)S(1)}, f32[25,80,128]{2,1,0:T(8,128)S(1)}, u32[]{:S(2)}, u32[]{:S(2)}) collective-permute-start(f32[25,80,128]{2,1,0:T(8,128)S(1)} %pack.1.refs_2_.a.refs_0_.refs_1_), channel_id=1, source_target_pairs={{0,1},{1,0},{2,3},{3,2},{4,5},{5,4},{6,7},{7,6},{8,9},{9,8},{10,11... | collective-permute-start | bytes 3072008 | tf_op jit(solution)/shard_map/ppermute | solution.py:388
  6.2 26.1 %collective-permute-start.2 = (f32[25,80,128]{2,1,0:T(8,128)S(1)}, f32[25,80,128]{2,1,0:T(8,128)}, u32[]{:S(2)}, u32[]{:S(2)}) collective-permute-start(f32[25,80,128]{2,1,0:T(8,128)S(1)} %pack.1.refs_2_.a.refs_0_.refs_1_), channel_id=1, source_target_pairs={{2,0},{0,2},{6,4},{4,6},{10,8},{8,10},{14,12},{12,14},{18,16},{16,... | collective-permute-start | bytes 3072008 | tf_op jit(solution)/shard_map/ppermute | solution.py:362
  7.2 26.8 %collective-permute-start = (f32[25,80,128]{2,1,0:T(8,128)S(1)}, f32[25,80,128]{2,1,0:T(8,128)}, u32[]{:S(2)}, u32[]{:S(2)}) collective-permute-start(f32[25,80,128]{2,1,0:T(8,128)S(1)} %pack.1.refs_2_.a.refs_0_.refs_1_), channel_id=1, source_target_pairs={{4,0},{8,4},{2,6},{12,8},{6,10},{16,12},{10,14},{20,16},{14,18},{2... | collective-permute-start | bytes 3072008 | tf_op jit(solution)/shard_map/ppermute | solution.py:365
  11.3 22.8 %collective-permute-start.1 = (f32[25,80,128]{2,1,0:T(8,128)S(1)}, f32[25,80,128]{2,1,0:T(8,128)}, u32[]{:S(2)}, u32[]{:S(2)}) collective-permute-start(f32[25,80,128]{2,1,0:T(8,128)S(1)} %pack.1.refs_2_.a.refs_0_.refs_1_), channel_id=1, source_target_pairs={{6,2},{0,4},{10,6},{4,8},{14,10},{8,12},{18,14},{12,16},{22,18},{1... | collective-permute-start | bytes 3072008 | tf_op jit(solution)/shard_map/ppermute | solution.py:365
  27.5 6.5 %collective-permute-start.4 = (f32[25,80,128]{2,1,0:T(8,128)S(1)}, f32[25,80,128]{2,1,0:T(8,128)}, u32[]{:S(2)}, u32[]{:S(2)}) collective-permute-start(f32[25,80,128]{2,1,0:T(8,128)S(1)} %collective-permute-done.3.refs_4_.b.refs_2_.refs_3_), channel_id=1, source_target_pairs={{2,0},{0,2},{6,4},{4,6},{10,8},{8,10},{14,12},{12,14},{18,16},{16,... | collective-permute-start | bytes 3072008 | tf_op jit(solution)/shard_map/ppermute | solution.py:362
  29.8 22.1 %collective-permute-start.5 = (f32[25,80,128]{2,1,0:T(8,128)S(1)}, f32[25,80,128]{2,1,0:T(8,128)}, u32[]{:S(2)}, u32[]{:S(2)}) collective-permute-start(f32[25,80,128]{2,1,0:T(8,128)S(1)} %pack.1.refs_2_.a.refs_0_.refs_1_), channel_id=1, source_target_pairs={{254,2},{128,124},{126,130},{0,252},{255,3},{129,125},{127,131},{1... | collective-permute-start | bytes 3072008 | tf_op jit(solution)/shard_map/ppermute | solution.py:371
  32.4 32.0 %collective-permute-start.6 = (f32[25,80,128]{2,1,0:T(8,128)}, f32[25,80,128]{2,1,0:T(8,128)}, u32[]{:S(2)}, u32[]{:S(2)}) collective-permute-start(f32[25,80,128]{2,1,0:T(8,128)} %choose.5), channel_id=1, source_target_pairs={{4,0},{5,1},{255,2},{254,3},{8,4},{9,5},{2,6},{3,7},{12,8},{13,9},... | collective-permute-start | bytes 3072008 | tf_op jit(solution)/shard_map/ppermute | solution.py:396
  40.6 1.0 copy-start.5
  55.3 29.0 %collective-permute-start.7 = (f32[25,80,128]{2,1,0:T(8,128)}, f32[25,80,128]{2,1,0:T(8,128)}, u32[]{:S(2)}, u32[]{:S(2)}) collective-permute-start(f32[25,80,128]{2,1,0:T(8,128)} %choose.4.refs_1_.refs_0_.refs_2_), channel_id=1, source_target_pairs={{2,0},{0,2},{6,4},{4,6},{10,8},{8,10},{14,12},{12,14},{18,16},{16,... | collective-permute-start | bytes 3072008 | tf_op jit(solution)/shard_map/ppermute | solution.py:362
  64.4 20.0 %collective-permute-start.8 = (f32[25,80,128]{2,1,0:T(8,128)}, f32[25,80,128]{2,1,0:T(8,128)}, u32[]{:S(2)}, u32[]{:S(2)}) collective-permute-start(f32[25,80,128]{2,1,0:T(8,128)} %collective-permute-done.6.refs_3_.refs_2_.refs_4_), channel_id=1, source_target_pairs={{2,0},{0,2},{6,4},{4,6},{10,8},{8,10},{14,12},{12,14},{18,16},{16,... | collective-permute-start | bytes 3072008 | tf_op jit(solution)/shard_map/ppermute | solution.py:362
  66.2 26.2 %collective-permute-start.9 = (f32[25,80,128]{2,1,0:T(8,128)}, f32[25,80,128]{2,1,0:T(8,128)}, u32[]{:S(2)}, u32[]{:S(2)}) collective-permute-start(f32[25,80,128]{2,1,0:T(8,128)} %choose.6), channel_id=1, source_target_pairs={{253,0},{252,1},{6,2},{7,3},{0,4},{1,5},{10,6},{11,7},{4,8},{5,9},... | collective-permute-start | bytes 3072008 | tf_op jit(solution)/shard_map/ppermute | solution.py:401
  73.4 26.7 %collective-permute-start.10 = (f32[25,80,128]{2,1,0:T(8,128)S(1)}, f32[25,80,128]{2,1,0:T(8,128)}, u32[]{:S(2)}, u32[]{:S(2)}) collective-permute-start(f32[25,80,128]{2,1,0:T(8,128)S(1)} %pack.1.refs_2_.a.refs_0_.refs_1_), channel_id=1, source_target_pairs={{252,0},{130,126},{124,128},{2,254},{253,1},{131,127},{125,129},{3... | collective-permute-start | bytes 3072008 | tf_op jit(solution)/shard_map/ppermute | solution.py:371
  76.0 1.2 %copy-start.6 = (f32[25,80,128]{2,1,0:T(8,128)S(1)}, f32[25,80,128]{2,1,0:T(8,128)}, u32[]{:S(2)}) copy-start(f32[25,80,128]{2,1,0:T(8,128)} %copy-done.5) | copy-start | bytes 3072004
  92.1 18.0 %collective-permute-start.11 = (f32[25,80,128]{2,1,0:T(8,128)S(1)}, f32[25,80,128]{2,1,0:T(8,128)S(1)}, u32[]{:S(2)}, u32[]{:S(2)}) collective-permute-start(f32[25,80,128]{2,1,0:T(8,128)S(1)} %get-tuple-element.27), channel_id=1, source_target_pairs={{252,0},{6,2},{0,4},{10,6},{4,8},{14,10},{8,12},{18,14},{12,16},{2... | collective-permute-start | bytes 3072008 | tf_op jit(solution)/shard_map/ppermute | solution.py:362
  110.0 6.9 %collective-permute-start.12 = (f32[25,80,128]{2,1,0:T(8,128)S(1)}, f32[25,80,128]{2,1,0:T(8,128)S(1)}, u32[]{:S(2)}, u32[]{:S(2)}) collective-permute-start(f32[25,80,128]{2,1,0:T(8,128)S(1)} %get-tuple-element.30), channel_id=1, source_target_pairs={{2,0},{0,2},{6,4},{4,6},{10,8},{8,10},{14,12},{12,14},{18,16},{16,... | collective-permute-start | bytes 3072008 | tf_op jit(solution)/shard_map/ppermute | solution.py:362

commit v2 on v1

--- a/solution.py
+++ b/solution.py
@@ -243,11 +243,18 @@
         backward_y(group)
 
 
-def unit(a, b, constants, after, total=None, waits=()):
+def unit(a, b, constants, after, total=None, waits=(), again=False):
     operands = [a[0], b[0], a[1], b[1], *constants]
 
     def body(order, *refs):
-        refs = refs[len(waits) :]
+        refs = list(refs[len(waits) :])
+        if again:
+            copied = refs.pop(len(operands) + (total is not None) + 2)
+
+            @pl.loop(0, GROUPS * PLANES)
+            def _(plane):
+                copied[plane] = refs[2][plane]
+
         ins, rest = refs[: len(operands)], refs[len(operands) :]
         if total is None:
             unit_body(*ins, None, *rest)
@@ -260,8 +267,9 @@
     return pl.pallas_call(
         body,
         in_specs=[scalar] + [pl.BlockSpec(memory_space=pl.ANY)] * len(waits) + [here] * len(operands_all),
-        out_specs=(here, scalar),
-        out_shape=(jax.ShapeDtypeStruct(PACKED, F32), jax.ShapeDtypeStruct((1, 1), jnp.int32)),
+        out_specs=(here, scalar) + (here,) * again,
+        out_shape=(jax.ShapeDtypeStruct(PACKED, F32), jax.ShapeDtypeStruct((1, 1), jnp.int32))
+        + (jax.ShapeDtypeStruct(PACKED, F32),) * again,
         scratch_shapes=[
             pltpu.VMEM((N, N, LANES), F32),
             pltpu.VMEM((HALF, N, LANES), F32),
@@ -274,24 +282,34 @@
     )(after, *waits, *operands_all)
 
 
-def choose_body(order, flag, a, b, out):
-    @pl.loop(0, GROUPS * PLANES)
-    def _(plane):
-        out[plane] = jnp.where(flag[0, 0] != 0, a[plane], b[plane])
-
-
-def choose(flag, a, b, after):
+def choose_body(places, order, a, b, out):
+    place = lax.axis_index("band")
+    takes = functools.reduce(jnp.logical_or, [place == p for p in places])
+
+    @pl.when(takes)
+    def _():
+        @pl.loop(0, GROUPS * PLANES)
+        def _(plane):
+            out[plane] = a[plane]
+
+    @pl.when(jnp.logical_not(takes))
+    def _():
+        @pl.loop(0, GROUPS * PLANES)
+        def _(plane):
+            out[plane] = b[plane]
+
+
+def choose(places, a, b, after):
     here = pl.BlockSpec(memory_space=pltpu.VMEM)
-    scalar = pl.BlockSpec(memory_space=pltpu.SMEM)
     return pl.pallas_call(
-        choose_body,
-        in_specs=[scalar, scalar, here, here],
+        functools.partial(choose_body, places),
+        in_specs=[pl.BlockSpec(memory_space=pltpu.SMEM), here, here],
         out_specs=here,
         out_shape=jax.ShapeDtypeStruct(PACKED, F32),
         compiler_params=pltpu.CompilerParams(vmem_limit_bytes=8 * 2**20),
         cost_estimate=pl.CostEstimate(flops=1, bytes_accessed=1, transcendentals=0),
         name="choose",
-    )(after, flag.astype(jnp.int32).reshape(1, 1), a, b)
+    )(after, a, b)
 
 
 def pack_body(data, out):
@@ -346,7 +364,6 @@
 def shards(orbitals):
     bands = lax.axis_size("band")
     half = bands // 2
-    place = lax.axis_index("band")
     sides = [1 if b % 2 else -1 for b in range(bands)]
 
     def sources(distance):
@@ -354,9 +371,6 @@
 
     def crosses(b, source):
         return b // half != source // half
-
-    def holds(places):
-        return functools.reduce(jnp.logical_or, [place == p for p in places])
 
     def from_place(data, distance):
         return lax.ppermute(data, "band", [(source, b) for b, source in enumerate(sources(distance))])
@@ -366,19 +380,8 @@
             data, "band", [(source, b) for b, source in enumerate(sources(distance)) if not crosses(b, source)]
         )
 
-    def near_across(data, distance):
-        route = [(source, b) for b, source in enumerate(sources(distance)) if crosses(b, source)]
-        return lax.ppermute(data, "band", route), holds([b for _, b in route])
-
-    def far_route(distance):
-        route, across = [], []
-        for b, source in enumerate(sources(distance)):
-            cross = crosses(b, source)
-            if cross:
-                across.append(source)
-            for slab in range(2):
-                route.append((2 * source + (1 - slab if cross else slab), 2 * b + slab))
-        return route, holds(across)
+    def across(distance):
+        return [(source, b) for b, source in enumerate(sources(distance)) if crosses(b, source)]
 
     def other_core(data):
         return from_place(data, -1)
@@ -388,24 +391,25 @@
     far = lax.ppermute(near, "grid", [(0, 1), (1, 0)])
     m2_inside = near_inside(near, -2)
     p2_inside = near_inside(near, 2)
-    near_later, far = lax.optimization_barrier((near, far))
+    p2_inside, m2_inside, far = lax.optimization_barrier((p2_inside, m2_inside, far))
     own = (near, far)
-    m2_route, m2_across = far_route(-2)
-    p2_route, p2_across = far_route(2)
+    m2_far = from_place(far, -2)
+    crossed = lax.ppermute(
+        far, ("band", "grid"), [(2 * a + 1 - slab, 2 * b + slab) for a, b in across(-2) + across(2) for slab in range(2)]
+    )
+    m2_takes, p2_takes = ([b for _, b in across(distance)] for distance in (-2, 2))
+    m1 = (other_core(near), other_core(far))
     first = jnp.zeros((1, 1), jnp.int32)
-    m2_far = lax.ppermute(choose(m2_across, near, far, first), ("band", "grid"), m2_route)
-    m2_crossed, m2_takes = near_across(near_later, -2)
-    p2_crossed, p2_takes = near_across(near_later, 2)
-    m1 = (other_core(near), other_core(far))
-    total, after = unit(own, m1, constants, first, waits=(m2_inside, p2_inside))
-    p2_far = lax.ppermute(choose(p2_across, near, far, after), ("band", "grid"), p2_route)
-    m2 = (choose(m2_takes, m2_crossed, m2_inside, after), m2_far)
+    total, after, far_later = unit(own, m1, constants, first, waits=(m2_inside, p2_inside), again=True)
+    p2_far = from_place(far_later, 2)
+    m2_far, after = lax.optimization_barrier((m2_far, after))
+    m2 = (choose(m2_takes, crossed, m2_inside, after), m2_far)
     p1 = (other_core(m2[0]), other_core(m2_far))
     total, after = unit(own, m2, constants, after, total)
     lent, after = unit(m2, p1, constants, after)
     returned = from_place(lent, 2)
     partner, after = unit(m1, m2, constants, after, waits=(p2_far,))
-    p2 = (choose(p2_takes, p2_crossed, p2_inside, after), p2_far)
+    p2 = (choose(p2_takes, crossed, p2_inside, after), p2_far)
     partner, after = unit(m1, p2, constants, after, partner)
     theirs = other_core(partner)
     total, after = unit(own, p2, constants, after, total, waits=(returned,))

time: 120 us -> 116 us (0.967)
  Pallas kernels: 55.2 us -> 38 us
  waiting for transfers between devices: 33.5 us -> 47.5 us
  starting transfers between devices: 26.4 us -> 28.6 us
  local copies, waits for them, and re-layouts: 3.64 us -> 1.53 us
    pallas_call x6, Pallas kernels: 43.3 us -> 33.3 us  [unit(): pl.pallas_call(body, in_specs=[scalar] + [pl.BlockSpec(memory_space=pl.AN...]
    ppermute x6 -> x8, waiting for transfers between devices: 0.02 us -> 7.6 us  [from_place(): lax.ppermute(data, 'band', [(source, b) for b, source in enumerate(source...]
    ppermute x6 -> x8, starting transfers between devices: 4.53 us -> 12 us  [from_place(): lax.ppermute(data, 'band', [(source, b) for b, source in enumerate(source...]
    pallas_call x4 -> x2, Pallas kernels: 8.83 us -> 1.57 us  [choose(): pl.pallas_call(functools.partial(choose_body, places), in_specs=[pl.Block...]
    ppermute x2, waiting for transfers between devices: 0.01 us -> 6.35 us  [near_inside(): lax.ppermute(data, 'band', [(source, b) for b, source in enumerate(source...]
    ppermute x4 -> x1, starting transfers between devices: 12.7 us -> 8.22 us  [shards(): lax.ppermute(far, ('band', 'grid'), [(2 * a + 1 - slab, 2 * b + slab) for...]
    unnamed x14 -> x10, local copies, waits for them, and re-layouts: 3.64 us -> 1.53 us
    ppermute x4 -> x1, waiting for transfers between devices: 18.5 us -> 19.2 us  [shards(): lax.ppermute(far, ('band', 'grid'), [(2 * a + 1 - slab, 2 * b + slab) for...]
  transfers between devices with their start and end apart: 13 -> 12, of which waited for: 3 -> 5; matrix products, arithmetic and copies ran while one was open for 0% -> 0% of each run, Pallas kernels for 44% -> 29%
where the time goes in v2:
time: 116 us
  waiting for transfers between devices  47.5 us (41%)
  Pallas kernels  38 us (33%)
  starting transfers between devices  28.6 us (25%)
  local copies, waits for them, and re-layouts  1.53 us (1%)
    pallas_call x6, Pallas kernels, unit(): pl.pallas_call(body, in_specs=[scalar] + [pl.BlockSpec(memory_space=pl.AN...  33.3 us
    ppermute x1, waiting for transfers between devices, shards(): lax.ppermute(far, ('band', 'grid'), [(2 * a + 1 - slab, 2 * b + slab) for...  19.2 us
    ppermute x1, waiting for transfers between devices, shards(): far = lax.ppermute(near, 'grid', [(0, 1), (1, 0)])  14.4 us
    ppermute x8, starting transfers between devices, from_place(): lax.ppermute(data, 'band', [(source, b) for b, source in enumerate(source...  12 us
    ppermute x1, starting transfers between devices, shards(): lax.ppermute(far, ('band', 'grid'), [(2 * a + 1 - slab, 2 * b + slab) for...  8.22 us
    ppermute x8, waiting for transfers between devices, from_place(): lax.ppermute(data, 'band', [(source, b) for b, source in enumerate(source...  7.6 us
    ppermute x2, waiting for transfers between devices, near_inside(): lax.ppermute(data, 'band', [(source, b) for b, source in enumerate(source...  6.35 us
    ppermute x2, starting transfers between devices, near_inside(): lax.ppermute(data, 'band', [(source, b) for b, source in enumerate(source...  4.46 us
  transfers between devices with their start and end apart: 12, of which 5 were waited for; matrix products, arithmetic and copies ran while one was open for 0% of the time, Pallas kernels for 29%

profile of v2, /device:TPU:1, one launch (start us, length us, event | category | flops | bytes accessed | tf_op | source)
XLA Modules:
  0.0 115.8 jit_solution(1320043260325139211)
XLA Ops:
  0.0 0.0 copy-start
  0.0 0.0 copy-start.1
  0.0 1.5 %copy-done.1 = f32[1,40,80,80]{3,2,1,0:T(8,128)S(1)} copy-done((f32[1,40,80,80]{3,2,1,0:T(8,128)S(1)}, f32[1,40,80,80]{3,2,1,0:T(8,128)}, u32[]{:S(2)}) %copy-start.1) | copy-done | bytes 1024024
  1.5 0.0 copy-start.2
  1.5 0.0 copy-start.3
  1.5 0.0 copy-start.4
  1.5 0.9 pack.1.refs_2_.refs_0_.refs_1_
  2.5 3.8 %collective-permute-start.2 = (f32[25,80,128]{2,1,0:T(8,128)S(1)}, f32[25,80,128]{2,1,0:T(8,128)S(1)}, u32[]{:S(2)}, u32[]{:S(2)}) collective-permute-start(f32[25,80,128]{2,1,0:T(8,128)S(1)} %pack.1.refs_2_.refs_0_.refs_1_), channel_id=1, source_target_pairs={{0,1},{1,0},{2,3},{3,2},{4,5},{5,4},{6,7},{7,6},{8,9},{9,8},{10,11... | collective-permute-start | bytes 3072008 | tf_op jit(solution)/shard_map/ppermute | solution.py:391
  6.3 3.2 %collective-permute-start.1 = (f32[25,80,128]{2,1,0:T(8,128)S(1)}, f32[25,80,128]{2,1,0:T(8,128)S(1)}, u32[]{:S(2)}, u32[]{:S(2)}) collective-permute-start(f32[25,80,128]{2,1,0:T(8,128)S(1)} %pack.1.refs_2_.refs_0_.refs_1_), channel_id=1, source_target_pairs={{4,0},{8,4},{2,6},{12,8},{6,10},{16,12},{10,14},{20,16},{14,18},{2... | collective-permute-start | bytes 3072008 | tf_op jit(solution)/shard_map/ppermute | solution.py:379
  9.5 1.3 %collective-permute-start = (f32[25,80,128]{2,1,0:T(8,128)S(1)}, f32[25,80,128]{2,1,0:T(8,128)S(1)}, u32[]{:S(2)}, u32[]{:S(2)}) collective-permute-start(f32[25,80,128]{2,1,0:T(8,128)S(1)} %pack.1.refs_2_.refs_0_.refs_1_), channel_id=1, source_target_pairs={{6,2},{0,4},{10,6},{4,8},{14,10},{8,12},{18,14},{12,16},{22,18},{1... | collective-permute-start | bytes 3072008 | tf_op jit(solution)/shard_map/ppermute | solution.py:379
  10.8 2.5 %collective-permute-start.4 = (f32[25,80,128]{2,1,0:T(8,128)S(1)}, f32[25,80,128]{2,1,0:T(8,128)S(1)}, u32[]{:S(2)}, u32[]{:S(2)}) collective-permute-start(f32[25,80,128]{2,1,0:T(8,128)S(1)} %pack.1.refs_2_.refs_0_.refs_1_), channel_id=1, source_target_pairs={{2,0},{0,2},{6,4},{4,6},{10,8},{8,10},{14,12},{12,14},{18,16},{16,... | collective-permute-start | bytes 3072008 | tf_op jit(solution)/shard_map/ppermute | solution.py:376
  13.2 14.4 %collective-permute-done.2.refs_4_.refs_2_.refs_3_ = f32[25,80,128]{2,1,0:T(8,128)S(1)} collective-permute-done((f32[25,80,128]{2,1,0:T(8,128)S(1)}, f32[25,80,128]{2,1,0:T(8,128)S(1)}, u32[]{:S(2)}, u32[]{:S(2)}) %collective-permute-start.2) | collective-permute-done | bytes 1024032 | tf_op jit(solution)/shard_map/ppermute | solution.py:391
  27.6 0.3 collective-permute-done.1.refs_0_.b
  27.9 6.0 %collective-permute-done.refs_1_.b = f32[25,80,128]{2,1,0:T(8,128)S(1)} collective-permute-done((f32[25,80,128]{2,1,0:T(8,128)S(1)}, f32[25,80,128]{2,1,0:T(8,128)S(1)}, u32[]{:S(2)}, u32[]{:S(2)}) %collective-permute-start) | collective-permute-done | bytes 1024032 | tf_op jit(solution)/shard_map/ppermute | solution.py:379
  33.9 0.0 collective-permute-start.5
  33.9 1.2 %collective-permute-start.3 = (f32[25,80,128]{2,1,0:T(8,128)S(1)}, f32[25,80,128]{2,1,0:T(8,128)S(1)}, u32[]{:S(2)}, u32[]{:S(2)}) collective-permute-start(f32[25,80,128]{2,1,0:T(8,128)S(1)} %collective-permute-done.2.refs_4_.refs_2_.refs_3_), channel_id=1, source_target_pairs={{4,0},{254,2},{8,4},{2,6},{12,8},{6,10},{16,12},{10,14},{20,16},{1... | collective-permute-start | bytes 3072008 | tf_op jit(solution)/shard_map/ppermute | solution.py:376
  35.2 8.2 %collective-permute-start.6 = (f32[25,80,128]{2,1,0:T(8,128)S(1)}, f32[25,80,128]{2,1,0:T(8,128)S(1)}, u32[]{:S(2)}, u32[]{:S(2)}) collective-permute-start(f32[25,80,128]{2,1,0:T(8,128)S(1)} %collective-permute-done.2.refs_4_.refs_2_.refs_3_), channel_id=1, source_target_pairs={{255,2},{254,3},{129,124},{128,125},{127,130},{126,131},{1,252},{0... | collective-permute-start | bytes 3072008 | tf_op jit(solution)/shard_map/ppermute | solution.py:397
  43.4 0.0 collective-permute-done.4.refs_3_.refs_1_.refs_0_
  43.4 0.0 collective-permute-done.5.refs_5_.refs_3_.refs_2_
  43.4 0.0 copy-done
  43.4 0.0 copy-done.2
  43.4 0.0 copy-done.3
  43.4 0.0 copy-done.4
  43.4 5.1 %unit.6 = (f32[25,80,128]{2,1,0:T(8,128)S(1)}, s32[1,1]{1,0:T(1,128)}, f32[25,80,128]{2,1,0:T(8,128)S(1)}) custom-call(s32[1,1]{1,0:T(1,128)} %constant.4.clone.1.order, f32[25,80,128]{2,1,0:T(8,128)S(1)} %collective-permute-done.1.refs_0_.b, f32[25,80,128]{2,1,0:T(8,128)S(1)} %collective-permute-done.refs_1_.b, ...), custom_call_target="tpu_custom_call" | custom-call | flops 1 | bytes 1 | tf_op jit(solution)/shard_map/unit/pallas_call | solution.py:267
  48.6 7.6 %collective-permute-done.3.refs_3_.refs_2_.refs_4_ = f32[25,80,128]{2,1,0:T(8,128)S(1)} collective-permute-done((f32[25,80,128]{2,1,0:T(8,128)S(1)}, f32[25,80,128]{2,1,0:T(8,128)S(1)}, u32[]{:S(2)}, u32[]{:S(2)}) %collective-permute-start.3) | collective-permute-done | bytes 1024032 | tf_op jit(solution)/shard_map/ppermute | solution.py:376
  56.1 19.2 %collective-permute-done.6.a = f32[25,80,128]{2,1,0:T(8,128)S(1)} collective-permute-done((f32[25,80,128]{2,1,0:T(8,128)S(1)}, f32[25,80,128]{2,1,0:T(8,128)S(1)}, u32[]{:S(2)}, u32[]{:S(2)}) %collective-permute-start.6) | collective-permute-done | bytes 1024032 | tf_op jit(solution)/shard_map/ppermute | solution.py:397
  75.3 0.8 choose.2.refs_1_.refs_0_.refs_2_
  76.1 0.1 collective-permute-start.7
  76.3 0.5 collective-permute-start.8
  76.7 5.8 %collective-permute-start.9 = (f32[25,80,128]{2,1,0:T(8,128)S(1)}, f32[25,80,128]{2,1,0:T(8,128)S(1)}, u32[]{:S(2)}, u32[]{:S(2)}) collective-permute-start(f32[25,80,128]{2,1,0:T(8,128)S(1)} %get-tuple-element.31), channel_id=1, source_target_pairs={{252,0},{6,2},{0,4},{10,6},{4,8},{14,10},{8,12},{18,14},{12,16},{2... | collective-permute-start | bytes 3072008 | tf_op jit(solution)/shard_map/ppermute | solution.py:376
  82.6 5.7 %unit.7 = (f32[25,80,128]{2,1,0:T(8,128)S(1)}, s32[1,1]{1,0:T(1,128)}) custom-call(s32[1,1]{1,0:T(1,128)} %get-tuple-element.26.order, f32[25,80,128]{2,1,0:T(8,128)S(1)} %pack.1.refs_2_.refs_0_.refs_1_, f32[25,80,128]{2,1,0:T(8,128)S(1)} %choose.2.refs_1_.refs_0_.refs_2_, f32[25,80,128]{2,1,0:T(8,128)S(1)} %collective-permute-done.2.refs_4_.refs_2_.refs_3_, ...), custom_call_target="tpu_custom_call" | custom-call | flops 1 | bytes 1 | tf_op jit(solution)/shard_map/unit/pallas_call | solution.py:267
  88.2 0.0 collective-permute-done.7.refs_1_
  88.3 0.0 collective-permute-done.8.refs_3_
  88.3 5.6 %unit.8 = (f32[25,80,128]{2,1,0:T(8,128)S(1)}, s32[1,1]{1,0:T(1,128)}) custom-call(s32[1,1]{1,0:T(1,128)} %get-tuple-element.29.order, f32[25,80,128]{2,1,0:T(8,128)S(1)} %choose.2.refs_1_.refs_0_.refs_2_, f32[25,80,128]{2,1,0:T(8,128)S(1)} %collective-permute-done.7.refs_1_, f32[25,80,128]{2,1,0:T(8,128)S(1)} %collective-permute-done.3.refs_3_.refs_2_.refs_4_, ...), custom_call_target="tpu_custom_call" | custom-call | flops 1 | bytes 1 | tf_op jit(solution)/shard_map/unit/pallas_call | solution.py:267
  93.9 0.3 collective-permute-start.10
  94.2 0.0 collective-permute-done.9.refs_0_.refs_3_.refs_4_
  94.2 5.7 %unit.9 = (f32[25,80,128]{2,1,0:T(8,128)S(1)}, s32[1,1]{1,0:T(1,128)}) custom-call(s32[1,1]{1,0:T(1,128)} %get-tuple-element.30.order, f32[25,80,128]{2,1,0:T(8,128)S(1)} %collective-permute-done.9.refs_0_.refs_3_.refs_4_, f32[25,80,128]{2,1,0:T(8,128)S(1)} %collective-permute-done.4.refs_3_.refs_1_.refs_0_, ...), custom_call_target="tpu_custom_call" | custom-call | flops 1 | bytes 1 | tf_op jit(solution)/shard_map/unit/pallas_call | solution.py:267
  99.8 0.8 choose.3.refs_1_.refs_2_
  100.6 5.6 %unit.10 = (f32[25,80,128]{2,1,0:T(8,128)S(1)}, s32[1,1]{1,0:T(1,128)}) custom-call(s32[1,1]{1,0:T(1,128)} %get-tuple-element.32.order, f32[25,80,128]{2,1,0:T(8,128)S(1)} %collective-permute-done.4.refs_3_.refs_1_.refs_0_, f32[25,80,128]{2,1,0:T(8,128)S(1)} %choose.3.refs_1_.refs_2_, f32[25,80,128]{2,1,0:T(8,128)S(1)} %collective-permute-done.5.refs_5_.refs_3_.refs_2_, ...), custom_call_target="tpu_custom_call" | custom-call | flops 1 | bytes 1 | tf_op jit(solution)/shard_map/unit/pallas_call | solution.py:267
  106.3 1.7 %collective-permute-start.11 = (f32[25,80,128]{2,1,0:T(8,128)S(1)}, f32[25,80,128]{2,1,0:T(8,128)S(1)}, u32[]{:S(2)}, u32[]{:S(2)}) collective-permute-start(f32[25,80,128]{2,1,0:T(8,128)S(1)} %get-tuple-element.38), channel_id=1, source_target_pairs={{2,0},{0,2},{6,4},{4,6},{10,8},{8,10},{14,12},{12,14},{18,16},{16,... | collective-permute-start | bytes 3072008 | tf_op jit(solution)/shard_map/ppermute | solution.py:376
  107.9 0.0 collective-permute-done.10.refs_0_.returned
  107.9 5.6 %unit.11 = (f32[25,80,128]{2,1,0:T(8,128)S(1)}, s32[1,1]{1,0:T(1,128)}) custom-call(s32[1,1]{1,0:T(1,128)} %get-tuple-element.34.order, f32[25,80,128]{2,1,0:T(8,128)S(1)} %collective-permute-done.10.refs_0_.returned, f32[25,80,128]{2,1,0:T(8,128)S(1)} %pack.1.refs_2_.refs_0_.refs_1_, f32[25,80,128]{2,1,0:T(8,128)S(1)} %choose.3.refs_1_.refs_2_, ...), custom_call_target="tpu_custom_call" | custom-call | flops 1 | bytes 1 | tf_op jit(solution)/shard_map/unit/pallas_call | solution.py:267
  113.6 0.0 collective-permute-done.11.theirs
  113.6 2.1 %unpack_sum.1 = f32[40,80,80]{2,1,0:T(8,128)} custom-call(f32[25,80,128]{2,1,0:T(8,128)S(1)} %get-tuple-element.37.total, f32[25,80,128]{2,1,0:T(8,128)S(1)} %collective-permute-done.10.refs_0_.returned, f32[25,80,128]{2,1,0:T(8,128)S(1)} %collective-permute-done.11.theirs), custom_call_target="tpu_custom_call" | custom-call | tf_op jit(solution)/shard_map/unpack_sum/pallas_call | solution.py:356
Async XLA Ops:
  0.0 43.4 %copy-start = (f32[6,41,8,128]{3,2,1,0:T(8,128)S(1)}, f32[6,41,8,128]{3,2,1,0:T(8,128)}, u32[]{:S(2)}) copy-start(f32[6,41,8,128]{3,2,1,0:T(8,128)} %constant.13.clone.refs_9_.refs_7_.refs_8_) | copy-start | bytes 3022852
  0.0 1.5 %copy-start.1 = (f32[1,40,80,80]{3,2,1,0:T(8,128)S(1)}, f32[1,40,80,80]{3,2,1,0:T(8,128)}, u32[]{:S(2)}) copy-start(f32[1,40,80,80]{3,2,1,0:T(8,128)} %param.5) | copy-start | bytes 3072004
  1.5 41.9 %copy-start.2 = (bf16[80,240]{1,0:T(8,128)(2,1)S(1)}, bf16[80,240]{1,0:T(8,128)(2,1)}, u32[]{:S(2)}) copy-start(bf16[80,240]{1,0:T(8,128)(2,1)} %constant.12.clone.refs_8_.refs_6_.refs_7_) | copy-start | bytes 115204
  1.5 41.9 %copy-start.3 = (bf16[80,240]{1,0:T(8,128)(2,1)S(1)}, bf16[80,240]{1,0:T(8,128)(2,1)}, u32[]{:S(2)}) copy-start(bf16[80,240]{1,0:T(8,128)(2,1)} %constant.11.clone.refs_7_.refs_5_.refs_6_) | copy-start | bytes 115204
  1.5 41.9 %copy-start.4 = (bf16[80,240]{1,0:T(8,128)(2,1)S(1)}, bf16[80,240]{1,0:T(8,128)(2,1)}, u32[]{:S(2)}) copy-start(bf16[80,240]{1,0:T(8,128)(2,1)} %constant.10.clone.refs_6_.refs_4_.refs_5_) | copy-start | bytes 115204
  2.5 25.1 %collective-permute-start.2 = (f32[25,80,128]{2,1,0:T(8,128)S(1)}, f32[25,80,128]{2,1,0:T(8,128)S(1)}, u32[]{:S(2)}, u32[]{:S(2)}) collective-permute-start(f32[25,80,128]{2,1,0:T(8,128)S(1)} %pack.1.refs_2_.refs_0_.refs_1_), channel_id=1, source_target_pairs={{0,1},{1,0},{2,3},{3,2},{4,5},{5,4},{6,7},{7,6},{8,9},{9,8},{10,11... | collective-permute-start | bytes 3072008 | tf_op jit(solution)/shard_map/ppermute | solution.py:391
  6.3 21.6 %collective-permute-start.1 = (f32[25,80,128]{2,1,0:T(8,128)S(1)}, f32[25,80,128]{2,1,0:T(8,128)S(1)}, u32[]{:S(2)}, u32[]{:S(2)}) collective-permute-start(f32[25,80,128]{2,1,0:T(8,128)S(1)} %pack.1.refs_2_.refs_0_.refs_1_), channel_id=1, source_target_pairs={{4,0},{8,4},{2,6},{12,8},{6,10},{16,12},{10,14},{20,16},{14,18},{2... | collective-permute-start | bytes 3072008 | tf_op jit(solution)/shard_map/ppermute | solution.py:379
  9.5 24.5 %collective-permute-start = (f32[25,80,128]{2,1,0:T(8,128)S(1)}, f32[25,80,128]{2,1,0:T(8,128)S(1)}, u32[]{:S(2)}, u32[]{:S(2)}) collective-permute-start(f32[25,80,128]{2,1,0:T(8,128)S(1)} %pack.1.refs_2_.refs_0_.refs_1_), channel_id=1, source_target_pairs={{6,2},{0,4},{10,6},{4,8},{14,10},{8,12},{18,14},{12,16},{22,18},{1... | collective-permute-start | bytes 3072008 | tf_op jit(solution)/shard_map/ppermute | solution.py:379
  10.8 32.6 %collective-permute-start.4 = (f32[25,80,128]{2,1,0:T(8,128)S(1)}, f32[25,80,128]{2,1,0:T(8,128)S(1)}, u32[]{:S(2)}, u32[]{:S(2)}) collective-permute-start(f32[25,80,128]{2,1,0:T(8,128)S(1)} %pack.1.refs_2_.refs_0_.refs_1_), channel_id=1, source_target_pairs={{2,0},{0,2},{6,4},{4,6},{10,8},{8,10},{14,12},{12,14},{18,16},{16,... | collective-permute-start | bytes 3072008 | tf_op jit(solution)/shard_map/ppermute | solution.py:376
  33.9 9.5 %collective-permute-start.5 = (f32[25,80,128]{2,1,0:T(8,128)S(1)}, f32[25,80,128]{2,1,0:T(8,128)S(1)}, u32[]{:S(2)}, u32[]{:S(2)}) collective-permute-start(f32[25,80,128]{2,1,0:T(8,128)S(1)} %collective-permute-done.2.refs_4_.refs_2_.refs_3_), channel_id=1, source_target_pairs={{2,0},{0,2},{6,4},{4,6},{10,8},{8,10},{14,12},{12,14},{18,16},{16,... | collective-permute-start | bytes 3072008 | tf_op jit(solution)/shard_map/ppermute | solution.py:376
  33.9 22.2 %collective-permute-start.3 = (f32[25,80,128]{2,1,0:T(8,128)S(1)}, f32[25,80,128]{2,1,0:T(8,128)S(1)}, u32[]{:S(2)}, u32[]{:S(2)}) collective-permute-start(f32[25,80,128]{2,1,0:T(8,128)S(1)} %collective-permute-done.2.refs_4_.refs_2_.refs_3_), channel_id=1, source_target_pairs={{4,0},{254,2},{8,4},{2,6},{12,8},{6,10},{16,12},{10,14},{20,16},{1... | collective-permute-start | bytes 3072008 | tf_op jit(solution)/shard_map/ppermute | solution.py:376
  35.2 40.2 %collective-permute-start.6 = (f32[25,80,128]{2,1,0:T(8,128)S(1)}, f32[25,80,128]{2,1,0:T(8,128)S(1)}, u32[]{:S(2)}, u32[]{:S(2)}) collective-permute-start(f32[25,80,128]{2,1,0:T(8,128)S(1)} %collective-permute-done.2.refs_4_.refs_2_.refs_3_), channel_id=1, source_target_pairs={{255,2},{254,3},{129,124},{128,125},{127,130},{126,131},{1,252},{0... | collective-permute-start | bytes 3072008 | tf_op jit(solution)/shard_map/ppermute | solution.py:397
  76.1 12.1 %collective-permute-start.7 = (f32[25,80,128]{2,1,0:T(8,128)S(1)}, f32[25,80,128]{2,1,0:T(8,128)S(1)}, u32[]{:S(2)}, u32[]{:S(2)}) collective-permute-start(f32[25,80,128]{2,1,0:T(8,128)S(1)} %choose.2.refs_1_.refs_0_.refs_2_), channel_id=1, source_target_pairs={{2,0},{0,2},{6,4},{4,6},{10,8},{8,10},{14,12},{12,14},{18,16},{16,... | collective-permute-start | bytes 3072008 | tf_op jit(solution)/shard_map/ppermute | solution.py:376
  76.3 12.0 %collective-permute-start.8 = (f32[25,80,128]{2,1,0:T(8,128)S(1)}, f32[25,80,128]{2,1,0:T(8,128)S(1)}, u32[]{:S(2)}, u32[]{:S(2)}) collective-permute-start(f32[25,80,128]{2,1,0:T(8,128)S(1)} %collective-permute-done.3.refs_3_.refs_2_.refs_4_), channel_id=1, source_target_pairs={{2,0},{0,2},{6,4},{4,6},{10,8},{8,10},{14,12},{12,14},{18,16},{16,... | collective-permute-start | bytes 3072008 | tf_op jit(solution)/shard_map/ppermute | solution.py:376
  76.7 17.4 %collective-permute-start.9 = (f32[25,80,128]{2,1,0:T(8,128)S(1)}, f32[25,80,128]{2,1,0:T(8,128)S(1)}, u32[]{:S(2)}, u32[]{:S(2)}) collective-permute-start(f32[25,80,128]{2,1,0:T(8,128)S(1)} %get-tuple-element.31), channel_id=1, source_target_pairs={{252,0},{6,2},{0,4},{10,6},{4,8},{14,10},{8,12},{18,14},{12,16},{2... | collective-permute-start | bytes 3072008 | tf_op jit(solution)/shard_map/ppermute | solution.py:376
  93.9 14.1 %collective-permute-start.10 = (f32[25,80,128]{2,1,0:T(8,128)S(1)}, f32[25,80,128]{2,1,0:T(8,128)S(1)}, u32[]{:S(2)}, u32[]{:S(2)}) collective-permute-start(f32[25,80,128]{2,1,0:T(8,128)S(1)} %get-tuple-element.35), channel_id=1, source_target_pairs={{252,0},{6,2},{0,4},{10,6},{4,8},{14,10},{8,12},{18,14},{12,16},{2... | collective-permute-start | bytes 3072008 | tf_op jit(solution)/shard_map/ppermute | solution.py:376
  106.3 7.3 %collective-permute-start.11 = (f32[25,80,128]{2,1,0:T(8,128)S(1)}, f32[25,80,128]{2,1,0:T(8,128)S(1)}, u32[]{:S(2)}, u32[]{:S(2)}) collective-permute-start(f32[25,80,128]{2,1,0:T(8,128)S(1)} %get-tuple-element.38), channel_id=1, source_target_pairs={{2,0},{0,2},{6,4},{4,6},{10,8},{8,10},{14,12},{12,14},{18,16},{16,... | collective-permute-start | bytes 3072008 | tf_op jit(solution)/shard_map/ppermute | solution.py:376

commit v3 on v2

--- a/solution.py
+++ b/solution.py
@@ -243,18 +243,11 @@
         backward_y(group)
 
 
-def unit(a, b, constants, after, total=None, waits=(), again=False):
+def unit(a, b, constants, after, total=None, waits=()):
     operands = [a[0], b[0], a[1], b[1], *constants]
 
     def body(order, *refs):
-        refs = list(refs[len(waits) :])
-        if again:
-            copied = refs.pop(len(operands) + (total is not None) + 2)
-
-            @pl.loop(0, GROUPS * PLANES)
-            def _(plane):
-                copied[plane] = refs[2][plane]
-
+        refs = refs[len(waits) :]
         ins, rest = refs[: len(operands)], refs[len(operands) :]
         if total is None:
             unit_body(*ins, None, *rest)
@@ -267,9 +260,8 @@
     return pl.pallas_call(
         body,
         in_specs=[scalar] + [pl.BlockSpec(memory_space=pl.ANY)] * len(waits) + [here] * len(operands_all),
-        out_specs=(here, scalar) + (here,) * again,
-        out_shape=(jax.ShapeDtypeStruct(PACKED, F32), jax.ShapeDtypeStruct((1, 1), jnp.int32))
-        + (jax.ShapeDtypeStruct(PACKED, F32),) * again,
+        out_specs=(here, scalar),
+        out_shape=(jax.ShapeDtypeStruct(PACKED, F32), jax.ShapeDtypeStruct((1, 1), jnp.int32)),
         scratch_shapes=[
             pltpu.VMEM((N, N, LANES), F32),
             pltpu.VMEM((HALF, N, LANES), F32),
@@ -369,19 +361,25 @@
     def sources(distance):
         return [(b + distance * sides[b]) % bands for b in range(bands)]
 
-    def crosses(b, source):
-        return b // half != source // half
+    def takers(distance):
+        return [b for b, source in enumerate(sources(distance)) if b // half != source // half]
 
     def from_place(data, distance):
         return lax.ppermute(data, "band", [(source, b) for b, source in enumerate(sources(distance))])
 
-    def near_inside(data, distance):
-        return lax.ppermute(
-            data, "band", [(source, b) for b, source in enumerate(sources(distance)) if not crosses(b, source)]
-        )
-
-    def across(distance):
-        return [(source, b) for b, source in enumerate(sources(distance)) if crosses(b, source)]
+    def from_half(data, distance):
+        return lax.ppermute(data, "band", [(b // half * half + source % half, b) for b, source in enumerate(sources(distance))])
+
+    def swapped_halves(data, distance):
+        return lax.ppermute(data, "band", [((b + half) % bands, b) for b in takers(distance)])
+
+    def far_slabs(near, far, distance, after):
+        route = []
+        for b, source in enumerate(sources(distance)):
+            for slab in range(2):
+                route.append((2 * source + (1 - slab if b in takers(distance) else slab), 2 * b + slab))
+        across = [sources(distance)[b] for b in takers(distance)]
+        return lax.ppermute(choose(across, near, far, after), ("band", "grid"), route)
 
     def other_core(data):
         return from_place(data, -1)
@@ -389,27 +387,25 @@
     constants = tuple(jnp.asarray(t) for t in (*tables(), screened_kernel()))
     near = pack(orbitals[0])
     far = lax.ppermute(near, "grid", [(0, 1), (1, 0)])
-    m2_inside = near_inside(near, -2)
-    p2_inside = near_inside(near, 2)
-    p2_inside, m2_inside, far = lax.optimization_barrier((p2_inside, m2_inside, far))
+    m2_half = from_half(near, -2)
+    p2_half = from_half(near, 2)
+    far, m2_half, p2_half = lax.optimization_barrier((far, m2_half, p2_half))
     own = (near, far)
-    m2_far = from_place(far, -2)
-    crossed = lax.ppermute(
-        far, ("band", "grid"), [(2 * a + 1 - slab, 2 * b + slab) for a, b in across(-2) + across(2) for slab in range(2)]
-    )
-    m2_takes, p2_takes = ([b for _, b in across(distance)] for distance in (-2, 2))
+    first = jnp.zeros((1, 1), jnp.int32)
+    m2_far = far_slabs(near, far, -2, first)
+    m2_swapped = swapped_halves(m2_half, -2)
     m1 = (other_core(near), other_core(far))
-    first = jnp.zeros((1, 1), jnp.int32)
-    total, after, far_later = unit(own, m1, constants, first, waits=(m2_inside, p2_inside), again=True)
-    p2_far = from_place(far_later, 2)
-    m2_far, after = lax.optimization_barrier((m2_far, after))
-    m2 = (choose(m2_takes, crossed, m2_inside, after), m2_far)
+    total, after = unit(own, m1, constants, first)
+    p2_far = far_slabs(near, far, 2, after)
+    m2_far, p2_half, after = lax.optimization_barrier((m2_far, p2_half, after))
+    p2_swapped = swapped_halves(p2_half, 2)
+    m2 = (choose(takers(-2), m2_swapped, m2_half, after), m2_far)
     p1 = (other_core(m2[0]), other_core(m2_far))
     total, after = unit(own, m2, constants, after, total)
     lent, after = unit(m2, p1, constants, after)
     returned = from_place(lent, 2)
     partner, after = unit(m1, m2, constants, after, waits=(p2_far,))
-    p2 = (choose(p2_takes, crossed, p2_inside, after), p2_far)
+    p2 = (choose(takers(2), p2_swapped, p2_half, after), p2_far)
     partner, after = unit(m1, p2, constants, after, partner)
     theirs = other_core(partner)
     total, after = unit(own, p2, constants, after, total, waits=(returned,))

time: 116 us -> 99.6 us (0.86)
  waiting for transfers between devices: 47.5 us -> 31.2 us
    ppermute x8 -> x6, waiting for transfers between devices: 7.6 us -> 0.02 us  [from_place(): lax.ppermute(data, 'band', [(source, b) for b, source in enumerate(source...]
    ppermute x3 -> x6, waiting for transfers between devices: 25.6 us -> 18.9 us  [the longest x2 11.4 us: far_slabs(): lax.ppermute(choose(across, near, far, after), ('band', 'grid'), route)]
    ppermute x8 -> x6, starting transfers between devices: 12 us -> 6.71 us  [from_place(): lax.ppermute(data, 'band', [(source, b) for b, source in enumerate(source...]
    ppermute x3 -> x6, starting transfers between devices: 12.7 us -> 17.2 us  [the longest x2 7.77 us: from_half(): lax.ppermute(data, 'band', [(b // half * half + source % half, b) for b,...]
    ppermute x1, waiting for transfers between devices: 14.4 us -> 12.3 us  [shards(): far = lax.ppermute(near, 'grid', [(0, 1), (1, 0)])]
    pallas_call x2 -> x4, Pallas kernels: 1.57 us -> 2.48 us  [choose(): pl.pallas_call(functools.partial(choose_body, places), in_specs=[pl.Block...]
  transfers between devices with their start and end apart: 12 -> 13, of which waited for: 5 -> 4; matrix products, arithmetic and copies ran while one was open for 0% -> 0% of each run, Pallas kernels for 29% -> 35%
where the time goes in v3:
time: 99.6 us; the launch traced here: 99.4 us
  Pallas kernels  38.8 us (39%)
  waiting for transfers between devices  31.2 us (31%)
  starting transfers between devices  27.7 us (28%)
  local copies, waits for them, and re-layouts  1.46 us (1%)
    pallas_call x6, Pallas kernels, unit(): pl.pallas_call(body, in_specs=[scalar] + [pl.BlockSpec(memory_space=pl.AN...  33.2 us
    ppermute x1, waiting for transfers between devices, shards(): far = lax.ppermute(near, 'grid', [(0, 1), (1, 0)])  12.3 us
    ppermute x2, waiting for transfers between devices, far_slabs(): lax.ppermute(choose(across, near, far, after), ('band', 'grid'), route)  11.4 us
    ppermute x2, starting transfers between devices, from_half(): lax.ppermute(data, 'band', [(b // half * half + source % half, b) for b,...  7.77 us
    ppermute x2, waiting for transfers between devices, from_half(): lax.ppermute(data, 'band', [(b // half * half + source % half, b) for b,...  7.46 us
    ppermute x6, starting transfers between devices, from_place(): lax.ppermute(data, 'band', [(source, b) for b, source in enumerate(source...  6.71 us
    ppermute x2, starting transfers between devices, far_slabs(): lax.ppermute(choose(across, near, far, after), ('band', 'grid'), route)  6.18 us
    ppermute x1, starting transfers between devices, shards(): far = lax.ppermute(near, 'grid', [(0, 1), (1, 0)])  3.83 us
  transfers between devices with their start and end apart: 13, of which 4 were waited for; matrix products, arithmetic and copies ran while one was open for 0% of the time, Pallas kernels for 35%

profile of v3, /device:TPU:1, one launch (start us, length us, event | category | flops | bytes accessed | tf_op | source)
XLA Modules:
  0.0 99.4 jit_solution(16078067126979832526)
XLA Ops:
  0.0 0.0 copy-start.1
  0.0 1.4 %copy-done.1 = f32[1,40,80,80]{3,2,1,0:T(8,128)S(1)} copy-done((f32[1,40,80,80]{3,2,1,0:T(8,128)S(1)}, f32[1,40,80,80]{3,2,1,0:T(8,128)}, u32[]{:S(2)}) %copy-start.1) | copy-done | bytes 1024024
  1.4 0.9 pack.1.a.refs_0_.refs_1_
  2.4 0.0 copy-start
  2.4 0.0 copy-start.2
  2.4 0.0 copy-start.3
  2.4 0.0 copy-start.4
  2.4 3.8 %collective-permute-start = (f32[25,80,128]{2,1,0:T(8,128)S(1)}, f32[25,80,128]{2,1,0:T(8,128)S(1)}, u32[]{:S(2)}, u32[]{:S(2)}) collective-permute-start(f32[25,80,128]{2,1,0:T(8,128)S(1)} %pack.1.a.refs_0_.refs_1_), channel_id=1, source_target_pairs={{0,1},{1,0},{2,3},{3,2},{4,5},{5,4},{6,7},{7,6},{8,9},{9,8},{10,11... | collective-permute-start | bytes 3072008 | tf_op jit(solution)/shard_map/ppermute | solution.py:389
  6.2 1.2 %collective-permute-start.1 = (f32[25,80,128]{2,1,0:T(8,128)S(1)}, f32[25,80,128]{2,1,0:T(8,128)S(1)}, u32[]{:S(2)}, u32[]{:S(2)}) collective-permute-start(f32[25,80,128]{2,1,0:T(8,128)S(1)} %pack.1.a.refs_0_.refs_1_), channel_id=1, source_target_pairs={{4,0},{126,2},{8,4},{2,6},{12,8},{6,10},{16,12},{10,14},{20,16},{1... | collective-permute-start | bytes 3072008 | tf_op jit(solution)/shard_map/ppermute | solution.py:371
  7.5 6.6 %collective-permute-start.2 = (f32[25,80,128]{2,1,0:T(8,128)S(1)}, f32[25,80,128]{2,1,0:T(8,128)S(1)}, u32[]{:S(2)}, u32[]{:S(2)}) collective-permute-start(f32[25,80,128]{2,1,0:T(8,128)S(1)} %pack.1.a.refs_0_.refs_1_), channel_id=1, source_target_pairs={{124,0},{6,2},{0,4},{10,6},{4,8},{14,10},{8,12},{18,14},{12,16},{2... | collective-permute-start | bytes 3072008 | tf_op jit(solution)/shard_map/ppermute | solution.py:371
  14.0 1.2 %collective-permute-start.4 = (f32[25,80,128]{2,1,0:T(8,128)S(1)}, f32[25,80,128]{2,1,0:T(8,128)S(1)}, u32[]{:S(2)}, u32[]{:S(2)}) collective-permute-start(f32[25,80,128]{2,1,0:T(8,128)S(1)} %pack.1.a.refs_0_.refs_1_), channel_id=1, source_target_pairs={{2,0},{0,2},{6,4},{4,6},{10,8},{8,10},{14,12},{12,14},{18,16},{16,... | collective-permute-start | bytes 3072008 | tf_op jit(solution)/shard_map/ppermute | solution.py:368
  15.3 12.3 %collective-permute-done.b.refs_2_.refs_3_ = f32[25,80,128]{2,1,0:T(8,128)S(1)} collective-permute-done((f32[25,80,128]{2,1,0:T(8,128)S(1)}, f32[25,80,128]{2,1,0:T(8,128)S(1)}, u32[]{:S(2)}, u32[]{:S(2)}) %collective-permute-start) | collective-permute-done | bytes 1024032 | tf_op jit(solution)/shard_map/ppermute | solution.py:389
  27.5 3.1 %collective-permute-done.1.b = f32[25,80,128]{2,1,0:T(8,128)S(1)} collective-permute-done((f32[25,80,128]{2,1,0:T(8,128)S(1)}, f32[25,80,128]{2,1,0:T(8,128)S(1)}, u32[]{:S(2)}, u32[]{:S(2)}) %collective-permute-start.1) | collective-permute-done | bytes 1024032 | tf_op jit(solution)/shard_map/ppermute | solution.py:371
  30.7 4.3 %collective-permute-done.2.b = f32[25,80,128]{2,1,0:T(8,128)S(1)} collective-permute-done((f32[25,80,128]{2,1,0:T(8,128)S(1)}, f32[25,80,128]{2,1,0:T(8,128)S(1)}, u32[]{:S(2)}, u32[]{:S(2)}) %collective-permute-start.2) | collective-permute-done | bytes 1024032 | tf_op jit(solution)/shard_map/ppermute | solution.py:371
  35.0 2.6 %collective-permute-start.5 = (f32[25,80,128]{2,1,0:T(8,128)S(1)}, f32[25,80,128]{2,1,0:T(8,128)S(1)}, u32[]{:S(2)}, u32[]{:S(2)}) collective-permute-start(f32[25,80,128]{2,1,0:T(8,128)S(1)} %collective-permute-done.b.refs_2_.refs_3_), channel_id=1, source_target_pairs={{2,0},{0,2},{6,4},{4,6},{10,8},{8,10},{14,12},{12,14},{18,16},{16,... | collective-permute-start | bytes 3072008 | tf_op jit(solution)/shard_map/ppermute | solution.py:368
  37.6 0.1 choose.4
  37.7 0.1 collective-permute-start.3
  37.8 2.3 %collective-permute-start.6 = (f32[25,80,128]{2,1,0:T(8,128)S(1)}, f32[25,80,128]{2,1,0:T(8,128)S(1)}, u32[]{:S(2)}, u32[]{:S(2)}) collective-permute-start(f32[25,80,128]{2,1,0:T(8,128)S(1)} %collective-permute-done.1.b), channel_id=1, source_target_pairs={{130,2},{252,124},{2,130},{124,252},{131,3},{253,125},{3,131},{125... | collective-permute-start | bytes 3072008 | tf_op jit(solution)/shard_map/ppermute | solution.py:374
  40.1 0.0 collective-permute-done.4.refs_1_.refs_0_
  40.1 0.0 collective-permute-done.5.refs_3_.refs_2_
  40.2 0.0 copy-done
  40.2 0.0 copy-done.2
  40.2 0.0 copy-done.3
  40.2 0.0 copy-done.4
  40.2 5.0 %unit.6 = (f32[25,80,128]{2,1,0:T(8,128)S(1)}, s32[1,1]{1,0:T(1,128)}) custom-call(s32[1,1]{1,0:T(1,128)} %constant.4.clone.1.order, f32[25,80,128]{2,1,0:T(8,128)S(1)} %pack.1.a.refs_0_.refs_1_, f32[25,80,128]{2,1,0:T(8,128)S(1)} %collective-permute-done.4.refs_1_.refs_0_, f32[25,80,128]{2,1,0:T(8,128)S(1)} %collective-permute-done.b.refs_2_.refs_3_, ...), custom_call_target="tpu_custom_call" | custom-call | flops 1 | bytes 1 | tf_op jit(solution)/shard_map/unit/pallas_call | solution.py:260
  45.2 11.4 %collective-permute-done.3.refs_3_.refs_2_.refs_4_ = f32[25,80,128]{2,1,0:T(8,128)S(1)} collective-permute-done((f32[25,80,128]{2,1,0:T(8,128)S(1)}, f32[25,80,128]{2,1,0:T(8,128)S(1)}, u32[]{:S(2)}, u32[]{:S(2)}) %collective-permute-start.3) | collective-permute-done | bytes 1024032 | tf_op jit(solution)/shard_map/ppermute | solution.py:382
  56.6 0.0 collective-permute-done.6.a
  56.6 0.8 choose.5.refs_1_.refs_0_.refs_2_
  57.4 0.1 collective-permute-start.7
  57.5 0.5 collective-permute-start.8
  58.0 0.8 choose.6
  58.8 6.1 %collective-permute-start.9 = (f32[25,80,128]{2,1,0:T(8,128)S(1)}, f32[25,80,128]{2,1,0:T(8,128)S(1)}, u32[]{:S(2)}, u32[]{:S(2)}) collective-permute-start(f32[25,80,128]{2,1,0:T(8,128)S(1)} %choose.6), channel_id=1, source_target_pairs={{253,0},{252,1},{6,2},{7,3},{0,4},{1,5},{10,6},{11,7},{4,8},{5,9},... | collective-permute-start | bytes 3072008 | tf_op jit(solution)/shard_map/ppermute | solution.py:382
  64.9 0.9 collective-permute-start.10
  65.8 5.7 %unit.7 = (f32[25,80,128]{2,1,0:T(8,128)S(1)}, s32[1,1]{1,0:T(1,128)}) custom-call(s32[1,1]{1,0:T(1,128)} %get-tuple-element.25.order, f32[25,80,128]{2,1,0:T(8,128)S(1)} %pack.1.a.refs_0_.refs_1_, f32[25,80,128]{2,1,0:T(8,128)S(1)} %choose.5.refs_1_.refs_0_.refs_2_, f32[25,80,128]{2,1,0:T(8,128)S(1)} %collective-permute-done.b.refs_2_.refs_3_, ...), custom_call_target="tpu_custom_call" | custom-call | flops 1 | bytes 1 | tf_op jit(solution)/shard_map/unit/pallas_call | solution.py:260
  71.5 0.0 collective-permute-done.7.refs_1_
  71.5 0.0 collective-permute-done.8.refs_3_
  71.5 5.6 %unit.8 = (f32[25,80,128]{2,1,0:T(8,128)S(1)}, s32[1,1]{1,0:T(1,128)}) custom-call(s32[1,1]{1,0:T(1,128)} %get-tuple-element.29.order, f32[25,80,128]{2,1,0:T(8,128)S(1)} %choose.5.refs_1_.refs_0_.refs_2_, f32[25,80,128]{2,1,0:T(8,128)S(1)} %collective-permute-done.7.refs_1_, f32[25,80,128]{2,1,0:T(8,128)S(1)} %collective-permute-done.3.refs_3_.refs_2_.refs_4_, ...), custom_call_target="tpu_custom_call" | custom-call | flops 1 | bytes 1 | tf_op jit(solution)/shard_map/unit/pallas_call | solution.py:260
  77.1 2.0 %collective-permute-start.11 = (f32[25,80,128]{2,1,0:T(8,128)S(1)}, f32[25,80,128]{2,1,0:T(8,128)S(1)}, u32[]{:S(2)}, u32[]{:S(2)}) collective-permute-start(f32[25,80,128]{2,1,0:T(8,128)S(1)} %get-tuple-element.35), channel_id=1, source_target_pairs={{252,0},{6,2},{0,4},{10,6},{4,8},{14,10},{8,12},{18,14},{12,16},{2... | collective-permute-start | bytes 3072008 | tf_op jit(solution)/shard_map/ppermute | solution.py:368
  79.1 0.0 collective-permute-done.9.refs_0_.refs_3_.refs_4_
  79.1 5.6 %unit.9 = (f32[25,80,128]{2,1,0:T(8,128)S(1)}, s32[1,1]{1,0:T(1,128)}) custom-call(s32[1,1]{1,0:T(1,128)} %get-tuple-element.30.order, f32[25,80,128]{2,1,0:T(8,128)S(1)} %collective-permute-done.9.refs_0_.refs_3_.refs_4_, f32[25,80,128]{2,1,0:T(8,128)S(1)} %collective-permute-done.4.refs_1_.refs_0_, f32[25,80,128]{2,1,0:T(8,128)S(1)} %choose.5.refs_1_.refs_0_.refs_2_, ...), custom_call_target="tpu_custom_call" | custom-call | flops 1 | bytes 1 | tf_op jit(solution)/shard_map/unit/pallas_call | solution.py:260
  84.8 0.0 collective-permute-done.10.a
  84.8 0.8 choose.7.refs_1_.refs_2_
  85.5 5.6 %unit.10 = (f32[25,80,128]{2,1,0:T(8,128)S(1)}, s32[1,1]{1,0:T(1,128)}) custom-call(s32[1,1]{1,0:T(1,128)} %get-tuple-element.31.order, f32[25,80,128]{2,1,0:T(8,128)S(1)} %collective-permute-done.4.refs_1_.refs_0_, f32[25,80,128]{2,1,0:T(8,128)S(1)} %choose.7.refs_1_.refs_2_, f32[25,80,128]{2,1,0:T(8,128)S(1)} %collective-permute-done.5.refs_3_.refs_2_, ...), custom_call_target="tpu_custom_call" | custom-call | flops 1 | bytes 1 | tf_op jit(solution)/shard_map/unit/pallas_call | solution.py:260
  91.2 0.3 collective-permute-start.12
  91.5 0.0 collective-permute-done.11.refs_0_.returned
  91.5 5.7 %unit.11 = (f32[25,80,128]{2,1,0:T(8,128)S(1)}, s32[1,1]{1,0:T(1,128)}) custom-call(s32[1,1]{1,0:T(1,128)} %get-tuple-element.34.order, f32[25,80,128]{2,1,0:T(8,128)S(1)} %collective-permute-done.11.refs_0_.returned, f32[25,80,128]{2,1,0:T(8,128)S(1)} %pack.1.a.refs_0_.refs_1_, f32[25,80,128]{2,1,0:T(8,128)S(1)} %choose.7.refs_1_.refs_2_, ...), custom_call_target="tpu_custom_call" | custom-call | flops 1 | bytes 1 | tf_op jit(solution)/shard_map/unit/pallas_call | solution.py:260
  97.2 0.0 collective-permute-done.12.theirs
  97.2 2.2 %unpack_sum.1 = f32[40,80,80]{2,1,0:T(8,128)} custom-call(f32[25,80,128]{2,1,0:T(8,128)S(1)} %get-tuple-element.37.total, f32[25,80,128]{2,1,0:T(8,128)S(1)} %collective-permute-done.11.refs_0_.returned, f32[25,80,128]{2,1,0:T(8,128)S(1)} %collective-permute-done.12.theirs), custom_call_target="tpu_custom_call" | custom-call | tf_op jit(solution)/shard_map/unpack_sum/pallas_call | solution.py:348
Async XLA Ops:
  0.0 1.4 %copy-start.1 = (f32[1,40,80,80]{3,2,1,0:T(8,128)S(1)}, f32[1,40,80,80]{3,2,1,0:T(8,128)}, u32[]{:S(2)}) copy-start(f32[1,40,80,80]{3,2,1,0:T(8,128)} %param.5) | copy-start | bytes 3072004
  2.4 37.8 %copy-start = (f32[6,41,8,128]{3,2,1,0:T(8,128)S(1)}, f32[6,41,8,128]{3,2,1,0:T(8,128)}, u32[]{:S(2)}) copy-start(f32[6,41,8,128]{3,2,1,0:T(8,128)} %constant.13.clone.refs_7_.refs_8_) | copy-start | bytes 3022852
  2.4 37.8 %copy-start.2 = (bf16[80,240]{1,0:T(8,128)(2,1)S(1)}, bf16[80,240]{1,0:T(8,128)(2,1)}, u32[]{:S(2)}) copy-start(bf16[80,240]{1,0:T(8,128)(2,1)} %constant.10.clone.refs_4_.refs_5_) | copy-start | bytes 115204
  2.4 37.8 %copy-start.3 = (bf16[80,240]{1,0:T(8,128)(2,1)S(1)}, bf16[80,240]{1,0:T(8,128)(2,1)}, u32[]{:S(2)}) copy-start(bf16[80,240]{1,0:T(8,128)(2,1)} %constant.11.clone.refs_5_.refs_6_) | copy-start | bytes 115204
  2.4 37.8 %copy-start.4 = (bf16[80,240]{1,0:T(8,128)(2,1)S(1)}, bf16[80,240]{1,0:T(8,128)(2,1)}, u32[]{:S(2)}) copy-start(bf16[80,240]{1,0:T(8,128)(2,1)} %constant.12.clone.refs_6_.refs_7_) | copy-start | bytes 115204
  2.4 25.1 %collective-permute-start = (f32[25,80,128]{2,1,0:T(8,128)S(1)}, f32[25,80,128]{2,1,0:T(8,128)S(1)}, u32[]{:S(2)}, u32[]{:S(2)}) collective-permute-start(f32[25,80,128]{2,1,0:T(8,128)S(1)} %pack.1.a.refs_0_.refs_1_), channel_id=1, source_target_pairs={{0,1},{1,0},{2,3},{3,2},{4,5},{5,4},{6,7},{7,6},{8,9},{9,8},{10,11... | collective-permute-start | bytes 3072008 | tf_op jit(solution)/shard_map/ppermute | solution.py:389
  6.2 24.4 %collective-permute-start.1 = (f32[25,80,128]{2,1,0:T(8,128)S(1)}, f32[25,80,128]{2,1,0:T(8,128)S(1)}, u32[]{:S(2)}, u32[]{:S(2)}) collective-permute-start(f32[25,80,128]{2,1,0:T(8,128)S(1)} %pack.1.a.refs_0_.refs_1_), channel_id=1, source_target_pairs={{4,0},{126,2},{8,4},{2,6},{12,8},{6,10},{16,12},{10,14},{20,16},{1... | collective-permute-start | bytes 3072008 | tf_op jit(solution)/shard_map/ppermute | solution.py:371
  7.5 27.5 %collective-permute-start.2 = (f32[25,80,128]{2,1,0:T(8,128)S(1)}, f32[25,80,128]{2,1,0:T(8,128)S(1)}, u32[]{:S(2)}, u32[]{:S(2)}) collective-permute-start(f32[25,80,128]{2,1,0:T(8,128)S(1)} %pack.1.a.refs_0_.refs_1_), channel_id=1, source_target_pairs={{124,0},{6,2},{0,4},{10,6},{4,8},{14,10},{8,12},{18,14},{12,16},{2... | collective-permute-start | bytes 3072008 | tf_op jit(solution)/shard_map/ppermute | solution.py:371
  14.0 26.1 %collective-permute-start.4 = (f32[25,80,128]{2,1,0:T(8,128)S(1)}, f32[25,80,128]{2,1,0:T(8,128)S(1)}, u32[]{:S(2)}, u32[]{:S(2)}) collective-permute-start(f32[25,80,128]{2,1,0:T(8,128)S(1)} %pack.1.a.refs_0_.refs_1_), channel_id=1, source_target_pairs={{2,0},{0,2},{6,4},{4,6},{10,8},{8,10},{14,12},{12,14},{18,16},{16,... | collective-permute-start | bytes 3072008 | tf_op jit(solution)/shard_map/ppermute | solution.py:368
  35.0 5.1 %collective-permute-start.5 = (f32[25,80,128]{2,1,0:T(8,128)S(1)}, f32[25,80,128]{2,1,0:T(8,128)S(1)}, u32[]{:S(2)}, u32[]{:S(2)}) collective-permute-start(f32[25,80,128]{2,1,0:T(8,128)S(1)} %collective-permute-done.b.refs_2_.refs_3_), channel_id=1, source_target_pairs={{2,0},{0,2},{6,4},{4,6},{10,8},{8,10},{14,12},{12,14},{18,16},{16,... | collective-permute-start | bytes 3072008 | tf_op jit(solution)/shard_map/ppermute | solution.py:368
  37.7 18.9 %collective-permute-start.3 = (f32[25,80,128]{2,1,0:T(8,128)S(1)}, f32[25,80,128]{2,1,0:T(8,128)S(1)}, u32[]{:S(2)}, u32[]{:S(2)}) collective-permute-start(f32[25,80,128]{2,1,0:T(8,128)S(1)} %choose.4), channel_id=1, source_target_pairs={{4,0},{5,1},{255,2},{254,3},{8,4},{9,5},{2,6},{3,7},{12,8},{13,9},... | collective-permute-start | bytes 3072008 | tf_op jit(solution)/shard_map/ppermute | solution.py:382
  37.8 18.8 %collective-permute-start.6 = (f32[25,80,128]{2,1,0:T(8,128)S(1)}, f32[25,80,128]{2,1,0:T(8,128)S(1)}, u32[]{:S(2)}, u32[]{:S(2)}) collective-permute-start(f32[25,80,128]{2,1,0:T(8,128)S(1)} %collective-permute-done.1.b), channel_id=1, source_target_pairs={{130,2},{252,124},{2,130},{124,252},{131,3},{253,125},{3,131},{125... | collective-permute-start | bytes 3072008 | tf_op jit(solution)/shard_map/ppermute | solution.py:374
  57.4 14.1 %collective-permute-start.7 = (f32[25,80,128]{2,1,0:T(8,128)S(1)}, f32[25,80,128]{2,1,0:T(8,128)S(1)}, u32[]{:S(2)}, u32[]{:S(2)}) collective-permute-start(f32[25,80,128]{2,1,0:T(8,128)S(1)} %choose.5.refs_1_.refs_0_.refs_2_), channel_id=1, source_target_pairs={{2,0},{0,2},{6,4},{4,6},{10,8},{8,10},{14,12},{12,14},{18,16},{16,... | collective-permute-start | bytes 3072008 | tf_op jit(solution)/shard_map/ppermute | solution.py:368
  57.5 14.0 %collective-permute-start.8 = (f32[25,80,128]{2,1,0:T(8,128)S(1)}, f32[25,80,128]{2,1,0:T(8,128)S(1)}, u32[]{:S(2)}, u32[]{:S(2)}) collective-permute-start(f32[25,80,128]{2,1,0:T(8,128)S(1)} %collective-permute-done.3.refs_3_.refs_2_.refs_4_), channel_id=1, source_target_pairs={{2,0},{0,2},{6,4},{4,6},{10,8},{8,10},{14,12},{12,14},{18,16},{16,... | collective-permute-start | bytes 3072008 | tf_op jit(solution)/shard_map/ppermute | solution.py:368
  58.8 20.3 %collective-permute-start.9 = (f32[25,80,128]{2,1,0:T(8,128)S(1)}, f32[25,80,128]{2,1,0:T(8,128)S(1)}, u32[]{:S(2)}, u32[]{:S(2)}) collective-permute-start(f32[25,80,128]{2,1,0:T(8,128)S(1)} %choose.6), channel_id=1, source_target_pairs={{253,0},{252,1},{6,2},{7,3},{0,4},{1,5},{10,6},{11,7},{4,8},{5,9},... | collective-permute-start | bytes 3072008 | tf_op jit(solution)/shard_map/ppermute | solution.py:382
  64.9 19.8 %collective-permute-start.10 = (f32[25,80,128]{2,1,0:T(8,128)S(1)}, f32[25,80,128]{2,1,0:T(8,128)S(1)}, u32[]{:S(2)}, u32[]{:S(2)}) collective-permute-start(f32[25,80,128]{2,1,0:T(8,128)S(1)} %collective-permute-done.2.b), channel_id=1, source_target_pairs={{128,0},{254,126},{0,128},{126,254},{129,1},{255,127},{1,129},{127... | collective-permute-start | bytes 3072008 | tf_op jit(solution)/shard_map/ppermute | solution.py:374
  77.1 14.4 %collective-permute-start.11 = (f32[25,80,128]{2,1,0:T(8,128)S(1)}, f32[25,80,128]{2,1,0:T(8,128)S(1)}, u32[]{:S(2)}, u32[]{:S(2)}) collective-permute-start(f32[25,80,128]{2,1,0:T(8,128)S(1)} %get-tuple-element.35), channel_id=1, source_target_pairs={{252,0},{6,2},{0,4},{10,6},{4,8},{14,10},{8,12},{18,14},{12,16},{2... | collective-permute-start | bytes 3072008 | tf_op jit(solution)/shard_map/ppermute | solution.py:368
  91.2 6.0 %collective-permute-start.12 = (f32[25,80,128]{2,1,0:T(8,128)S(1)}, f32[25,80,128]{2,1,0:T(8,128)S(1)}, u32[]{:S(2)}, u32[]{:S(2)}) collective-permute-start(f32[25,80,128]{2,1,0:T(8,128)S(1)} %get-tuple-element.38), channel_id=1, source_target_pairs={{2,0},{0,2},{6,4},{4,6},{10,8},{8,10},{14,12},{12,14},{18,16},{16,... | collective-permute-start | bytes 3072008 | tf_op jit(solution)/shard_map/ppermute | solution.py:368

commit v4 on v3

--- a/solution.py
+++ b/solution.py
@@ -243,11 +243,14 @@
         backward_y(group)
 
 
-def unit(a, b, constants, after, total=None, waits=()):
+def unit(a, b, constants, after, total=None, waits=(), near_at=None):
     operands = [a[0], b[0], a[1], b[1], *constants]
 
     def body(order, *refs):
-        refs = refs[len(waits) :]
+        refs = list(refs[len(waits) :])
+        if near_at is not None:
+            sent = refs.pop(len(operands) + (total is not None) + 2)
+            copy_chosen(near_at, refs[0], refs[2], sent)
         ins, rest = refs[: len(operands)], refs[len(operands) :]
         if total is None:
             unit_body(*ins, None, *rest)
@@ -260,8 +263,9 @@
     return pl.pallas_call(
         body,
         in_specs=[scalar] + [pl.BlockSpec(memory_space=pl.ANY)] * len(waits) + [here] * len(operands_all),
-        out_specs=(here, scalar),
-        out_shape=(jax.ShapeDtypeStruct(PACKED, F32), jax.ShapeDtypeStruct((1, 1), jnp.int32)),
+        out_specs=(here, scalar) + (here,) * (near_at is not None),
+        out_shape=(jax.ShapeDtypeStruct(PACKED, F32), jax.ShapeDtypeStruct((1, 1), jnp.int32))
+        + (jax.ShapeDtypeStruct(PACKED, F32),) * (near_at is not None),
         scratch_shapes=[
             pltpu.VMEM((N, N, LANES), F32),
             pltpu.VMEM((HALF, N, LANES), F32),
@@ -274,7 +278,7 @@
     )(after, *waits, *operands_all)
 
 
-def choose_body(places, order, a, b, out):
+def copy_chosen(places, a, b, out):
     place = lax.axis_index("band")
     takes = functools.reduce(jnp.logical_or, [place == p for p in places])
 
@@ -289,6 +293,10 @@
         @pl.loop(0, GROUPS * PLANES)
         def _(plane):
             out[plane] = b[plane]
+
+
+def choose_body(places, order, a, b, out):
+    copy_chosen(places, a, b, out)
 
 
 def choose(places, a, b, after):
@@ -330,24 +338,30 @@
     )(data)
 
 
-def unpack_body(total, returned, theirs, out):
+def unpack_body(total, returned, theirs, out, held, sems):
     lane = lax.broadcasted_iota(jnp.int32, (N, LANES), 1)
-
-    @pl.loop(0, GROUPS)
-    def _(group):
+    copies = []
+    for group in range(GROUPS):
         start = group * PLANES
         planes = [total[start + i] + returned[start + i] + theirs[start + i] for i in range(PLANES)]
         for j in range(GROUP):
             low = planes[j // 2] if j % 2 == 0 else pltpu.roll(planes[j // 2], LOW, 1)
             place = HIGH * j
             high = pltpu.roll(planes[4], (LOW - place) % LANES, 1) if place != LOW else planes[4]
-            out[group * GROUP + j] = jnp.where(lane < LOW, low, high)[:, :N]
+            held[group, j] = jnp.where(lane < LOW, low, high)[:, :N]
+        copies.append(pltpu.make_async_copy(held.at[group], out.at[pl.ds(group * GROUP, GROUP)], sems.at[group]))
+        copies[-1].start()
+    for copy in copies:
+        copy.wait()
 
 
 def unpack_sum(total, returned, theirs):
     return pl.pallas_call(
         unpack_body,
+        in_specs=[pl.BlockSpec(memory_space=pltpu.VMEM)] * 3,
+        out_specs=pl.BlockSpec(memory_space=pltpu.HBM),
         out_shape=jax.ShapeDtypeStruct((HALF, N, N), F32),
+        scratch_shapes=[pltpu.VMEM((GROUPS, GROUP, N, N), F32), pltpu.SemaphoreType.DMA((GROUPS,))],
         compiler_params=pltpu.CompilerParams(vmem_limit_bytes=16 * 2**20),
         name="unpack_sum",
     )(total, returned, theirs)
@@ -370,16 +384,15 @@
     def from_half(data, distance):
         return lax.ppermute(data, "band", [(b // half * half + source % half, b) for b, source in enumerate(sources(distance))])
 
-    def swapped_halves(data, distance):
-        return lax.ppermute(data, "band", [((b + half) % bands, b) for b in takers(distance)])
-
-    def far_slabs(near, far, distance, after):
+    def far_route(distance):
         route = []
         for b, source in enumerate(sources(distance)):
             for slab in range(2):
                 route.append((2 * source + (1 - slab if b in takers(distance) else slab), 2 * b + slab))
-        across = [sources(distance)[b] for b in takers(distance)]
-        return lax.ppermute(choose(across, near, far, after), ("band", "grid"), route)
+        return route
+
+    def givers(distance):
+        return [sources(distance)[b] for b in takers(distance)]
 
     def other_core(data):
         return from_place(data, -1)
@@ -389,23 +402,26 @@
     far = lax.ppermute(near, "grid", [(0, 1), (1, 0)])
     m2_half = from_half(near, -2)
     p2_half = from_half(near, 2)
-    far, m2_half, p2_half = lax.optimization_barrier((far, m2_half, p2_half))
+    p2_half, m2_half, far = lax.optimization_barrier((p2_half, m2_half, far))
     own = (near, far)
     first = jnp.zeros((1, 1), jnp.int32)
-    m2_far = far_slabs(near, far, -2, first)
-    m2_swapped = swapped_halves(m2_half, -2)
+    m2_far = lax.ppermute(choose(givers(-2), near, far, first), ("band", "grid"), far_route(-2))
     m1 = (other_core(near), other_core(far))
-    total, after = unit(own, m1, constants, first)
-    p2_far = far_slabs(near, far, 2, after)
-    m2_far, p2_half, after = lax.optimization_barrier((m2_far, p2_half, after))
-    p2_swapped = swapped_halves(p2_half, 2)
-    m2 = (choose(takers(-2), m2_swapped, m2_half, after), m2_far)
-    p1 = (other_core(m2[0]), other_core(m2_far))
+    swapped = lax.ppermute(
+        choose(takers(2), p2_half, m2_half, first), "band", [((b + half) % bands, b) for b in takers(-2) + takers(2)]
+    )
+    total, after, p2_sent = unit(own, m1, constants, first, near_at=givers(2))
+    p2_far = lax.ppermute(p2_sent, ("band", "grid"), far_route(2))
+    m2_near = choose(takers(-2), swapped, m2_half, after)
+    p1_near = other_core(m2_near)
+    m2_far, p1_near, after = lax.optimization_barrier((m2_far, p1_near, after))
+    m2 = (m2_near, m2_far)
+    p1 = (p1_near, other_core(m2_far))
     total, after = unit(own, m2, constants, after, total)
     lent, after = unit(m2, p1, constants, after)
     returned = from_place(lent, 2)
     partner, after = unit(m1, m2, constants, after, waits=(p2_far,))
-    p2 = (choose(takers(2), p2_swapped, p2_half, after), p2_far)
+    p2 = (choose(takers(2), swapped, p2_half, after), p2_far)
     partner, after = unit(m1, p2, constants, after, partner)
     theirs = other_core(partner)
     total, after = unit(own, p2, constants, after, total, waits=(returned,))

time: 99.6 us -> 108 us (1.084)
  waiting for transfers between devices: 31.2 us -> 40.5 us
  Pallas kernels: 38.8 us -> 37.6 us
    ppermute x4 -> x3, waiting for transfers between devices: 11.4 us -> 18.5 us  [the longest x1 18.4 us: shards(): lax.ppermute(choose(takers(2), p2_half, m2_half, first), 'band', [((b + h...]
    ppermute x6, waiting for transfers between devices: 0.02 us -> 2.26 us  [from_place(): lax.ppermute(data, 'band', [(source, b) for b, source in enumerate(source...]
    ppermute x6, starting transfers between devices: 6.71 us -> 8.81 us  [from_place(): lax.ppermute(data, 'band', [(source, b) for b, source in enumerate(source...]
    ppermute x4 -> x3, starting transfers between devices: 9.39 us -> 7.81 us  [the longest x1 5.29 us: shards(): p2_far = lax.ppermute(p2_sent, ('band', 'grid'), far_route(2))]
  transfers between devices with their start and end apart: 13 -> 12, of which waited for: 4 -> 6; matrix products, arithmetic and copies ran while one was open for 0% -> 0% of each run, Pallas kernels for 35% -> 33%
where the time goes in v4:
time: 108 us
  waiting for transfers between devices  40.5 us (38%)
  Pallas kernels  37.6 us (35%)
  starting transfers between devices  28.2 us (26%)
  local copies, waits for them, and re-layouts  1.46 us (1%)
    pallas_call x6, Pallas kernels, unit(): pl.pallas_call(body, in_specs=[scalar] + [pl.BlockSpec(memory_space=pl.AN...  33.4 us
    ppermute x1, waiting for transfers between devices, shards(): lax.ppermute(choose(takers(2), p2_half, m2_half, first), 'band', [((b + h...  18.4 us
    ppermute x1, waiting for transfers between devices, shards(): far = lax.ppermute(near, 'grid', [(0, 1), (1, 0)])  12.3 us
    ppermute x6, starting transfers between devices, from_place(): lax.ppermute(data, 'band', [(source, b) for b, source in enumerate(source...  8.81 us
    ppermute x2, starting transfers between devices, from_half(): lax.ppermute(data, 'band', [(b // half * half + source % half, b) for b,...  7.77 us
    ppermute x2, waiting for transfers between devices, from_half(): lax.ppermute(data, 'band', [(b // half * half + source % half, b) for b,...  7.46 us
    ppermute x1, starting transfers between devices, shards(): p2_far = lax.ppermute(p2_sent, ('band', 'grid'), far_route(2))  5.29 us
    ppermute x1, starting transfers between devices, shards(): far = lax.ppermute(near, 'grid', [(0, 1), (1, 0)])  3.83 us
  transfers between devices with their start and end apart: 12, of which 6 were waited for; matrix products, arithmetic and copies ran while one was open for 0% of the time, Pallas kernels for 33%

profile of v4, /device:TPU:1, one launch (start us, length us, event | category | flops | bytes accessed | tf_op | source)
XLA Modules:
  0.0 108.1 jit_solution(7478387526779139910)
XLA Ops:
  0.0 0.0 copy-start.1
  0.0 1.4 %copy-done.1 = f32[1,40,80,80]{3,2,1,0:T(8,128)S(1)} copy-done((f32[1,40,80,80]{3,2,1,0:T(8,128)S(1)}, f32[1,40,80,80]{3,2,1,0:T(8,128)}, u32[]{:S(2)}) %copy-start.1) | copy-done | bytes 1024024
  1.4 0.9 pack.1.a.refs_0_.refs_1_
  2.4 3.8 %collective-permute-start.2 = (f32[25,80,128]{2,1,0:T(8,128)S(1)}, f32[25,80,128]{2,1,0:T(8,128)S(1)}, u32[]{:S(2)}, u32[]{:S(2)}) collective-permute-start(f32[25,80,128]{2,1,0:T(8,128)S(1)} %pack.1.a.refs_0_.refs_1_), channel_id=1, source_target_pairs={{0,1},{1,0},{2,3},{3,2},{4,5},{5,4},{6,7},{7,6},{8,9},{9,8},{10,11... | collective-permute-start | bytes 3072008 | tf_op jit(solution)/shard_map/ppermute | solution.py:402
  6.2 1.2 %collective-permute-start.1 = (f32[25,80,128]{2,1,0:T(8,128)S(1)}, f32[25,80,128]{2,1,0:T(8,128)S(1)}, u32[]{:S(2)}, u32[]{:S(2)}) collective-permute-start(f32[25,80,128]{2,1,0:T(8,128)S(1)} %pack.1.a.refs_0_.refs_1_), channel_id=1, source_target_pairs={{4,0},{126,2},{8,4},{2,6},{12,8},{6,10},{16,12},{10,14},{20,16},{1... | collective-permute-start | bytes 3072008 | tf_op jit(solution)/shard_map/ppermute | solution.py:385
  7.4 6.6 %collective-permute-start = (f32[25,80,128]{2,1,0:T(8,128)S(1)}, f32[25,80,128]{2,1,0:T(8,128)S(1)}, u32[]{:S(2)}, u32[]{:S(2)}) collective-permute-start(f32[25,80,128]{2,1,0:T(8,128)S(1)} %pack.1.a.refs_0_.refs_1_), channel_id=1, source_target_pairs={{124,0},{6,2},{0,4},{10,6},{4,8},{14,10},{8,12},{18,14},{12,16},{2... | collective-permute-start | bytes 3072008 | tf_op jit(solution)/shard_map/ppermute | solution.py:385
  14.0 1.2 %collective-permute-start.4 = (f32[25,80,128]{2,1,0:T(8,128)S(1)}, f32[25,80,128]{2,1,0:T(8,128)S(1)}, u32[]{:S(2)}, u32[]{:S(2)}) collective-permute-start(f32[25,80,128]{2,1,0:T(8,128)S(1)} %pack.1.a.refs_0_.refs_1_), channel_id=1, source_target_pairs={{2,0},{0,2},{6,4},{4,6},{10,8},{8,10},{14,12},{12,14},{18,16},{16,... | collective-permute-start | bytes 3072008 | tf_op jit(solution)/shard_map/ppermute | solution.py:382
  15.2 12.3 %collective-permute-done.2.b.refs_2_.refs_3_ = f32[25,80,128]{2,1,0:T(8,128)S(1)} collective-permute-done((f32[25,80,128]{2,1,0:T(8,128)S(1)}, f32[25,80,128]{2,1,0:T(8,128)S(1)}, u32[]{:S(2)}, u32[]{:S(2)}) %collective-permute-start.2) | collective-permute-done | bytes 1024032 | tf_op jit(solution)/shard_map/ppermute | solution.py:402
  27.5 3.1 %collective-permute-done.1.b = f32[25,80,128]{2,1,0:T(8,128)S(1)} collective-permute-done((f32[25,80,128]{2,1,0:T(8,128)S(1)}, f32[25,80,128]{2,1,0:T(8,128)S(1)}, u32[]{:S(2)}, u32[]{:S(2)}) %collective-permute-start.1) | collective-permute-done | bytes 1024032 | tf_op jit(solution)/shard_map/ppermute | solution.py:385
  30.6 4.3 %collective-permute-done.a.b = f32[25,80,128]{2,1,0:T(8,128)S(1)} collective-permute-done((f32[25,80,128]{2,1,0:T(8,128)S(1)}, f32[25,80,128]{2,1,0:T(8,128)S(1)}, u32[]{:S(2)}, u32[]{:S(2)}) %collective-permute-start) | collective-permute-done | bytes 1024032 | tf_op jit(solution)/shard_map/ppermute | solution.py:385
  34.9 2.6 %collective-permute-start.5 = (f32[25,80,128]{2,1,0:T(8,128)S(1)}, f32[25,80,128]{2,1,0:T(8,128)S(1)}, u32[]{:S(2)}, u32[]{:S(2)}) collective-permute-start(f32[25,80,128]{2,1,0:T(8,128)S(1)} %collective-permute-done.2.b.refs_2_.refs_3_), channel_id=1, source_target_pairs={{2,0},{0,2},{6,4},{4,6},{10,8},{8,10},{14,12},{12,14},{18,16},{16,... | collective-permute-start | bytes 3072008 | tf_op jit(solution)/shard_map/ppermute | solution.py:382
  37.5 0.1 choose.5
  37.7 0.0 copy-start
  37.7 0.0 copy-start.2
  37.7 0.0 copy-start.3
  37.7 0.0 copy-start.4
  37.7 2.4 %collective-permute-start.6 = (f32[25,80,128]{2,1,0:T(8,128)S(1)}, f32[25,80,128]{2,1,0:T(8,128)S(1)}, u32[]{:S(2)}, u32[]{:S(2)}) collective-permute-start(f32[25,80,128]{2,1,0:T(8,128)S(1)} %choose.5), channel_id=1, source_target_pairs={{130,2},{252,124},{2,130},{124,252},{128,0},{254,126},{0,128},{126... | collective-permute-start | bytes 3072008 | tf_op jit(solution)/shard_map/ppermute | solution.py:410
  40.2 0.2 choose.4
  40.3 0.1 collective-permute-start.3
  40.4 0.0 collective-permute-done.4.refs_1_.refs_0_
  40.4 0.0 collective-permute-done.5.refs_3_.refs_2_
  40.4 0.0 copy-done
  40.5 0.0 copy-done.2
  40.5 0.0 copy-done.3
  40.5 0.0 copy-done.4
  40.5 5.1 %unit.6 = (f32[25,80,128]{2,1,0:T(8,128)S(1)}, s32[1,1]{1,0:T(1,128)}, f32[25,80,128]{2,1,0:T(8,128)S(1)}) custom-call(s32[1,1]{1,0:T(1,128)} %constant.4.clone.1.order, f32[25,80,128]{2,1,0:T(8,128)S(1)} %pack.1.a.refs_0_.refs_1_, f32[25,80,128]{2,1,0:T(8,128)S(1)} %collective-permute-done.4.refs_1_.refs_0_, ...), custom_call_target="tpu_custom_call" | custom-call | flops 1 | bytes 1 | tf_op jit(solution)/shard_map/unit/pallas_call | solution.py:263
  45.6 18.4 %collective-permute-done.6.a = f32[25,80,128]{2,1,0:T(8,128)S(1)} collective-permute-done((f32[25,80,128]{2,1,0:T(8,128)S(1)}, f32[25,80,128]{2,1,0:T(8,128)S(1)}, u32[]{:S(2)}, u32[]{:S(2)}) %collective-permute-start.6) | collective-permute-done | bytes 1024032 | tf_op jit(solution)/shard_map/ppermute | solution.py:410
  64.0 0.8 choose.6.refs_1_.refs_0_.refs_2_
  64.8 0.9 collective-permute-start.7
  65.7 0.0 collective-permute-done.3.refs_3_.refs_2_.refs_4_
  65.7 2.2 %collective-permute-done.7.refs_1_ = f32[25,80,128]{2,1,0:T(8,128)S(1)} collective-permute-done((f32[25,80,128]{2,1,0:T(8,128)S(1)}, f32[25,80,128]{2,1,0:T(8,128)S(1)}, u32[]{:S(2)}, u32[]{:S(2)}) %collective-permute-start.7) | collective-permute-done | bytes 1024032 | tf_op jit(solution)/shard_map/ppermute | solution.py:382
  67.9 0.4 collective-permute-start.8
  68.3 5.3 %collective-permute-start.9 = (f32[25,80,128]{2,1,0:T(8,128)S(1)}, f32[25,80,128]{2,1,0:T(8,128)S(1)}, u32[]{:S(2)}, u32[]{:S(2)}) collective-permute-start(f32[25,80,128]{2,1,0:T(8,128)S(1)} %get-tuple-element.33), channel_id=1, source_target_pairs={{253,0},{252,1},{6,2},{7,3},{0,4},{1,5},{10,6},{11,7},{4,8},{5,9},... | collective-permute-start | bytes 3072008 | tf_op jit(solution)/shard_map/ppermute | solution.py:414
  73.6 5.6 %unit.7 = (f32[25,80,128]{2,1,0:T(8,128)S(1)}, s32[1,1]{1,0:T(1,128)}) custom-call(s32[1,1]{1,0:T(1,128)} %get-tuple-element.27.order, f32[25,80,128]{2,1,0:T(8,128)S(1)} %pack.1.a.refs_0_.refs_1_, f32[25,80,128]{2,1,0:T(8,128)S(1)} %choose.6.refs_1_.refs_0_.refs_2_, f32[25,80,128]{2,1,0:T(8,128)S(1)} %collective-permute-done.2.b.refs_2_.refs_3_, ...), custom_call_target="tpu_custom_call" | custom-call | flops 1 | bytes 1 | tf_op jit(solution)/shard_map/unit/pallas_call | solution.py:263
  79.3 0.0 collective-permute-done.8.refs_3_
  79.3 5.6 %unit.8 = (f32[25,80,128]{2,1,0:T(8,128)S(1)}, s32[1,1]{1,0:T(1,128)}) custom-call(s32[1,1]{1,0:T(1,128)} %get-tuple-element.30.order, f32[25,80,128]{2,1,0:T(8,128)S(1)} %choose.6.refs_1_.refs_0_.refs_2_, f32[25,80,128]{2,1,0:T(8,128)S(1)} %collective-permute-done.7.refs_1_, f32[25,80,128]{2,1,0:T(8,128)S(1)} %collective-permute-done.3.refs_3_.refs_2_.refs_4_, ...), custom_call_target="tpu_custom_call" | custom-call | flops 1 | bytes 1 | tf_op jit(solution)/shard_map/unit/pallas_call | solution.py:263
  84.9 0.1 collective-permute-start.10
  85.0 0.1 collective-permute-done.9.refs_0_.refs_3_.refs_4_
  85.1 5.6 %unit.9 = (f32[25,80,128]{2,1,0:T(8,128)S(1)}, s32[1,1]{1,0:T(1,128)}) custom-call(s32[1,1]{1,0:T(1,128)} %get-tuple-element.32.order, f32[25,80,128]{2,1,0:T(8,128)S(1)} %collective-permute-done.9.refs_0_.refs_3_.refs_4_, f32[25,80,128]{2,1,0:T(8,128)S(1)} %collective-permute-done.4.refs_1_.refs_0_, f32[25,80,128]{2,1,0:T(8,128)S(1)} %choose.6.refs_1_.refs_0_.refs_2_, ...), custom_call_target="tpu_custom_call" | custom-call | flops 1 | bytes 1 | tf_op jit(solution)/shard_map/unit/pallas_call | solution.py:263
  90.7 0.8 choose.7.refs_1_.refs_2_
  91.5 5.7 %unit.10 = (f32[25,80,128]{2,1,0:T(8,128)S(1)}, s32[1,1]{1,0:T(1,128)}) custom-call(s32[1,1]{1,0:T(1,128)} %get-tuple-element.34.order, f32[25,80,128]{2,1,0:T(8,128)S(1)} %collective-permute-done.4.refs_1_.refs_0_, f32[25,80,128]{2,1,0:T(8,128)S(1)} %choose.7.refs_1_.refs_2_, f32[25,80,128]{2,1,0:T(8,128)S(1)} %collective-permute-done.5.refs_3_.refs_2_, ...), custom_call_target="tpu_custom_call" | custom-call | flops 1 | bytes 1 | tf_op jit(solution)/shard_map/unit/pallas_call | solution.py:263
  97.2 3.6 %collective-permute-start.11 = (f32[25,80,128]{2,1,0:T(8,128)S(1)}, f32[25,80,128]{2,1,0:T(8,128)S(1)}, u32[]{:S(2)}, u32[]{:S(2)}) collective-permute-start(f32[25,80,128]{2,1,0:T(8,128)S(1)} %get-tuple-element.40), channel_id=1, source_target_pairs={{2,0},{0,2},{6,4},{4,6},{10,8},{8,10},{14,12},{12,14},{18,16},{16,... | collective-permute-start | bytes 3072008 | tf_op jit(solution)/shard_map/ppermute | solution.py:382
  100.8 0.0 collective-permute-done.10.refs_0_.returned
  100.8 5.7 %unit.11 = (f32[25,80,128]{2,1,0:T(8,128)S(1)}, s32[1,1]{1,0:T(1,128)}) custom-call(s32[1,1]{1,0:T(1,128)} %get-tuple-element.36.order, f32[25,80,128]{2,1,0:T(8,128)S(1)} %collective-permute-done.10.refs_0_.returned, f32[25,80,128]{2,1,0:T(8,128)S(1)} %pack.1.a.refs_0_.refs_1_, f32[25,80,128]{2,1,0:T(8,128)S(1)} %choose.7.refs_1_.refs_2_, ...), custom_call_target="tpu_custom_call" | custom-call | flops 1 | bytes 1 | tf_op jit(solution)/shard_map/unit/pallas_call | solution.py:263
  106.5 0.0 collective-permute-done.11.theirs
  106.5 1.5 %unpack_sum.1 = f32[40,80,80]{2,1,0:T(8,128)} custom-call(f32[25,80,128]{2,1,0:T(8,128)S(1)} %get-tuple-element.39.total, f32[25,80,128]{2,1,0:T(8,128)S(1)} %collective-permute-done.10.refs_0_.returned, f32[25,80,128]{2,1,0:T(8,128)S(1)} %collective-permute-done.11.theirs), custom_call_target="tpu_custom_call" | custom-call | tf_op jit(solution)/shard_map/unpack_sum/pallas_call | solution.py:359
Async XLA Ops:
  0.0 1.4 %copy-start.1 = (f32[1,40,80,80]{3,2,1,0:T(8,128)S(1)}, f32[1,40,80,80]{3,2,1,0:T(8,128)}, u32[]{:S(2)}) copy-start(f32[1,40,80,80]{3,2,1,0:T(8,128)} %param.5) | copy-start | bytes 3072004
  2.4 25.1 %collective-permute-start.2 = (f32[25,80,128]{2,1,0:T(8,128)S(1)}, f32[25,80,128]{2,1,0:T(8,128)S(1)}, u32[]{:S(2)}, u32[]{:S(2)}) collective-permute-start(f32[25,80,128]{2,1,0:T(8,128)S(1)} %pack.1.a.refs_0_.refs_1_), channel_id=1, source_target_pairs={{0,1},{1,0},{2,3},{3,2},{4,5},{5,4},{6,7},{7,6},{8,9},{9,8},{10,11... | collective-permute-start | bytes 3072008 | tf_op jit(solution)/shard_map/ppermute | solution.py:402
  6.2 24.4 %collective-permute-start.1 = (f32[25,80,128]{2,1,0:T(8,128)S(1)}, f32[25,80,128]{2,1,0:T(8,128)S(1)}, u32[]{:S(2)}, u32[]{:S(2)}) collective-permute-start(f32[25,80,128]{2,1,0:T(8,128)S(1)} %pack.1.a.refs_0_.refs_1_), channel_id=1, source_target_pairs={{4,0},{126,2},{8,4},{2,6},{12,8},{6,10},{16,12},{10,14},{20,16},{1... | collective-permute-start | bytes 3072008 | tf_op jit(solution)/shard_map/ppermute | solution.py:385
  7.4 27.5 %collective-permute-start = (f32[25,80,128]{2,1,0:T(8,128)S(1)}, f32[25,80,128]{2,1,0:T(8,128)S(1)}, u32[]{:S(2)}, u32[]{:S(2)}) collective-permute-start(f32[25,80,128]{2,1,0:T(8,128)S(1)} %pack.1.a.refs_0_.refs_1_), channel_id=1, source_target_pairs={{124,0},{6,2},{0,4},{10,6},{4,8},{14,10},{8,12},{18,14},{12,16},{2... | collective-permute-start | bytes 3072008 | tf_op jit(solution)/shard_map/ppermute | solution.py:385
  14.0 26.5 %collective-permute-start.4 = (f32[25,80,128]{2,1,0:T(8,128)S(1)}, f32[25,80,128]{2,1,0:T(8,128)S(1)}, u32[]{:S(2)}, u32[]{:S(2)}) collective-permute-start(f32[25,80,128]{2,1,0:T(8,128)S(1)} %pack.1.a.refs_0_.refs_1_), channel_id=1, source_target_pairs={{2,0},{0,2},{6,4},{4,6},{10,8},{8,10},{14,12},{12,14},{18,16},{16,... | collective-permute-start | bytes 3072008 | tf_op jit(solution)/shard_map/ppermute | solution.py:382
  34.9 5.5 %collective-permute-start.5 = (f32[25,80,128]{2,1,0:T(8,128)S(1)}, f32[25,80,128]{2,1,0:T(8,128)S(1)}, u32[]{:S(2)}, u32[]{:S(2)}) collective-permute-start(f32[25,80,128]{2,1,0:T(8,128)S(1)} %collective-permute-done.2.b.refs_2_.refs_3_), channel_id=1, source_target_pairs={{2,0},{0,2},{6,4},{4,6},{10,8},{8,10},{14,12},{12,14},{18,16},{16,... | collective-permute-start | bytes 3072008 | tf_op jit(solution)/shard_map/ppermute | solution.py:382
  37.7 2.8 %copy-start = (f32[6,41,8,128]{3,2,1,0:T(8,128)S(1)}, f32[6,41,8,128]{3,2,1,0:T(8,128)}, u32[]{:S(2)}) copy-start(f32[6,41,8,128]{3,2,1,0:T(8,128)} %constant.13.clone.refs_7_.refs_8_) | copy-start | bytes 3022852
  37.7 2.8 %copy-start.2 = (bf16[80,240]{1,0:T(8,128)(2,1)S(1)}, bf16[80,240]{1,0:T(8,128)(2,1)}, u32[]{:S(2)}) copy-start(bf16[80,240]{1,0:T(8,128)(2,1)} %constant.12.clone.refs_6_.refs_7_) | copy-start | bytes 115204
  37.7 2.8 %copy-start.3 = (bf16[80,240]{1,0:T(8,128)(2,1)S(1)}, bf16[80,240]{1,0:T(8,128)(2,1)}, u32[]{:S(2)}) copy-start(bf16[80,240]{1,0:T(8,128)(2,1)} %constant.11.clone.refs_5_.refs_6_) | copy-start | bytes 115204
  37.7 2.8 %copy-start.4 = (bf16[80,240]{1,0:T(8,128)(2,1)S(1)}, bf16[80,240]{1,0:T(8,128)(2,1)}, u32[]{:S(2)}) copy-start(bf16[80,240]{1,0:T(8,128)(2,1)} %constant.10.clone.refs_4_.refs_5_) | copy-start | bytes 115204
  37.7 26.3 %collective-permute-start.6 = (f32[25,80,128]{2,1,0:T(8,128)S(1)}, f32[25,80,128]{2,1,0:T(8,128)S(1)}, u32[]{:S(2)}, u32[]{:S(2)}) collective-permute-start(f32[25,80,128]{2,1,0:T(8,128)S(1)} %choose.5), channel_id=1, source_target_pairs={{130,2},{252,124},{2,130},{124,252},{128,0},{254,126},{0,128},{126... | collective-permute-start | bytes 3072008 | tf_op jit(solution)/shard_map/ppermute | solution.py:410
  40.3 25.4 %collective-permute-start.3 = (f32[25,80,128]{2,1,0:T(8,128)S(1)}, f32[25,80,128]{2,1,0:T(8,128)S(1)}, u32[]{:S(2)}, u32[]{:S(2)}) collective-permute-start(f32[25,80,128]{2,1,0:T(8,128)S(1)} %choose.4), channel_id=1, source_target_pairs={{4,0},{5,1},{255,2},{254,3},{8,4},{9,5},{2,6},{3,7},{12,8},{13,9},... | collective-permute-start | bytes 3072008 | tf_op jit(solution)/shard_map/ppermute | solution.py:408
  64.8 3.1 %collective-permute-start.7 = (f32[25,80,128]{2,1,0:T(8,128)S(1)}, f32[25,80,128]{2,1,0:T(8,128)S(1)}, u32[]{:S(2)}, u32[]{:S(2)}) collective-permute-start(f32[25,80,128]{2,1,0:T(8,128)S(1)} %choose.6.refs_1_.refs_0_.refs_2_), channel_id=1, source_target_pairs={{2,0},{0,2},{6,4},{4,6},{10,8},{8,10},{14,12},{12,14},{18,16},{16,... | collective-permute-start | bytes 3072008 | tf_op jit(solution)/shard_map/ppermute | solution.py:382
  67.9 11.3 %collective-permute-start.8 = (f32[25,80,128]{2,1,0:T(8,128)S(1)}, f32[25,80,128]{2,1,0:T(8,128)S(1)}, u32[]{:S(2)}, u32[]{:S(2)}) collective-permute-start(f32[25,80,128]{2,1,0:T(8,128)S(1)} %collective-permute-done.3.refs_3_.refs_2_.refs_4_), channel_id=1, source_target_pairs={{2,0},{0,2},{6,4},{4,6},{10,8},{8,10},{14,12},{12,14},{18,16},{16,... | collective-permute-start | bytes 3072008 | tf_op jit(solution)/shard_map/ppermute | solution.py:382
  68.3 16.8 %collective-permute-start.9 = (f32[25,80,128]{2,1,0:T(8,128)S(1)}, f32[25,80,128]{2,1,0:T(8,128)S(1)}, u32[]{:S(2)}, u32[]{:S(2)}) collective-permute-start(f32[25,80,128]{2,1,0:T(8,128)S(1)} %get-tuple-element.33), channel_id=1, source_target_pairs={{253,0},{252,1},{6,2},{7,3},{0,4},{1,5},{10,6},{11,7},{4,8},{5,9},... | collective-permute-start | bytes 3072008 | tf_op jit(solution)/shard_map/ppermute | solution.py:414
  84.9 15.9 %collective-permute-start.10 = (f32[25,80,128]{2,1,0:T(8,128)S(1)}, f32[25,80,128]{2,1,0:T(8,128)S(1)}, u32[]{:S(2)}, u32[]{:S(2)}) collective-permute-start(f32[25,80,128]{2,1,0:T(8,128)S(1)} %get-tuple-element.37), channel_id=1, source_target_pairs={{252,0},{6,2},{0,4},{10,6},{4,8},{14,10},{8,12},{18,14},{12,16},{2... | collective-permute-start | bytes 3072008 | tf_op jit(solution)/shard_map/ppermute | solution.py:382
  97.2 9.3 %collective-permute-start.11 = (f32[25,80,128]{2,1,0:T(8,128)S(1)}, f32[25,80,128]{2,1,0:T(8,128)S(1)}, u32[]{:S(2)}, u32[]{:S(2)}) collective-permute-start(f32[25,80,128]{2,1,0:T(8,128)S(1)} %get-tuple-element.40), channel_id=1, source_target_pairs={{2,0},{0,2},{6,4},{4,6},{10,8},{8,10},{14,12},{12,14},{18,16},{16,... | collective-permute-start | bytes 3072008 | tf_op jit(solution)/shard_map/ppermute | solution.py:382

commit v5 on v4

--- a/solution.py
+++ b/solution.py
@@ -159,8 +159,7 @@
     return data[:, LANES * index : LANES * (index + 1)]
 
 
-def unit_body(near_a, near_b, far_a, far_b, table_y, table_to, table_from, kernel, total, out, done, there, back, mid, turned):
-    done[0, 0] = 0
+def forwards(table_y, table_to, there, turned):
     fill = jnp.zeros((LANES - N, LANES), F32)
 
     def forward_y(a, b, first, group):
@@ -186,10 +185,20 @@
         for j in range(GROUP):
             there[group * GROUP + j] = piece(along_z, j)
 
+    return forward_y, forward_z
+
+
+def unit_body(ready, near_a, near_b, far_a, far_b, table_y, table_to, table_from, kernel, total, out, done, there, back, mid, turned):
+    done[0, 0] = 0
+    forward_y, forward_z = forwards(table_y, table_to, there, turned)
+
+    def plane_at(x):
+        return (there if ready is None or x >= HALF else ready).at[x]
+
     def middle(group, kernel_group):
         rows = pl.ds(pl.multiple_of(group * GROUP, GROUP), GROUP)
         for n2 in range(5):
-            for k1, (re, im) in enumerate(real_transform([there[point(n1, n2), rows, :] for n1 in range(16)])):
+            for k1, (re, im) in enumerate(real_transform([plane_at(point(n1, n2))[rows, :] for n1 in range(16)])):
                 mid[2 * k1, n2] = re
                 if im is not None:
                     mid[2 * k1 + 1, n2] = im
@@ -228,9 +237,10 @@
             out[start + i] = term if total is None else total[start + i] + term
 
     for group in range(GROUPS):
-        forward_y(near_a, near_b, 0, group)
+        if ready is None:
+            forward_y(near_a, near_b, 0, group)
         forward_y(far_a, far_b, GROUPS * PLANES, group)
-    for group in range(2 * GROUPS):
+    for group in range(0 if ready is None else GROUPS, 2 * GROUPS):
         forward_z(group)
 
     @pl.loop(0, 2 * GROUPS)
@@ -243,23 +253,24 @@
         backward_y(group)
 
 
-def unit(a, b, constants, after, total=None, waits=(), near_at=None):
+def unit(a, b, constants, after, total=None, waits=(), near_at=None, ready=None):
     operands = [a[0], b[0], a[1], b[1], *constants]
 
     def body(order, *refs):
         refs = list(refs[len(waits) :])
+        near_ready = None if ready is None else refs.pop(0)
         if near_at is not None:
             sent = refs.pop(len(operands) + (total is not None) + 2)
             copy_chosen(near_at, refs[0], refs[2], sent)
         ins, rest = refs[: len(operands)], refs[len(operands) :]
         if total is None:
-            unit_body(*ins, None, *rest)
+            unit_body(near_ready, *ins, None, *rest)
         else:
-            unit_body(*ins, *rest)
+            unit_body(near_ready, *ins, *rest)
 
     here = pl.BlockSpec(memory_space=pltpu.VMEM)
     scalar = pl.BlockSpec(memory_space=pltpu.SMEM)
-    operands_all = (*operands, *(() if total is None else (total,)))
+    operands_all = (*(() if ready is None else (ready,)), *operands, *(() if total is None else (total,)))
     return pl.pallas_call(
         body,
         in_specs=[scalar] + [pl.BlockSpec(memory_space=pl.ANY)] * len(waits) + [here] * len(operands_all),
@@ -278,6 +289,30 @@
     )(after, *waits, *operands_all)
 
 
+def ahead_body(a, a_2, b, table_y, table_to, out, out_2, turned, turned_2):
+    steps = [forwards(table_y, table_to, out, turned), forwards(table_y, table_to, out_2, turned_2)]
+    for group in range(GROUPS):
+        steps[0][0](a, b, 0, group)
+        steps[1][0](a_2, b, 0, group)
+    for group in range(GROUPS):
+        steps[0][1](group)
+        steps[1][1](group)
+
+
+def ahead(a, a_2, b, constants):
+    here = pl.BlockSpec(memory_space=pltpu.VMEM)
+    return pl.pallas_call(
+        ahead_body,
+        in_specs=[here] * 5,
+        out_specs=(here, here),
+        out_shape=(jax.ShapeDtypeStruct((HALF, N, LANES), F32),) * 2,
+        scratch_shapes=[pltpu.VMEM((GROUPS * PLANES, LANES, LANES), F32)] * 2,
+        compiler_params=pltpu.CompilerParams(vmem_limit_bytes=16 * 2**20),
+        cost_estimate=pl.CostEstimate(flops=1, bytes_accessed=1, transcendentals=0),
+        name="ahead",
+    )(a, a_2, b, constants[0], constants[1])
+
+
 def copy_chosen(places, a, b, out):
     place = lax.axis_index("band")
     takes = functools.reduce(jnp.logical_or, [place == p for p in places])
@@ -391,6 +426,9 @@
                 route.append((2 * source + (1 - slab if b in takers(distance) else slab), 2 * b + slab))
         return route
 
+    def swapped_halves(data, distance):
+        return lax.ppermute(data, "band", [((b + half) % bands, b) for b in takers(distance)])
+
     def givers(distance):
         return [sources(distance)[b] for b in takers(distance)]
 
@@ -402,26 +440,27 @@
     far = lax.ppermute(near, "grid", [(0, 1), (1, 0)])
     m2_half = from_half(near, -2)
     p2_half = from_half(near, 2)
-    p2_half, m2_half, far = lax.optimization_barrier((p2_half, m2_half, far))
+    far, m2_half, p2_half = lax.optimization_barrier((far, m2_half, p2_half))
     own = (near, far)
     first = jnp.zeros((1, 1), jnp.int32)
     m2_far = lax.ppermute(choose(givers(-2), near, far, first), ("band", "grid"), far_route(-2))
     m1 = (other_core(near), other_core(far))
-    swapped = lax.ppermute(
-        choose(takers(2), p2_half, m2_half, first), "band", [((b + half) % bands, b) for b in takers(-2) + takers(2)]
-    )
+    m2_swapped = swapped_halves(m2_half, -2)
     total, after, p2_sent = unit(own, m1, constants, first, near_at=givers(2))
     p2_far = lax.ppermute(p2_sent, ("band", "grid"), far_route(2))
-    m2_near = choose(takers(-2), swapped, m2_half, after)
+    p2_half, after = lax.optimization_barrier((p2_half, after))
+    p2_swapped = swapped_halves(p2_half, 2)
+    m2_near = choose(takers(-2), m2_swapped, m2_half, after)
     p1_near = other_core(m2_near)
-    m2_far, p1_near, after = lax.optimization_barrier((m2_far, p1_near, after))
+    own_m2, m1_m2 = ahead(near, m1[0], m2_near, constants)
+    m2_far, p1_near, own_m2, m1_m2, after = lax.optimization_barrier((m2_far, p1_near, own_m2, m1_m2, after))
     m2 = (m2_near, m2_far)
     p1 = (p1_near, other_core(m2_far))
-    total, after = unit(own, m2, constants, after, total)
+    total, after = unit(own, m2, constants, after, total, ready=own_m2)
     lent, after = unit(m2, p1, constants, after)
     returned = from_place(lent, 2)
-    partner, after = unit(m1, m2, constants, after, waits=(p2_far,))
-    p2 = (choose(takers(2), swapped, p2_half, after), p2_far)
+    partner, after = unit(m1, m2, constants, after, waits=(p2_far,), ready=m1_m2)
+    p2 = (choose(takers(2), p2_swapped, p2_half, after), p2_far)
     partner, after = unit(m1, p2, constants, after, partner)
     theirs = other_core(partner)
     total, after = unit(own, p2, constants, after, total, waits=(returned,))

time: 108 us -> 98.6 us (0.913)
  waiting for transfers between devices: 40.5 us -> 30.8 us
    ppermute x1 -> x2, waiting for transfers between devices: 18.4 us -> 7.51 us  [swapped_halves(): lax.ppermute(data, 'band', [((b + half) % bands, b) for b in takers(dista...]
    ppermute x1, waiting for transfers between devices: 0.01 us -> 3.48 us  [shards(): lax.ppermute(choose(givers(-2), near, far, first), ('band', 'grid'), far_...]
    ppermute x6, waiting for transfers between devices: 2.26 us -> 0.02 us  [from_place(): lax.ppermute(data, 'band', [(source, b) for b, source in enumerate(source...]
    pallas_call x0 -> x1, Pallas kernels: none -> 1.7 us  [ahead(): pl.pallas_call(ahead_body, in_specs=[here] * 5, out_specs=(here, here), o...]
    ppermute x6, starting transfers between devices: 8.81 us -> 7.19 us  [from_place(): lax.ppermute(data, 'band', [(source, b) for b, source in enumerate(source...]
    pallas_call x6, Pallas kernels: 33.4 us -> 31.9 us  [unit(): pl.pallas_call(body, in_specs=[scalar] + [pl.BlockSpec(memory_space=pl.AN...]
    ppermute x1 -> x2, starting transfers between devices: 2.44 us -> 3.19 us  [swapped_halves(): lax.ppermute(data, 'band', [((b + half) % bands, b) for b in takers(dista...]
  transfers between devices with their start and end apart: 12 -> 13, of which waited for: 6 -> 5; matrix products, arithmetic and copies ran while one was open for 0% -> 0% of each run, Pallas kernels for 33% -> 36%
where the time goes in v5:
time: 98.6 us; the launch traced here: 98.4 us
  Pallas kernels  37.7 us (38%)
  waiting for transfers between devices  30.8 us (31%)
  starting transfers between devices  28.1 us (28%)
  local copies, waits for them, and re-layouts  1.46 us (1%)
    pallas_call x6, Pallas kernels, unit(): pl.pallas_call(body, in_specs=[scalar] + [pl.BlockSpec(memory_space=pl.AN...  31.9 us
    ppermute x1, waiting for transfers between devices, shards(): far = lax.ppermute(near, 'grid', [(0, 1), (1, 0)])  12.3 us
    ppermute x2, starting transfers between devices, from_half(): lax.ppermute(data, 'band', [(b // half * half + source % half, b) for b,...  7.77 us
    ppermute x2, waiting for transfers between devices, swapped_halves(): lax.ppermute(data, 'band', [((b + half) % bands, b) for b in takers(dista...  7.51 us
    ppermute x2, waiting for transfers between devices, from_half(): lax.ppermute(data, 'band', [(b // half * half + source % half, b) for b,...  7.46 us
    ppermute x6, starting transfers between devices, from_place(): lax.ppermute(data, 'band', [(source, b) for b, source in enumerate(source...  7.19 us
    ppermute x1, starting transfers between devices, shards(): p2_far = lax.ppermute(p2_sent, ('band', 'grid'), far_route(2))  6.05 us
    ppermute x1, starting transfers between devices, shards(): far = lax.ppermute(near, 'grid', [(0, 1), (1, 0)])  3.83 us
  transfers between devices with their start and end apart: 13, of which 5 were waited for; matrix products, arithmetic and copies ran while one was open for 0% of the time, Pallas kernels for 36%

profile of v5, /device:TPU:1, one launch (start us, length us, event | category | flops | bytes accessed | tf_op | source)
XLA Modules:
  0.0 98.4 jit_solution(6463208907789961293)
XLA Ops:
  0.0 0.0 copy-start.3
  0.0 1.4 %copy-done.3 = f32[1,40,80,80]{3,2,1,0:T(8,128)S(1)} copy-done((f32[1,40,80,80]{3,2,1,0:T(8,128)S(1)}, f32[1,40,80,80]{3,2,1,0:T(8,128)}, u32[]{:S(2)}) %copy-start.3) | copy-done | bytes 1024024
  1.4 0.9 pack.1.a.refs_0_.refs_1_
  2.4 0.0 copy-start
  2.4 0.0 copy-start.1
  2.4 0.0 copy-start.2
  2.4 0.0 copy-start.4
  2.4 3.8 %collective-permute-start = (f32[25,80,128]{2,1,0:T(8,128)S(1)}, f32[25,80,128]{2,1,0:T(8,128)S(1)}, u32[]{:S(2)}, u32[]{:S(2)}) collective-permute-start(f32[25,80,128]{2,1,0:T(8,128)S(1)} %pack.1.a.refs_0_.refs_1_), channel_id=1, source_target_pairs={{0,1},{1,0},{2,3},{3,2},{4,5},{5,4},{6,7},{7,6},{8,9},{9,8},{10,11... | collective-permute-start | bytes 3072008 | tf_op jit(solution)/shard_map/ppermute | solution.py:440
  6.2 1.2 %collective-permute-start.1 = (f32[25,80,128]{2,1,0:T(8,128)S(1)}, f32[25,80,128]{2,1,0:T(8,128)S(1)}, u32[]{:S(2)}, u32[]{:S(2)}) collective-permute-start(f32[25,80,128]{2,1,0:T(8,128)S(1)} %pack.1.a.refs_0_.refs_1_), channel_id=1, source_target_pairs={{4,0},{126,2},{8,4},{2,6},{12,8},{6,10},{16,12},{10,14},{20,16},{1... | collective-permute-start | bytes 3072008 | tf_op jit(solution)/shard_map/ppermute | solution.py:420
  7.5 6.6 %collective-permute-start.2 = (f32[25,80,128]{2,1,0:T(8,128)S(1)}, f32[25,80,128]{2,1,0:T(8,128)S(1)}, u32[]{:S(2)}, u32[]{:S(2)}) collective-permute-start(f32[25,80,128]{2,1,0:T(8,128)S(1)} %pack.1.a.refs_0_.refs_1_), channel_id=1, source_target_pairs={{124,0},{6,2},{0,4},{10,6},{4,8},{14,10},{8,12},{18,14},{12,16},{2... | collective-permute-start | bytes 3072008 | tf_op jit(solution)/shard_map/ppermute | solution.py:420
  14.0 1.2 %collective-permute-start.4 = (f32[25,80,128]{2,1,0:T(8,128)S(1)}, f32[25,80,128]{2,1,0:T(8,128)S(1)}, u32[]{:S(2)}, u32[]{:S(2)}) collective-permute-start(f32[25,80,128]{2,1,0:T(8,128)S(1)} %pack.1.a.refs_0_.refs_1_), channel_id=1, source_target_pairs={{2,0},{0,2},{6,4},{4,6},{10,8},{8,10},{14,12},{12,14},{18,16},{16,... | collective-permute-start | bytes 3072008 | tf_op jit(solution)/shard_map/ppermute | solution.py:417
  15.3 12.3 %collective-permute-done.b.refs_2_.refs_3_ = f32[25,80,128]{2,1,0:T(8,128)S(1)} collective-permute-done((f32[25,80,128]{2,1,0:T(8,128)S(1)}, f32[25,80,128]{2,1,0:T(8,128)S(1)}, u32[]{:S(2)}, u32[]{:S(2)}) %collective-permute-start) | collective-permute-done | bytes 1024032 | tf_op jit(solution)/shard_map/ppermute | solution.py:440
  27.5 3.1 %collective-permute-done.1.b = f32[25,80,128]{2,1,0:T(8,128)S(1)} collective-permute-done((f32[25,80,128]{2,1,0:T(8,128)S(1)}, f32[25,80,128]{2,1,0:T(8,128)S(1)}, u32[]{:S(2)}, u32[]{:S(2)}) %collective-permute-start.1) | collective-permute-done | bytes 1024032 | tf_op jit(solution)/shard_map/ppermute | solution.py:420
  30.7 4.3 %collective-permute-done.2.b = f32[25,80,128]{2,1,0:T(8,128)S(1)} collective-permute-done((f32[25,80,128]{2,1,0:T(8,128)S(1)}, f32[25,80,128]{2,1,0:T(8,128)S(1)}, u32[]{:S(2)}, u32[]{:S(2)}) %collective-permute-start.2) | collective-permute-done | bytes 1024032 | tf_op jit(solution)/shard_map/ppermute | solution.py:420
  35.0 2.6 %collective-permute-start.5 = (f32[25,80,128]{2,1,0:T(8,128)S(1)}, f32[25,80,128]{2,1,0:T(8,128)S(1)}, u32[]{:S(2)}, u32[]{:S(2)}) collective-permute-start(f32[25,80,128]{2,1,0:T(8,128)S(1)} %collective-permute-done.b.refs_2_.refs_3_), channel_id=1, source_target_pairs={{2,0},{0,2},{6,4},{4,6},{10,8},{8,10},{14,12},{12,14},{18,16},{16,... | collective-permute-start | bytes 3072008 | tf_op jit(solution)/shard_map/ppermute | solution.py:417
  37.6 2.3 %collective-permute-start.6 = (f32[25,80,128]{2,1,0:T(8,128)S(1)}, f32[25,80,128]{2,1,0:T(8,128)S(1)}, u32[]{:S(2)}, u32[]{:S(2)}) collective-permute-start(f32[25,80,128]{2,1,0:T(8,128)S(1)} %collective-permute-done.1.b), channel_id=1, source_target_pairs={{130,2},{252,124},{2,130},{124,252},{131,3},{253,125},{3,131},{125... | collective-permute-start | bytes 3072008 | tf_op jit(solution)/shard_map/ppermute | solution.py:430
  39.9 0.2 choose.3
  40.1 0.1 collective-permute-start.3
  40.1 0.0 collective-permute-done.4.refs_1_.a_2.refs_2_.refs_0_
  40.2 0.0 collective-permute-done.5.refs_3_.refs_4_.refs_2_
  40.2 0.0 copy-done
  40.2 0.0 copy-done.1
  40.2 0.0 copy-done.2
  40.2 0.0 copy-done.4
  40.2 5.1 %unit.6 = (f32[25,80,128]{2,1,0:T(8,128)S(1)}, s32[1,1]{1,0:T(1,128)}, f32[25,80,128]{2,1,0:T(8,128)S(1)}) custom-call(s32[1,1]{1,0:T(1,128)} %constant.4.clone.1.order, f32[25,80,128]{2,1,0:T(8,128)S(1)} %pack.1.a.refs_0_.refs_1_, f32[25,80,128]{2,1,0:T(8,128)S(1)} %collective-permute-done.4.refs_1_.a_2.refs_2_.refs_0_, ...), custom_call_target="tpu_custom_call" | custom-call | flops 1 | bytes 1 | tf_op jit(solution)/shard_map/unit/pallas_call | solution.py:274
  45.4 7.5 %collective-permute-done.6.a = f32[25,80,128]{2,1,0:T(8,128)S(1)} collective-permute-done((f32[25,80,128]{2,1,0:T(8,128)S(1)}, f32[25,80,128]{2,1,0:T(8,128)S(1)}, u32[]{:S(2)}, u32[]{:S(2)}) %collective-permute-start.6) | collective-permute-done | bytes 1024032 | tf_op jit(solution)/shard_map/ppermute | solution.py:430
  52.9 0.8 choose.4.b.refs_2_.refs_0_.refs_3_
  53.7 0.1 collective-permute-start.7
  53.8 1.7 %ahead.1 = (f32[40,80,128]{2,1,0:T(8,128)S(1)}, f32[40,80,128]{2,1,0:T(8,128)S(1)}) custom-call(f32[25,80,128]{2,1,0:T(8,128)S(1)} %pack.1.a.refs_0_.refs_1_, f32[25,80,128]{2,1,0:T(8,128)S(1)} %collective-permute-done.4.refs_1_.a_2.refs_2_.refs_0_, f32[25,80,128]{2,1,0:T(8,128)S(1)} %choose.4.b.refs_2_.refs_0_.refs_3_, bf16[80,240]{1,0:T(8,128)(2,1)S(1)} %copy-done.1, ...), custom_call_target="tpu_custom_call" | custom-call | flops 1 | bytes 1 | tf_op jit(solution)/shard_map/ahead/pallas_call | solution.py:304
  55.5 3.5 %collective-permute-done.3.refs_4_.refs_2_.refs_5_ = f32[25,80,128]{2,1,0:T(8,128)S(1)} collective-permute-done((f32[25,80,128]{2,1,0:T(8,128)S(1)}, f32[25,80,128]{2,1,0:T(8,128)S(1)}, u32[]{:S(2)}, u32[]{:S(2)}) %collective-permute-start.3) | collective-permute-done | bytes 1024032 | tf_op jit(solution)/shard_map/ppermute | solution.py:446
  59.0 0.0 collective-permute-done.7.refs_1_
  59.0 0.0 collective-permute-start.8
  59.0 6.0 %collective-permute-start.9 = (f32[25,80,128]{2,1,0:T(8,128)S(1)}, f32[25,80,128]{2,1,0:T(8,128)S(1)}, u32[]{:S(2)}, u32[]{:S(2)}) collective-permute-start(f32[25,80,128]{2,1,0:T(8,128)S(1)} %get-tuple-element.43), channel_id=1, source_target_pairs={{253,0},{252,1},{6,2},{7,3},{0,4},{1,5},{10,6},{11,7},{4,8},{5,9},... | collective-permute-start | bytes 3072008 | tf_op jit(solution)/shard_map/ppermute | solution.py:450
  65.0 0.9 collective-permute-start.10
  65.9 4.9 %unit.7 = (f32[25,80,128]{2,1,0:T(8,128)S(1)}, s32[1,1]{1,0:T(1,128)}) custom-call(s32[1,1]{1,0:T(1,128)} %get-tuple-element.36.order, f32[40,80,128]{2,1,0:T(8,128)S(1)} %get-tuple-element.37.refs_0_, f32[25,80,128]{2,1,0:T(8,128)S(1)} %pack.1.a.refs_0_.refs_1_, f32[25,80,128]{2,1,0:T(8,128)S(1)} %choose.4.b.refs_2_.refs_0_.refs_3_, ...), custom_call_target="tpu_custom_call" | custom-call | flops 1 | bytes 1 | tf_op jit(solution)/shard_map/unit/pallas_call | solution.py:274
  70.8 0.0 collective-permute-done.8.refs_3_
  70.9 5.6 %unit.8 = (f32[25,80,128]{2,1,0:T(8,128)S(1)}, s32[1,1]{1,0:T(1,128)}) custom-call(s32[1,1]{1,0:T(1,128)} %get-tuple-element.40.order, f32[25,80,128]{2,1,0:T(8,128)S(1)} %choose.4.b.refs_2_.refs_0_.refs_3_, f32[25,80,128]{2,1,0:T(8,128)S(1)} %collective-permute-done.7.refs_1_, f32[25,80,128]{2,1,0:T(8,128)S(1)} %collective-permute-done.3.refs_4_.refs_2_.refs_5_, ...), custom_call_target="tpu_custom_call" | custom-call | flops 1 | bytes 1 | tf_op jit(solution)/shard_map/unit/pallas_call | solution.py:274
  76.5 2.6 %collective-permute-start.11 = (f32[25,80,128]{2,1,0:T(8,128)S(1)}, f32[25,80,128]{2,1,0:T(8,128)S(1)}, u32[]{:S(2)}, u32[]{:S(2)}) collective-permute-start(f32[25,80,128]{2,1,0:T(8,128)S(1)} %get-tuple-element.49), channel_id=1, source_target_pairs={{252,0},{6,2},{0,4},{10,6},{4,8},{14,10},{8,12},{18,14},{12,16},{2... | collective-permute-start | bytes 3072008 | tf_op jit(solution)/shard_map/ppermute | solution.py:417
  79.1 0.0 collective-permute-done.9.refs_0_.refs_3_.refs_4_
  79.1 5.0 %unit.9 = (f32[25,80,128]{2,1,0:T(8,128)S(1)}, s32[1,1]{1,0:T(1,128)}) custom-call(s32[1,1]{1,0:T(1,128)} %get-tuple-element.42.order, f32[25,80,128]{2,1,0:T(8,128)S(1)} %collective-permute-done.9.refs_0_.refs_3_.refs_4_, f32[40,80,128]{2,1,0:T(8,128)S(1)} %get-tuple-element.44.refs_1_, ...), custom_call_target="tpu_custom_call" | custom-call | flops 1 | bytes 1 | tf_op jit(solution)/shard_map/unit/pallas_call | solution.py:274
  84.1 0.0 collective-permute-done.10.a
  84.1 0.8 choose.5.refs_1_.refs_2_
  84.9 5.6 %unit.10 = (f32[25,80,128]{2,1,0:T(8,128)S(1)}, s32[1,1]{1,0:T(1,128)}) custom-call(s32[1,1]{1,0:T(1,128)} %get-tuple-element.45.order, f32[25,80,128]{2,1,0:T(8,128)S(1)} %collective-permute-done.4.refs_1_.a_2.refs_2_.refs_0_, f32[25,80,128]{2,1,0:T(8,128)S(1)} %choose.5.refs_1_.refs_2_, f32[25,80,128]{2,1,0:T(8,128)S(1)} %collective-permute-done.5.refs_3_.refs_4_.refs_2_, ...), custom_call_target="tpu_custom_call" | custom-call | flops 1 | bytes 1 | tf_op jit(solution)/shard_map/unit/pallas_call | solution.py:274
  90.5 0.6 collective-permute-start.12
  91.2 0.0 collective-permute-done.11.refs_0_.returned
  91.2 5.6 %unit.11 = (f32[25,80,128]{2,1,0:T(8,128)S(1)}, s32[1,1]{1,0:T(1,128)}) custom-call(s32[1,1]{1,0:T(1,128)} %get-tuple-element.48.order, f32[25,80,128]{2,1,0:T(8,128)S(1)} %collective-permute-done.11.refs_0_.returned, f32[25,80,128]{2,1,0:T(8,128)S(1)} %pack.1.a.refs_0_.refs_1_, f32[25,80,128]{2,1,0:T(8,128)S(1)} %choose.5.refs_1_.refs_2_, ...), custom_call_target="tpu_custom_call" | custom-call | flops 1 | bytes 1 | tf_op jit(solution)/shard_map/unit/pallas_call | solution.py:274
  96.8 0.0 collective-permute-done.12.theirs
  96.8 1.4 %unpack_sum.1 = f32[40,80,80]{2,1,0:T(8,128)} custom-call(f32[25,80,128]{2,1,0:T(8,128)S(1)} %get-tuple-element.51.total, f32[25,80,128]{2,1,0:T(8,128)S(1)} %collective-permute-done.11.refs_0_.returned, f32[25,80,128]{2,1,0:T(8,128)S(1)} %collective-permute-done.12.theirs), custom_call_target="tpu_custom_call" | custom-call | tf_op jit(solution)/shard_map/unpack_sum/pallas_call | solution.py:394
Async XLA Ops:
  0.0 1.4 %copy-start.3 = (f32[1,40,80,80]{3,2,1,0:T(8,128)S(1)}, f32[1,40,80,80]{3,2,1,0:T(8,128)}, u32[]{:S(2)}) copy-start(f32[1,40,80,80]{3,2,1,0:T(8,128)} %param.5) | copy-start | bytes 3072004
  2.4 37.8 %copy-start = (f32[6,41,8,128]{3,2,1,0:T(8,128)S(1)}, f32[6,41,8,128]{3,2,1,0:T(8,128)}, u32[]{:S(2)}) copy-start(f32[6,41,8,128]{3,2,1,0:T(8,128)} %constant.13.clone.refs_7_.refs_8_.refs_9_) | copy-start | bytes 3022852
  2.4 37.8 %copy-start.1 = (bf16[80,240]{1,0:T(8,128)(2,1)S(1)}, bf16[80,240]{1,0:T(8,128)(2,1)}, u32[]{:S(2)}) copy-start(bf16[80,240]{1,0:T(8,128)(2,1)} %constant.10.clone.refs_4_.table_y.refs_5_.refs_6_) | copy-start | bytes 115204
  2.4 37.8 %copy-start.2 = (bf16[80,240]{1,0:T(8,128)(2,1)S(1)}, bf16[80,240]{1,0:T(8,128)(2,1)}, u32[]{:S(2)}) copy-start(bf16[80,240]{1,0:T(8,128)(2,1)} %constant.11.clone.refs_5_.table_to.refs_6_.refs_7_) | copy-start | bytes 115204
  2.4 37.8 %copy-start.4 = (bf16[80,240]{1,0:T(8,128)(2,1)S(1)}, bf16[80,240]{1,0:T(8,128)(2,1)}, u32[]{:S(2)}) copy-start(bf16[80,240]{1,0:T(8,128)(2,1)} %constant.12.clone.refs_6_.refs_7_.refs_8_) | copy-start | bytes 115204
  2.4 25.1 %collective-permute-start = (f32[25,80,128]{2,1,0:T(8,128)S(1)}, f32[25,80,128]{2,1,0:T(8,128)S(1)}, u32[]{:S(2)}, u32[]{:S(2)}) collective-permute-start(f32[25,80,128]{2,1,0:T(8,128)S(1)} %pack.1.a.refs_0_.refs_1_), channel_id=1, source_target_pairs={{0,1},{1,0},{2,3},{3,2},{4,5},{5,4},{6,7},{7,6},{8,9},{9,8},{10,11... | collective-permute-start | bytes 3072008 | tf_op jit(solution)/shard_map/ppermute | solution.py:440
  6.2 24.4 %collective-permute-start.1 = (f32[25,80,128]{2,1,0:T(8,128)S(1)}, f32[25,80,128]{2,1,0:T(8,128)S(1)}, u32[]{:S(2)}, u32[]{:S(2)}) collective-permute-start(f32[25,80,128]{2,1,0:T(8,128)S(1)} %pack.1.a.refs_0_.refs_1_), channel_id=1, source_target_pairs={{4,0},{126,2},{8,4},{2,6},{12,8},{6,10},{16,12},{10,14},{20,16},{1... | collective-permute-start | bytes 3072008 | tf_op jit(solution)/shard_map/ppermute | solution.py:420
  7.5 27.5 %collective-permute-start.2 = (f32[25,80,128]{2,1,0:T(8,128)S(1)}, f32[25,80,128]{2,1,0:T(8,128)S(1)}, u32[]{:S(2)}, u32[]{:S(2)}) collective-permute-start(f32[25,80,128]{2,1,0:T(8,128)S(1)} %pack.1.a.refs_0_.refs_1_), channel_id=1, source_target_pairs={{124,0},{6,2},{0,4},{10,6},{4,8},{14,10},{8,12},{18,14},{12,16},{2... | collective-permute-start | bytes 3072008 | tf_op jit(solution)/shard_map/ppermute | solution.py:420
  14.0 26.1 %collective-permute-start.4 = (f32[25,80,128]{2,1,0:T(8,128)S(1)}, f32[25,80,128]{2,1,0:T(8,128)S(1)}, u32[]{:S(2)}, u32[]{:S(2)}) collective-permute-start(f32[25,80,128]{2,1,0:T(8,128)S(1)} %pack.1.a.refs_0_.refs_1_), channel_id=1, source_target_pairs={{2,0},{0,2},{6,4},{4,6},{10,8},{8,10},{14,12},{12,14},{18,16},{16,... | collective-permute-start | bytes 3072008 | tf_op jit(solution)/shard_map/ppermute | solution.py:417
  35.0 5.2 %collective-permute-start.5 = (f32[25,80,128]{2,1,0:T(8,128)S(1)}, f32[25,80,128]{2,1,0:T(8,128)S(1)}, u32[]{:S(2)}, u32[]{:S(2)}) collective-permute-start(f32[25,80,128]{2,1,0:T(8,128)S(1)} %collective-permute-done.b.refs_2_.refs_3_), channel_id=1, source_target_pairs={{2,0},{0,2},{6,4},{4,6},{10,8},{8,10},{14,12},{12,14},{18,16},{16,... | collective-permute-start | bytes 3072008 | tf_op jit(solution)/shard_map/ppermute | solution.py:417
  37.6 15.3 %collective-permute-start.6 = (f32[25,80,128]{2,1,0:T(8,128)S(1)}, f32[25,80,128]{2,1,0:T(8,128)S(1)}, u32[]{:S(2)}, u32[]{:S(2)}) collective-permute-start(f32[25,80,128]{2,1,0:T(8,128)S(1)} %collective-permute-done.1.b), channel_id=1, source_target_pairs={{130,2},{252,124},{2,130},{124,252},{131,3},{253,125},{3,131},{125... | collective-permute-start | bytes 3072008 | tf_op jit(solution)/shard_map/ppermute | solution.py:430
  40.1 18.9 %collective-permute-start.3 = (f32[25,80,128]{2,1,0:T(8,128)S(1)}, f32[25,80,128]{2,1,0:T(8,128)S(1)}, u32[]{:S(2)}, u32[]{:S(2)}) collective-permute-start(f32[25,80,128]{2,1,0:T(8,128)S(1)} %choose.3), channel_id=1, source_target_pairs={{4,0},{5,1},{255,2},{254,3},{8,4},{9,5},{2,6},{3,7},{12,8},{13,9},... | collective-permute-start | bytes 3072008 | tf_op jit(solution)/shard_map/ppermute | solution.py:446
  53.7 5.3 %collective-permute-start.7 = (f32[25,80,128]{2,1,0:T(8,128)S(1)}, f32[25,80,128]{2,1,0:T(8,128)S(1)}, u32[]{:S(2)}, u32[]{:S(2)}) collective-permute-start(f32[25,80,128]{2,1,0:T(8,128)S(1)} %choose.4.b.refs_2_.refs_0_.refs_3_), channel_id=1, source_target_pairs={{2,0},{0,2},{6,4},{4,6},{10,8},{8,10},{14,12},{12,14},{18,16},{16,... | collective-permute-start | bytes 3072008 | tf_op jit(solution)/shard_map/ppermute | solution.py:417
  59.0 11.9 %collective-permute-start.8 = (f32[25,80,128]{2,1,0:T(8,128)S(1)}, f32[25,80,128]{2,1,0:T(8,128)S(1)}, u32[]{:S(2)}, u32[]{:S(2)}) collective-permute-start(f32[25,80,128]{2,1,0:T(8,128)S(1)} %collective-permute-done.3.refs_4_.refs_2_.refs_5_), channel_id=1, source_target_pairs={{2,0},{0,2},{6,4},{4,6},{10,8},{8,10},{14,12},{12,14},{18,16},{16,... | collective-permute-start | bytes 3072008 | tf_op jit(solution)/shard_map/ppermute | solution.py:417
  59.0 20.1 %collective-permute-start.9 = (f32[25,80,128]{2,1,0:T(8,128)S(1)}, f32[25,80,128]{2,1,0:T(8,128)S(1)}, u32[]{:S(2)}, u32[]{:S(2)}) collective-permute-start(f32[25,80,128]{2,1,0:T(8,128)S(1)} %get-tuple-element.43), channel_id=1, source_target_pairs={{253,0},{252,1},{6,2},{7,3},{0,4},{1,5},{10,6},{11,7},{4,8},{5,9},... | collective-permute-start | bytes 3072008 | tf_op jit(solution)/shard_map/ppermute | solution.py:450
  65.0 19.1 %collective-permute-start.10 = (f32[25,80,128]{2,1,0:T(8,128)S(1)}, f32[25,80,128]{2,1,0:T(8,128)S(1)}, u32[]{:S(2)}, u32[]{:S(2)}) collective-permute-start(f32[25,80,128]{2,1,0:T(8,128)S(1)} %collective-permute-done.2.b), channel_id=1, source_target_pairs={{128,0},{254,126},{0,128},{126,254},{129,1},{255,127},{1,129},{127... | collective-permute-start | bytes 3072008 | tf_op jit(solution)/shard_map/ppermute | solution.py:430
  76.5 14.7 %collective-permute-start.11 = (f32[25,80,128]{2,1,0:T(8,128)S(1)}, f32[25,80,128]{2,1,0:T(8,128)S(1)}, u32[]{:S(2)}, u32[]{:S(2)}) collective-permute-start(f32[25,80,128]{2,1,0:T(8,128)S(1)} %get-tuple-element.49), channel_id=1, source_target_pairs={{252,0},{6,2},{0,4},{10,6},{4,8},{14,10},{8,12},{18,14},{12,16},{2... | collective-permute-start | bytes 3072008 | tf_op jit(solution)/shard_map/ppermute | solution.py:417
  90.5 6.3 %collective-permute-start.12 = (f32[25,80,128]{2,1,0:T(8,128)S(1)}, f32[25,80,128]{2,1,0:T(8,128)S(1)}, u32[]{:S(2)}, u32[]{:S(2)}) collective-permute-start(f32[25,80,128]{2,1,0:T(8,128)S(1)} %get-tuple-element.52), channel_id=1, source_target_pairs={{2,0},{0,2},{6,4},{4,6},{10,8},{8,10},{14,12},{12,14},{18,16},{16,... | collective-permute-start | bytes 3072008 | tf_op jit(solution)/shard_map/ppermute | solution.py:417

commit v6 on v5

--- a/solution.py
+++ b/solution.py
@@ -253,15 +253,15 @@
         backward_y(group)
 
 
-def unit(a, b, constants, after, total=None, waits=(), near_at=None, ready=None):
+def unit(a, b, constants, after, total=None, waits=(), pick=None, ready=None):
     operands = [a[0], b[0], a[1], b[1], *constants]
 
     def body(order, *refs):
         refs = list(refs[len(waits) :])
         near_ready = None if ready is None else refs.pop(0)
-        if near_at is not None:
-            sent = refs.pop(len(operands) + (total is not None) + 2)
-            copy_chosen(near_at, refs[0], refs[2], sent)
+        if pick is not None:
+            x, y, picked = refs.pop(0), refs.pop(0), refs.pop(len(operands) + (total is not None) + 2)
+            copy_chosen(pick[0], x, y, picked)
         ins, rest = refs[: len(operands)], refs[len(operands) :]
         if total is None:
             unit_body(near_ready, *ins, None, *rest)
@@ -270,13 +270,13 @@
 
     here = pl.BlockSpec(memory_space=pltpu.VMEM)
     scalar = pl.BlockSpec(memory_space=pltpu.SMEM)
-    operands_all = (*(() if ready is None else (ready,)), *operands, *(() if total is None else (total,)))
+    operands_all = (*(() if ready is None else (ready,)), *(() if pick is None else pick[1:]), *operands, *(() if total is None else (total,)))
     return pl.pallas_call(
         body,
         in_specs=[scalar] + [pl.BlockSpec(memory_space=pl.ANY)] * len(waits) + [here] * len(operands_all),
-        out_specs=(here, scalar) + (here,) * (near_at is not None),
+        out_specs=(here, scalar) + (here,) * (pick is not None),
         out_shape=(jax.ShapeDtypeStruct(PACKED, F32), jax.ShapeDtypeStruct((1, 1), jnp.int32))
-        + (jax.ShapeDtypeStruct(PACKED, F32),) * (near_at is not None),
+        + (jax.ShapeDtypeStruct(PACKED, F32),) * (pick is not None),
         scratch_shapes=[
             pltpu.VMEM((N, N, LANES), F32),
             pltpu.VMEM((HALF, N, LANES), F32),
@@ -446,7 +446,7 @@
     m2_far = lax.ppermute(choose(givers(-2), near, far, first), ("band", "grid"), far_route(-2))
     m1 = (other_core(near), other_core(far))
     m2_swapped = swapped_halves(m2_half, -2)
-    total, after, p2_sent = unit(own, m1, constants, first, near_at=givers(2))
+    total, after, p2_sent = unit(own, m1, constants, first, pick=(givers(2), near, far))
     p2_far = lax.ppermute(p2_sent, ("band", "grid"), far_route(2))
     p2_half, after = lax.optimization_barrier((p2_half, after))
     p2_swapped = swapped_halves(p2_half, 2)
@@ -459,8 +459,10 @@
     total, after = unit(own, m2, constants, after, total, ready=own_m2)
     lent, after = unit(m2, p1, constants, after)
     returned = from_place(lent, 2)
-    partner, after = unit(m1, m2, constants, after, waits=(p2_far,), ready=m1_m2)
-    p2 = (choose(takers(2), p2_swapped, p2_half, after), p2_far)
+    partner, after, p2_near = unit(
+        m1, m2, constants, after, waits=(p2_far,), pick=(takers(2), p2_swapped, p2_half), ready=m1_m2
+    )
+    p2 = (p2_near, p2_far)
     partner, after = unit(m1, p2, constants, after, partner)
     theirs = other_core(partner)
     total, after = unit(own, p2, constants, after, total, waits=(returned,))

time: 98.6 us -> 98.1 us (level)
  transfers between devices with their start and end apart: 13 -> 13, of which waited for: 5 -> 6; matrix products, arithmetic and copies ran while one was open for 0% -> 0% of each run, Pallas kernels for 36% -> 36%
where the time goes in v6:
time: 98.1 us; the launch traced here: 97.9 us
  Pallas kernels  37.1 us (38%)
  waiting for transfers between devices  30.9 us (31%)
  starting transfers between devices  28.1 us (29%)
  local copies, waits for them, and re-layouts  1.46 us (1%)
    pallas_call x6, Pallas kernels, unit(): pl.pallas_call(body, in_specs=[scalar] + [pl.BlockSpec(memory_space=pl.AN...  32.2 us
    ppermute x1, waiting for transfers between devices, shards(): far = lax.ppermute(near, 'grid', [(0, 1), (1, 0)])  12.3 us
    ppermute x2, starting transfers between devices, from_half(): lax.ppermute(data, 'band', [(b // half * half + source % half, b) for b,...  7.77 us
    ppermute x2, waiting for transfers between devices, swapped_halves(): lax.ppermute(data, 'band', [((b + half) % bands, b) for b in takers(dista...  7.52 us
    ppermute x2, waiting for transfers between devices, from_half(): lax.ppermute(data, 'band', [(b // half * half + source % half, b) for b,...  7.46 us
    ppermute x6, starting transfers between devices, from_place(): lax.ppermute(data, 'band', [(source, b) for b, source in enumerate(source...  7.13 us
    ppermute x1, starting transfers between devices, shards(): p2_far = lax.ppermute(p2_sent, ('band', 'grid'), far_route(2))  6.05 us
    ppermute x1, starting transfers between devices, shards(): far = lax.ppermute(near, 'grid', [(0, 1), (1, 0)])  3.83 us
  transfers between devices with their start and end apart: 13, of which 6 were waited for; matrix products, arithmetic and copies ran while one was open for 0% of the time, Pallas kernels for 36%

profile of v6, /device:TPU:1, one launch (start us, length us, event | category | flops | bytes accessed | tf_op | source)
XLA Modules:
  0.0 97.9 jit_solution(3080138447216779643)
XLA Ops:
  0.0 0.0 copy-start.3
  0.0 1.4 %copy-done.3 = f32[1,40,80,80]{3,2,1,0:T(8,128)S(1)} copy-done((f32[1,40,80,80]{3,2,1,0:T(8,128)S(1)}, f32[1,40,80,80]{3,2,1,0:T(8,128)}, u32[]{:S(2)}) %copy-start.3) | copy-done | bytes 1024024
  1.4 0.9 pack.1.a.refs_0_.refs_2_.refs_1_
  2.4 0.0 copy-start
  2.4 0.0 copy-start.1
  2.4 0.0 copy-start.2
  2.4 0.0 copy-start.4
  2.4 3.8 %collective-permute-start = (f32[25,80,128]{2,1,0:T(8,128)S(1)}, f32[25,80,128]{2,1,0:T(8,128)S(1)}, u32[]{:S(2)}, u32[]{:S(2)}) collective-permute-start(f32[25,80,128]{2,1,0:T(8,128)S(1)} %pack.1.a.refs_0_.refs_2_.refs_1_), channel_id=1, source_target_pairs={{0,1},{1,0},{2,3},{3,2},{4,5},{5,4},{6,7},{7,6},{8,9},{9,8},{10,11... | collective-permute-start | bytes 3072008 | tf_op jit(solution)/shard_map/ppermute | solution.py:440
  6.2 1.2 %collective-permute-start.1 = (f32[25,80,128]{2,1,0:T(8,128)S(1)}, f32[25,80,128]{2,1,0:T(8,128)S(1)}, u32[]{:S(2)}, u32[]{:S(2)}) collective-permute-start(f32[25,80,128]{2,1,0:T(8,128)S(1)} %pack.1.a.refs_0_.refs_2_.refs_1_), channel_id=1, source_target_pairs={{4,0},{126,2},{8,4},{2,6},{12,8},{6,10},{16,12},{10,14},{20,16},{1... | collective-permute-start | bytes 3072008 | tf_op jit(solution)/shard_map/ppermute | solution.py:420
  7.5 6.6 %collective-permute-start.2 = (f32[25,80,128]{2,1,0:T(8,128)S(1)}, f32[25,80,128]{2,1,0:T(8,128)S(1)}, u32[]{:S(2)}, u32[]{:S(2)}) collective-permute-start(f32[25,80,128]{2,1,0:T(8,128)S(1)} %pack.1.a.refs_0_.refs_2_.refs_1_), channel_id=1, source_target_pairs={{124,0},{6,2},{0,4},{10,6},{4,8},{14,10},{8,12},{18,14},{12,16},{2... | collective-permute-start | bytes 3072008 | tf_op jit(solution)/shard_map/ppermute | solution.py:420
  14.0 1.2 %collective-permute-start.4 = (f32[25,80,128]{2,1,0:T(8,128)S(1)}, f32[25,80,128]{2,1,0:T(8,128)S(1)}, u32[]{:S(2)}, u32[]{:S(2)}) collective-permute-start(f32[25,80,128]{2,1,0:T(8,128)S(1)} %pack.1.a.refs_0_.refs_2_.refs_1_), channel_id=1, source_target_pairs={{2,0},{0,2},{6,4},{4,6},{10,8},{8,10},{14,12},{12,14},{18,16},{16,... | collective-permute-start | bytes 3072008 | tf_op jit(solution)/shard_map/ppermute | solution.py:417
  15.3 12.3 %collective-permute-done.b.refs_1_.refs_4_.refs_3_ = f32[25,80,128]{2,1,0:T(8,128)S(1)} collective-permute-done((f32[25,80,128]{2,1,0:T(8,128)S(1)}, f32[25,80,128]{2,1,0:T(8,128)S(1)}, u32[]{:S(2)}, u32[]{:S(2)}) %collective-permute-start) | collective-permute-done | bytes 1024032 | tf_op jit(solution)/shard_map/ppermute | solution.py:440
  27.5 3.1 %collective-permute-done.1.b = f32[25,80,128]{2,1,0:T(8,128)S(1)} collective-permute-done((f32[25,80,128]{2,1,0:T(8,128)S(1)}, f32[25,80,128]{2,1,0:T(8,128)S(1)}, u32[]{:S(2)}, u32[]{:S(2)}) %collective-permute-start.1) | collective-permute-done | bytes 1024032 | tf_op jit(solution)/shard_map/ppermute | solution.py:420
  30.7 4.3 %collective-permute-done.2.refs_3_ = f32[25,80,128]{2,1,0:T(8,128)S(1)} collective-permute-done((f32[25,80,128]{2,1,0:T(8,128)S(1)}, f32[25,80,128]{2,1,0:T(8,128)S(1)}, u32[]{:S(2)}, u32[]{:S(2)}) %collective-permute-start.2) | collective-permute-done | bytes 1024032 | tf_op jit(solution)/shard_map/ppermute | solution.py:420
  35.0 2.6 %collective-permute-start.5 = (f32[25,80,128]{2,1,0:T(8,128)S(1)}, f32[25,80,128]{2,1,0:T(8,128)S(1)}, u32[]{:S(2)}, u32[]{:S(2)}) collective-permute-start(f32[25,80,128]{2,1,0:T(8,128)S(1)} %collective-permute-done.b.refs_1_.refs_4_.refs_3_), channel_id=1, source_target_pairs={{2,0},{0,2},{6,4},{4,6},{10,8},{8,10},{14,12},{12,14},{18,16},{16,... | collective-permute-start | bytes 3072008 | tf_op jit(solution)/shard_map/ppermute | solution.py:417
  37.6 2.3 %collective-permute-start.6 = (f32[25,80,128]{2,1,0:T(8,128)S(1)}, f32[25,80,128]{2,1,0:T(8,128)S(1)}, u32[]{:S(2)}, u32[]{:S(2)}) collective-permute-start(f32[25,80,128]{2,1,0:T(8,128)S(1)} %collective-permute-done.1.b), channel_id=1, source_target_pairs={{130,2},{252,124},{2,130},{124,252},{131,3},{253,125},{3,131},{125... | collective-permute-start | bytes 3072008 | tf_op jit(solution)/shard_map/ppermute | solution.py:430
  39.9 0.2 choose.2
  40.1 0.1 collective-permute-start.3
  40.1 0.0 collective-permute-done.4.refs_3_.a_2.refs_4_.refs_0_
  40.2 0.0 collective-permute-done.5.refs_5_.refs_6_.refs_2_
  40.2 0.0 copy-done
  40.2 0.0 copy-done.1
  40.2 0.0 copy-done.2
  40.2 0.0 copy-done.4
  40.2 5.1 %unit.6 = (f32[25,80,128]{2,1,0:T(8,128)S(1)}, s32[1,1]{1,0:T(1,128)}, f32[25,80,128]{2,1,0:T(8,128)S(1)}) custom-call(s32[1,1]{1,0:T(1,128)} %constant.4.clone.1.order, f32[25,80,128]{2,1,0:T(8,128)S(1)} %pack.1.a.refs_0_.refs_2_.refs_1_, f32[25,80,128]{2,1,0:T(8,128)S(1)} %collective-permute-done.b.refs_1_.refs_4_.refs_3_, ...), custom_call_target="tpu_custom_call" | custom-call | flops 1 | bytes 1 | tf_op jit(solution)/shard_map/unit/pallas_call | solution.py:274
  45.4 7.5 %collective-permute-done.6.a = f32[25,80,128]{2,1,0:T(8,128)S(1)} collective-permute-done((f32[25,80,128]{2,1,0:T(8,128)S(1)}, f32[25,80,128]{2,1,0:T(8,128)S(1)}, u32[]{:S(2)}, u32[]{:S(2)}) %collective-permute-start.6) | collective-permute-done | bytes 1024032 | tf_op jit(solution)/shard_map/ppermute | solution.py:430
  52.9 0.8 choose.3.b.refs_2_.refs_0_.refs_5_
  53.7 0.1 collective-permute-start.7
  53.8 1.7 %ahead.1 = (f32[40,80,128]{2,1,0:T(8,128)S(1)}, f32[40,80,128]{2,1,0:T(8,128)S(1)}) custom-call(f32[25,80,128]{2,1,0:T(8,128)S(1)} %pack.1.a.refs_0_.refs_2_.refs_1_, f32[25,80,128]{2,1,0:T(8,128)S(1)} %collective-permute-done.4.refs_3_.a_2.refs_4_.refs_0_, f32[25,80,128]{2,1,0:T(8,128)S(1)} %choose.3.b.refs_2_.refs_0_.refs_5_, ...), custom_call_target="tpu_custom_call" | custom-call | flops 1 | bytes 1 | tf_op jit(solution)/shard_map/ahead/pallas_call | solution.py:304
  55.5 3.5 %collective-permute-done.3.refs_4_.refs_2_.refs_7_ = f32[25,80,128]{2,1,0:T(8,128)S(1)} collective-permute-done((f32[25,80,128]{2,1,0:T(8,128)S(1)}, f32[25,80,128]{2,1,0:T(8,128)S(1)}, u32[]{:S(2)}, u32[]{:S(2)}) %collective-permute-start.3) | collective-permute-done | bytes 1024032 | tf_op jit(solution)/shard_map/ppermute | solution.py:446
  59.0 0.0 collective-permute-done.7.refs_1_
  59.0 0.0 collective-permute-start.8
  59.0 6.0 %collective-permute-start.9 = (f32[25,80,128]{2,1,0:T(8,128)S(1)}, f32[25,80,128]{2,1,0:T(8,128)S(1)}, u32[]{:S(2)}, u32[]{:S(2)}) collective-permute-start(f32[25,80,128]{2,1,0:T(8,128)S(1)} %get-tuple-element.44), channel_id=1, source_target_pairs={{253,0},{252,1},{6,2},{7,3},{0,4},{1,5},{10,6},{11,7},{4,8},{5,9},... | collective-permute-start | bytes 3072008 | tf_op jit(solution)/shard_map/ppermute | solution.py:450
  65.0 0.9 collective-permute-start.10
  65.9 5.0 %unit.7 = (f32[25,80,128]{2,1,0:T(8,128)S(1)}, s32[1,1]{1,0:T(1,128)}) custom-call(s32[1,1]{1,0:T(1,128)} %get-tuple-element.37.order, f32[40,80,128]{2,1,0:T(8,128)S(1)} %get-tuple-element.38.refs_0_, f32[25,80,128]{2,1,0:T(8,128)S(1)} %pack.1.a.refs_0_.refs_2_.refs_1_, f32[25,80,128]{2,1,0:T(8,128)S(1)} %choose.3.b.refs_2_.refs_0_.refs_5_, ...), custom_call_target="tpu_custom_call" | custom-call | flops 1 | bytes 1 | tf_op jit(solution)/shard_map/unit/pallas_call | solution.py:274
  70.9 0.0 collective-permute-done.8.refs_3_
  70.9 5.6 %unit.8 = (f32[25,80,128]{2,1,0:T(8,128)S(1)}, s32[1,1]{1,0:T(1,128)}) custom-call(s32[1,1]{1,0:T(1,128)} %get-tuple-element.41.order, f32[25,80,128]{2,1,0:T(8,128)S(1)} %choose.3.b.refs_2_.refs_0_.refs_5_, f32[25,80,128]{2,1,0:T(8,128)S(1)} %collective-permute-done.7.refs_1_, f32[25,80,128]{2,1,0:T(8,128)S(1)} %collective-permute-done.3.refs_4_.refs_2_.refs_7_, ...), custom_call_target="tpu_custom_call" | custom-call | flops 1 | bytes 1 | tf_op jit(solution)/shard_map/unit/pallas_call | solution.py:274
  76.5 2.6 %collective-permute-start.11 = (f32[25,80,128]{2,1,0:T(8,128)S(1)}, f32[25,80,128]{2,1,0:T(8,128)S(1)}, u32[]{:S(2)}, u32[]{:S(2)}) collective-permute-start(f32[25,80,128]{2,1,0:T(8,128)S(1)} %get-tuple-element.51), channel_id=1, source_target_pairs={{252,0},{6,2},{0,4},{10,6},{4,8},{14,10},{8,12},{18,14},{12,16},{2... | collective-permute-start | bytes 3072008 | tf_op jit(solution)/shard_map/ppermute | solution.py:417
  79.2 0.0 collective-permute-done.9.refs_0_.refs_3_.refs_4_
  79.2 0.0 collective-permute-done.10.refs_2_
  79.2 5.1 %unit.9 = (f32[25,80,128]{2,1,0:T(8,128)S(1)}, s32[1,1]{1,0:T(1,128)}, f32[25,80,128]{2,1,0:T(8,128)S(1)}) custom-call(s32[1,1]{1,0:T(1,128)} %get-tuple-element.43.order, f32[25,80,128]{2,1,0:T(8,128)S(1)} %collective-permute-done.9.refs_0_.refs_3_.refs_4_, f32[40,80,128]{2,1,0:T(8,128)S(1)} %get-tuple-element.45.refs_1_, ...), custom_call_target="tpu_custom_call" | custom-call | flops 1 | bytes 1 | tf_op jit(solution)/shard_map/unit/pallas_call | solution.py:274
  84.3 5.6 %unit.10 = (f32[25,80,128]{2,1,0:T(8,128)S(1)}, s32[1,1]{1,0:T(1,128)}) custom-call(s32[1,1]{1,0:T(1,128)} %get-tuple-element.47.order, f32[25,80,128]{2,1,0:T(8,128)S(1)} %collective-permute-done.4.refs_3_.a_2.refs_4_.refs_0_, f32[25,80,128]{2,1,0:T(8,128)S(1)} %get-tuple-element.48.refs_1_.refs_2_, ...), custom_call_target="tpu_custom_call" | custom-call | flops 1 | bytes 1 | tf_op jit(solution)/shard_map/unit/pallas_call | solution.py:274
  89.9 0.6 collective-permute-start.12
  90.5 0.1 collective-permute-done.11.refs_0_.returned
  90.6 5.7 %unit.11 = (f32[25,80,128]{2,1,0:T(8,128)S(1)}, s32[1,1]{1,0:T(1,128)}) custom-call(s32[1,1]{1,0:T(1,128)} %get-tuple-element.50.order, f32[25,80,128]{2,1,0:T(8,128)S(1)} %collective-permute-done.11.refs_0_.returned, f32[25,80,128]{2,1,0:T(8,128)S(1)} %pack.1.a.refs_0_.refs_2_.refs_1_, f32[25,80,128]{2,1,0:T(8,128)S(1)} %get-tuple-element.48.refs_1_.refs_2_, ...), custom_call_target="tpu_custom_call" | custom-call | flops 1 | bytes 1 | tf_op jit(solution)/shard_map/unit/pallas_call | solution.py:274
  96.3 0.0 collective-permute-done.12.theirs
  96.3 1.4 %unpack_sum.1 = f32[40,80,80]{2,1,0:T(8,128)} custom-call(f32[25,80,128]{2,1,0:T(8,128)S(1)} %get-tuple-element.53.total, f32[25,80,128]{2,1,0:T(8,128)S(1)} %collective-permute-done.11.refs_0_.returned, f32[25,80,128]{2,1,0:T(8,128)S(1)} %collective-permute-done.12.theirs), custom_call_target="tpu_custom_call" | custom-call | tf_op jit(solution)/shard_map/unpack_sum/pallas_call | solution.py:394
Async XLA Ops:
  0.0 1.4 %copy-start.3 = (f32[1,40,80,80]{3,2,1,0:T(8,128)S(1)}, f32[1,40,80,80]{3,2,1,0:T(8,128)}, u32[]{:S(2)}) copy-start(f32[1,40,80,80]{3,2,1,0:T(8,128)} %param.5) | copy-start | bytes 3072004
  2.4 37.8 %copy-start = (f32[6,41,8,128]{3,2,1,0:T(8,128)S(1)}, f32[6,41,8,128]{3,2,1,0:T(8,128)}, u32[]{:S(2)}) copy-start(f32[6,41,8,128]{3,2,1,0:T(8,128)} %constant.13.clone.refs_9_.refs_8_.refs_7_.refs_11_) | copy-start | bytes 3022852
  2.4 37.8 %copy-start.1 = (bf16[80,240]{1,0:T(8,128)(2,1)S(1)}, bf16[80,240]{1,0:T(8,128)(2,1)}, u32[]{:S(2)}) copy-start(bf16[80,240]{1,0:T(8,128)(2,1)} %constant.10.clone.refs_6_.table_y.refs_5_.refs_4_.refs_8_) | copy-start | bytes 115204
  2.4 37.8 %copy-start.2 = (bf16[80,240]{1,0:T(8,128)(2,1)S(1)}, bf16[80,240]{1,0:T(8,128)(2,1)}, u32[]{:S(2)}) copy-start(bf16[80,240]{1,0:T(8,128)(2,1)} %constant.11.clone.refs_7_.table_to.refs_6_.refs_5_.refs_9_) | copy-start | bytes 115204
  2.4 37.8 %copy-start.4 = (bf16[80,240]{1,0:T(8,128)(2,1)S(1)}, bf16[80,240]{1,0:T(8,128)(2,1)}, u32[]{:S(2)}) copy-start(bf16[80,240]{1,0:T(8,128)(2,1)} %constant.12.clone.refs_8_.refs_7_.refs_6_.refs_10_) | copy-start | bytes 115204
  2.4 25.1 %collective-permute-start = (f32[25,80,128]{2,1,0:T(8,128)S(1)}, f32[25,80,128]{2,1,0:T(8,128)S(1)}, u32[]{:S(2)}, u32[]{:S(2)}) collective-permute-start(f32[25,80,128]{2,1,0:T(8,128)S(1)} %pack.1.a.refs_0_.refs_2_.refs_1_), channel_id=1, source_target_pairs={{0,1},{1,0},{2,3},{3,2},{4,5},{5,4},{6,7},{7,6},{8,9},{9,8},{10,11... | collective-permute-start | bytes 3072008 | tf_op jit(solution)/shard_map/ppermute | solution.py:440
  6.2 24.4 %collective-permute-start.1 = (f32[25,80,128]{2,1,0:T(8,128)S(1)}, f32[25,80,128]{2,1,0:T(8,128)S(1)}, u32[]{:S(2)}, u32[]{:S(2)}) collective-permute-start(f32[25,80,128]{2,1,0:T(8,128)S(1)} %pack.1.a.refs_0_.refs_2_.refs_1_), channel_id=1, source_target_pairs={{4,0},{126,2},{8,4},{2,6},{12,8},{6,10},{16,12},{10,14},{20,16},{1... | collective-permute-start | bytes 3072008 | tf_op jit(solution)/shard_map/ppermute | solution.py:420
  7.5 27.5 %collective-permute-start.2 = (f32[25,80,128]{2,1,0:T(8,128)S(1)}, f32[25,80,128]{2,1,0:T(8,128)S(1)}, u32[]{:S(2)}, u32[]{:S(2)}) collective-permute-start(f32[25,80,128]{2,1,0:T(8,128)S(1)} %pack.1.a.refs_0_.refs_2_.refs_1_), channel_id=1, source_target_pairs={{124,0},{6,2},{0,4},{10,6},{4,8},{14,10},{8,12},{18,14},{12,16},{2... | collective-permute-start | bytes 3072008 | tf_op jit(solution)/shard_map/ppermute | solution.py:420
  14.0 26.1 %collective-permute-start.4 = (f32[25,80,128]{2,1,0:T(8,128)S(1)}, f32[25,80,128]{2,1,0:T(8,128)S(1)}, u32[]{:S(2)}, u32[]{:S(2)}) collective-permute-start(f32[25,80,128]{2,1,0:T(8,128)S(1)} %pack.1.a.refs_0_.refs_2_.refs_1_), channel_id=1, source_target_pairs={{2,0},{0,2},{6,4},{4,6},{10,8},{8,10},{14,12},{12,14},{18,16},{16,... | collective-permute-start | bytes 3072008 | tf_op jit(solution)/shard_map/ppermute | solution.py:417
  35.0 5.2 %collective-permute-start.5 = (f32[25,80,128]{2,1,0:T(8,128)S(1)}, f32[25,80,128]{2,1,0:T(8,128)S(1)}, u32[]{:S(2)}, u32[]{:S(2)}) collective-permute-start(f32[25,80,128]{2,1,0:T(8,128)S(1)} %collective-permute-done.b.refs_1_.refs_4_.refs_3_), channel_id=1, source_target_pairs={{2,0},{0,2},{6,4},{4,6},{10,8},{8,10},{14,12},{12,14},{18,16},{16,... | collective-permute-start | bytes 3072008 | tf_op jit(solution)/shard_map/ppermute | solution.py:417
  37.6 15.3 %collective-permute-start.6 = (f32[25,80,128]{2,1,0:T(8,128)S(1)}, f32[25,80,128]{2,1,0:T(8,128)S(1)}, u32[]{:S(2)}, u32[]{:S(2)}) collective-permute-start(f32[25,80,128]{2,1,0:T(8,128)S(1)} %collective-permute-done.1.b), channel_id=1, source_target_pairs={{130,2},{252,124},{2,130},{124,252},{131,3},{253,125},{3,131},{125... | collective-permute-start | bytes 3072008 | tf_op jit(solution)/shard_map/ppermute | solution.py:430
  40.1 18.9 %collective-permute-start.3 = (f32[25,80,128]{2,1,0:T(8,128)S(1)}, f32[25,80,128]{2,1,0:T(8,128)S(1)}, u32[]{:S(2)}, u32[]{:S(2)}) collective-permute-start(f32[25,80,128]{2,1,0:T(8,128)S(1)} %choose.2), channel_id=1, source_target_pairs={{4,0},{5,1},{255,2},{254,3},{8,4},{9,5},{2,6},{3,7},{12,8},{13,9},... | collective-permute-start | bytes 3072008 | tf_op jit(solution)/shard_map/ppermute | solution.py:446
  53.7 5.3 %collective-permute-start.7 = (f32[25,80,128]{2,1,0:T(8,128)S(1)}, f32[25,80,128]{2,1,0:T(8,128)S(1)}, u32[]{:S(2)}, u32[]{:S(2)}) collective-permute-start(f32[25,80,128]{2,1,0:T(8,128)S(1)} %choose.3.b.refs_2_.refs_0_.refs_5_), channel_id=1, source_target_pairs={{2,0},{0,2},{6,4},{4,6},{10,8},{8,10},{14,12},{12,14},{18,16},{16,... | collective-permute-start | bytes 3072008 | tf_op jit(solution)/shard_map/ppermute | solution.py:417
  59.0 11.9 %collective-permute-start.8 = (f32[25,80,128]{2,1,0:T(8,128)S(1)}, f32[25,80,128]{2,1,0:T(8,128)S(1)}, u32[]{:S(2)}, u32[]{:S(2)}) collective-permute-start(f32[25,80,128]{2,1,0:T(8,128)S(1)} %collective-permute-done.3.refs_4_.refs_2_.refs_7_), channel_id=1, source_target_pairs={{2,0},{0,2},{6,4},{4,6},{10,8},{8,10},{14,12},{12,14},{18,16},{16,... | collective-permute-start | bytes 3072008 | tf_op jit(solution)/shard_map/ppermute | solution.py:417
  59.0 20.2 %collective-permute-start.9 = (f32[25,80,128]{2,1,0:T(8,128)S(1)}, f32[25,80,128]{2,1,0:T(8,128)S(1)}, u32[]{:S(2)}, u32[]{:S(2)}) collective-permute-start(f32[25,80,128]{2,1,0:T(8,128)S(1)} %get-tuple-element.44), channel_id=1, source_target_pairs={{253,0},{252,1},{6,2},{7,3},{0,4},{1,5},{10,6},{11,7},{4,8},{5,9},... | collective-permute-start | bytes 3072008 | tf_op jit(solution)/shard_map/ppermute | solution.py:450
  65.0 14.2 %collective-permute-start.10 = (f32[25,80,128]{2,1,0:T(8,128)S(1)}, f32[25,80,128]{2,1,0:T(8,128)S(1)}, u32[]{:S(2)}, u32[]{:S(2)}) collective-permute-start(f32[25,80,128]{2,1,0:T(8,128)S(1)} %collective-permute-done.2.refs_3_), channel_id=1, source_target_pairs={{128,0},{254,126},{0,128},{126,254},{129,1},{255,127},{1,129},{127... | collective-permute-start | bytes 3072008 | tf_op jit(solution)/shard_map/ppermute | solution.py:430
  76.5 14.1 %collective-permute-start.11 = (f32[25,80,128]{2,1,0:T(8,128)S(1)}, f32[25,80,128]{2,1,0:T(8,128)S(1)}, u32[]{:S(2)}, u32[]{:S(2)}) collective-permute-start(f32[25,80,128]{2,1,0:T(8,128)S(1)} %get-tuple-element.51), channel_id=1, source_target_pairs={{252,0},{6,2},{0,4},{10,6},{4,8},{14,10},{8,12},{18,14},{12,16},{2... | collective-permute-start | bytes 3072008 | tf_op jit(solution)/shard_map/ppermute | solution.py:417
  89.9 6.4 %collective-permute-start.12 = (f32[25,80,128]{2,1,0:T(8,128)S(1)}, f32[25,80,128]{2,1,0:T(8,128)S(1)}, u32[]{:S(2)}, u32[]{:S(2)}) collective-permute-start(f32[25,80,128]{2,1,0:T(8,128)S(1)} %get-tuple-element.54), channel_id=1, source_target_pairs={{2,0},{0,2},{6,4},{4,6},{10,8},{8,10},{14,12},{12,14},{18,16},{16,... | collective-permute-start | bytes 3072008 | tf_op jit(solution)/shard_map/ppermute | solution.py:417

commit v7 on v6

--- a/solution.py
+++ b/solution.py
@@ -243,7 +243,7 @@
     for group in range(0 if ready is None else GROUPS, 2 * GROUPS):
         forward_z(group)
 
-    @pl.loop(0, 2 * GROUPS)
+    @functools.partial(pl.loop, 0, 2 * GROUPS, unroll=5)()
     def _(group):
         middle(group, jnp.where(group > GROUPS, group - GROUPS, group))
 

time: 98.1 us -> 98 us (level)
  transfers between devices with their start and end apart: 13 -> 13, of which waited for: 6 -> 6; matrix products, arithmetic and copies ran while one was open for 0% -> 0% of each run, Pallas kernels for 36% -> 35%
where the time goes in v7:
time: 98 us; the launch traced here: 97.8 us
  Pallas kernels  37 us (38%)
  waiting for transfers between devices  30.9 us (32%)
  starting transfers between devices  28 us (29%)
  local copies, waits for them, and re-layouts  1.46 us (1%)
    pallas_call x6, Pallas kernels, unit(): pl.pallas_call(body, in_specs=[scalar] + [pl.BlockSpec(memory_space=pl.AN...  32 us
    ppermute x1, waiting for transfers between devices, shards(): far = lax.ppermute(near, 'grid', [(0, 1), (1, 0)])  12.3 us
    ppermute x2, starting transfers between devices, from_half(): lax.ppermute(data, 'band', [(b // half * half + source % half, b) for b,...  7.77 us
    ppermute x2, waiting for transfers between devices, swapped_halves(): lax.ppermute(data, 'band', [((b + half) % bands, b) for b in takers(dista...  7.58 us
    ppermute x2, waiting for transfers between devices, from_half(): lax.ppermute(data, 'band', [(b // half * half + source % half, b) for b,...  7.46 us
    ppermute x6, starting transfers between devices, from_place(): lax.ppermute(data, 'band', [(source, b) for b, source in enumerate(source...  7.03 us
    ppermute x1, starting transfers between devices, shards(): p2_far = lax.ppermute(p2_sent, ('band', 'grid'), far_route(2))  6.05 us
    ppermute x1, starting transfers between devices, shards(): far = lax.ppermute(near, 'grid', [(0, 1), (1, 0)])  3.83 us
  transfers between devices with their start and end apart: 13, of which 6 were waited for; matrix products, arithmetic and copies ran while one was open for 0% of the time, Pallas kernels for 35%

profile of v7, /device:TPU:1, one launch (start us, length us, event | category | flops | bytes accessed | tf_op | source)
XLA Modules:
  0.0 97.8 jit_solution(8969065476901145819)
XLA Ops:
  0.0 0.0 copy-start.3
  0.0 1.4 %copy-done.3 = f32[1,40,80,80]{3,2,1,0:T(8,128)S(1)} copy-done((f32[1,40,80,80]{3,2,1,0:T(8,128)S(1)}, f32[1,40,80,80]{3,2,1,0:T(8,128)}, u32[]{:S(2)}) %copy-start.3) | copy-done | bytes 1024024
  1.4 0.9 pack.1.a.refs_0_.refs_2_.refs_1_
  2.4 0.0 copy-start
  2.4 0.0 copy-start.1
  2.4 0.0 copy-start.2
  2.4 0.0 copy-start.4
  2.4 3.8 %collective-permute-start = (f32[25,80,128]{2,1,0:T(8,128)S(1)}, f32[25,80,128]{2,1,0:T(8,128)S(1)}, u32[]{:S(2)}, u32[]{:S(2)}) collective-permute-start(f32[25,80,128]{2,1,0:T(8,128)S(1)} %pack.1.a.refs_0_.refs_2_.refs_1_), channel_id=1, source_target_pairs={{0,1},{1,0},{2,3},{3,2},{4,5},{5,4},{6,7},{7,6},{8,9},{9,8},{10,11... | collective-permute-start | bytes 3072008 | tf_op jit(solution)/shard_map/ppermute | solution.py:440
  6.2 1.2 %collective-permute-start.1 = (f32[25,80,128]{2,1,0:T(8,128)S(1)}, f32[25,80,128]{2,1,0:T(8,128)S(1)}, u32[]{:S(2)}, u32[]{:S(2)}) collective-permute-start(f32[25,80,128]{2,1,0:T(8,128)S(1)} %pack.1.a.refs_0_.refs_2_.refs_1_), channel_id=1, source_target_pairs={{4,0},{126,2},{8,4},{2,6},{12,8},{6,10},{16,12},{10,14},{20,16},{1... | collective-permute-start | bytes 3072008 | tf_op jit(solution)/shard_map/ppermute | solution.py:420
  7.5 6.6 %collective-permute-start.2 = (f32[25,80,128]{2,1,0:T(8,128)S(1)}, f32[25,80,128]{2,1,0:T(8,128)S(1)}, u32[]{:S(2)}, u32[]{:S(2)}) collective-permute-start(f32[25,80,128]{2,1,0:T(8,128)S(1)} %pack.1.a.refs_0_.refs_2_.refs_1_), channel_id=1, source_target_pairs={{124,0},{6,2},{0,4},{10,6},{4,8},{14,10},{8,12},{18,14},{12,16},{2... | collective-permute-start | bytes 3072008 | tf_op jit(solution)/shard_map/ppermute | solution.py:420
  14.0 1.2 %collective-permute-start.4 = (f32[25,80,128]{2,1,0:T(8,128)S(1)}, f32[25,80,128]{2,1,0:T(8,128)S(1)}, u32[]{:S(2)}, u32[]{:S(2)}) collective-permute-start(f32[25,80,128]{2,1,0:T(8,128)S(1)} %pack.1.a.refs_0_.refs_2_.refs_1_), channel_id=1, source_target_pairs={{2,0},{0,2},{6,4},{4,6},{10,8},{8,10},{14,12},{12,14},{18,16},{16,... | collective-permute-start | bytes 3072008 | tf_op jit(solution)/shard_map/ppermute | solution.py:417
  15.3 12.3 %collective-permute-done.b.refs_1_.refs_4_.refs_3_ = f32[25,80,128]{2,1,0:T(8,128)S(1)} collective-permute-done((f32[25,80,128]{2,1,0:T(8,128)S(1)}, f32[25,80,128]{2,1,0:T(8,128)S(1)}, u32[]{:S(2)}, u32[]{:S(2)}) %collective-permute-start) | collective-permute-done | bytes 1024032 | tf_op jit(solution)/shard_map/ppermute | solution.py:440
  27.5 3.1 %collective-permute-done.1.b = f32[25,80,128]{2,1,0:T(8,128)S(1)} collective-permute-done((f32[25,80,128]{2,1,0:T(8,128)S(1)}, f32[25,80,128]{2,1,0:T(8,128)S(1)}, u32[]{:S(2)}, u32[]{:S(2)}) %collective-permute-start.1) | collective-permute-done | bytes 1024032 | tf_op jit(solution)/shard_map/ppermute | solution.py:420
  30.7 4.3 %collective-permute-done.2.refs_3_ = f32[25,80,128]{2,1,0:T(8,128)S(1)} collective-permute-done((f32[25,80,128]{2,1,0:T(8,128)S(1)}, f32[25,80,128]{2,1,0:T(8,128)S(1)}, u32[]{:S(2)}, u32[]{:S(2)}) %collective-permute-start.2) | collective-permute-done | bytes 1024032 | tf_op jit(solution)/shard_map/ppermute | solution.py:420
  35.0 2.6 %collective-permute-start.5 = (f32[25,80,128]{2,1,0:T(8,128)S(1)}, f32[25,80,128]{2,1,0:T(8,128)S(1)}, u32[]{:S(2)}, u32[]{:S(2)}) collective-permute-start(f32[25,80,128]{2,1,0:T(8,128)S(1)} %collective-permute-done.b.refs_1_.refs_4_.refs_3_), channel_id=1, source_target_pairs={{2,0},{0,2},{6,4},{4,6},{10,8},{8,10},{14,12},{12,14},{18,16},{16,... | collective-permute-start | bytes 3072008 | tf_op jit(solution)/shard_map/ppermute | solution.py:417
  37.6 2.3 %collective-permute-start.6 = (f32[25,80,128]{2,1,0:T(8,128)S(1)}, f32[25,80,128]{2,1,0:T(8,128)S(1)}, u32[]{:S(2)}, u32[]{:S(2)}) collective-permute-start(f32[25,80,128]{2,1,0:T(8,128)S(1)} %collective-permute-done.1.b), channel_id=1, source_target_pairs={{130,2},{252,124},{2,130},{124,252},{131,3},{253,125},{3,131},{125... | collective-permute-start | bytes 3072008 | tf_op jit(solution)/shard_map/ppermute | solution.py:430
  39.9 0.2 choose.2
  40.1 0.1 collective-permute-start.3
  40.1 0.0 collective-permute-done.4.refs_3_.a_2.refs_4_.refs_0_
  40.2 0.0 collective-permute-done.5.refs_5_.refs_6_.refs_2_
  40.2 0.0 copy-done
  40.2 0.0 copy-done.1
  40.2 0.0 copy-done.2
  40.2 0.0 copy-done.4
  40.2 5.1 %unit.6 = (f32[25,80,128]{2,1,0:T(8,128)S(1)}, s32[1,1]{1,0:T(1,128)}, f32[25,80,128]{2,1,0:T(8,128)S(1)}) custom-call(s32[1,1]{1,0:T(1,128)} %constant.4.clone.1.order, f32[25,80,128]{2,1,0:T(8,128)S(1)} %pack.1.a.refs_0_.refs_2_.refs_1_, f32[25,80,128]{2,1,0:T(8,128)S(1)} %collective-permute-done.b.refs_1_.refs_4_.refs_3_, ...), custom_call_target="tpu_custom_call" | custom-call | flops 1 | bytes 1 | tf_op jit(solution)/shard_map/unit/pallas_call | solution.py:274
  45.3 7.6 %collective-permute-done.6.a = f32[25,80,128]{2,1,0:T(8,128)S(1)} collective-permute-done((f32[25,80,128]{2,1,0:T(8,128)S(1)}, f32[25,80,128]{2,1,0:T(8,128)S(1)}, u32[]{:S(2)}, u32[]{:S(2)}) %collective-permute-start.6) | collective-permute-done | bytes 1024032 | tf_op jit(solution)/shard_map/ppermute | solution.py:430
  52.9 0.8 choose.3.b.refs_2_.refs_0_.refs_5_
  53.7 0.1 collective-permute-start.7
  53.8 1.7 %ahead.1 = (f32[40,80,128]{2,1,0:T(8,128)S(1)}, f32[40,80,128]{2,1,0:T(8,128)S(1)}) custom-call(f32[25,80,128]{2,1,0:T(8,128)S(1)} %pack.1.a.refs_0_.refs_2_.refs_1_, f32[25,80,128]{2,1,0:T(8,128)S(1)} %collective-permute-done.4.refs_3_.a_2.refs_4_.refs_0_, f32[25,80,128]{2,1,0:T(8,128)S(1)} %choose.3.b.refs_2_.refs_0_.refs_5_, ...), custom_call_target="tpu_custom_call" | custom-call | flops 1 | bytes 1 | tf_op jit(solution)/shard_map/ahead/pallas_call | solution.py:304
  55.5 3.5 %collective-permute-done.3.refs_4_.refs_2_.refs_7_ = f32[25,80,128]{2,1,0:T(8,128)S(1)} collective-permute-done((f32[25,80,128]{2,1,0:T(8,128)S(1)}, f32[25,80,128]{2,1,0:T(8,128)S(1)}, u32[]{:S(2)}, u32[]{:S(2)}) %collective-permute-start.3) | collective-permute-done | bytes 1024032 | tf_op jit(solution)/shard_map/ppermute | solution.py:446
  59.0 0.0 collective-permute-done.7.refs_1_
  59.0 0.0 collective-permute-start.8
  59.0 6.0 %collective-permute-start.9 = (f32[25,80,128]{2,1,0:T(8,128)S(1)}, f32[25,80,128]{2,1,0:T(8,128)S(1)}, u32[]{:S(2)}, u32[]{:S(2)}) collective-permute-start(f32[25,80,128]{2,1,0:T(8,128)S(1)} %get-tuple-element.44), channel_id=1, source_target_pairs={{253,0},{252,1},{6,2},{7,3},{0,4},{1,5},{10,6},{11,7},{4,8},{5,9},... | collective-permute-start | bytes 3072008 | tf_op jit(solution)/shard_map/ppermute | solution.py:450
  65.0 0.9 collective-permute-start.10
  65.9 4.9 %unit.7 = (f32[25,80,128]{2,1,0:T(8,128)S(1)}, s32[1,1]{1,0:T(1,128)}) custom-call(s32[1,1]{1,0:T(1,128)} %get-tuple-element.37.order, f32[40,80,128]{2,1,0:T(8,128)S(1)} %get-tuple-element.38.refs_0_, f32[25,80,128]{2,1,0:T(8,128)S(1)} %pack.1.a.refs_0_.refs_2_.refs_1_, f32[25,80,128]{2,1,0:T(8,128)S(1)} %choose.3.b.refs_2_.refs_0_.refs_5_, ...), custom_call_target="tpu_custom_call" | custom-call | flops 1 | bytes 1 | tf_op jit(solution)/shard_map/unit/pallas_call | solution.py:274
  70.8 0.0 collective-permute-done.8.refs_3_
  70.8 5.6 %unit.8 = (f32[25,80,128]{2,1,0:T(8,128)S(1)}, s32[1,1]{1,0:T(1,128)}) custom-call(s32[1,1]{1,0:T(1,128)} %get-tuple-element.41.order, f32[25,80,128]{2,1,0:T(8,128)S(1)} %choose.3.b.refs_2_.refs_0_.refs_5_, f32[25,80,128]{2,1,0:T(8,128)S(1)} %collective-permute-done.7.refs_1_, f32[25,80,128]{2,1,0:T(8,128)S(1)} %collective-permute-done.3.refs_4_.refs_2_.refs_7_, ...), custom_call_target="tpu_custom_call" | custom-call | flops 1 | bytes 1 | tf_op jit(solution)/shard_map/unit/pallas_call | solution.py:274
  76.4 2.6 %collective-permute-start.11 = (f32[25,80,128]{2,1,0:T(8,128)S(1)}, f32[25,80,128]{2,1,0:T(8,128)S(1)}, u32[]{:S(2)}, u32[]{:S(2)}) collective-permute-start(f32[25,80,128]{2,1,0:T(8,128)S(1)} %get-tuple-element.51), channel_id=1, source_target_pairs={{252,0},{6,2},{0,4},{10,6},{4,8},{14,10},{8,12},{18,14},{12,16},{2... | collective-permute-start | bytes 3072008 | tf_op jit(solution)/shard_map/ppermute | solution.py:417
  79.0 0.0 collective-permute-done.9.refs_0_.refs_3_.refs_4_
  79.0 0.0 collective-permute-done.10.refs_2_
  79.0 5.3 %unit.9 = (f32[25,80,128]{2,1,0:T(8,128)S(1)}, s32[1,1]{1,0:T(1,128)}, f32[25,80,128]{2,1,0:T(8,128)S(1)}) custom-call(s32[1,1]{1,0:T(1,128)} %get-tuple-element.43.order, f32[25,80,128]{2,1,0:T(8,128)S(1)} %collective-permute-done.9.refs_0_.refs_3_.refs_4_, f32[40,80,128]{2,1,0:T(8,128)S(1)} %get-tuple-element.45.refs_1_, ...), custom_call_target="tpu_custom_call" | custom-call | flops 1 | bytes 1 | tf_op jit(solution)/shard_map/unit/pallas_call | solution.py:274
  84.3 5.6 %unit.10 = (f32[25,80,128]{2,1,0:T(8,128)S(1)}, s32[1,1]{1,0:T(1,128)}) custom-call(s32[1,1]{1,0:T(1,128)} %get-tuple-element.47.order, f32[25,80,128]{2,1,0:T(8,128)S(1)} %collective-permute-done.4.refs_3_.a_2.refs_4_.refs_0_, f32[25,80,128]{2,1,0:T(8,128)S(1)} %get-tuple-element.48.refs_1_.refs_2_, ...), custom_call_target="tpu_custom_call" | custom-call | flops 1 | bytes 1 | tf_op jit(solution)/shard_map/unit/pallas_call | solution.py:274
  89.9 0.5 collective-permute-start.12
  90.4 0.1 collective-permute-done.11.refs_0_.returned
  90.5 5.6 %unit.11 = (f32[25,80,128]{2,1,0:T(8,128)S(1)}, s32[1,1]{1,0:T(1,128)}) custom-call(s32[1,1]{1,0:T(1,128)} %get-tuple-element.50.order, f32[25,80,128]{2,1,0:T(8,128)S(1)} %collective-permute-done.11.refs_0_.returned, f32[25,80,128]{2,1,0:T(8,128)S(1)} %pack.1.a.refs_0_.refs_2_.refs_1_, f32[25,80,128]{2,1,0:T(8,128)S(1)} %get-tuple-element.48.refs_1_.refs_2_, ...), custom_call_target="tpu_custom_call" | custom-call | flops 1 | bytes 1 | tf_op jit(solution)/shard_map/unit/pallas_call | solution.py:274
  96.1 0.0 collective-permute-done.12.theirs
  96.2 1.4 %unpack_sum.1 = f32[40,80,80]{2,1,0:T(8,128)} custom-call(f32[25,80,128]{2,1,0:T(8,128)S(1)} %get-tuple-element.53.total, f32[25,80,128]{2,1,0:T(8,128)S(1)} %collective-permute-done.11.refs_0_.returned, f32[25,80,128]{2,1,0:T(8,128)S(1)} %collective-permute-done.12.theirs), custom_call_target="tpu_custom_call" | custom-call | tf_op jit(solution)/shard_map/unpack_sum/pallas_call | solution.py:394
Async XLA Ops:
  0.0 1.4 %copy-start.3 = (f32[1,40,80,80]{3,2,1,0:T(8,128)S(1)}, f32[1,40,80,80]{3,2,1,0:T(8,128)}, u32[]{:S(2)}) copy-start(f32[1,40,80,80]{3,2,1,0:T(8,128)} %param.5) | copy-start | bytes 3072004
  2.4 37.8 %copy-start = (f32[6,41,8,128]{3,2,1,0:T(8,128)S(1)}, f32[6,41,8,128]{3,2,1,0:T(8,128)}, u32[]{:S(2)}) copy-start(f32[6,41,8,128]{3,2,1,0:T(8,128)} %constant.13.clone.refs_9_.refs_8_.refs_7_.refs_11_) | copy-start | bytes 3022852
  2.4 37.8 %copy-start.1 = (bf16[80,240]{1,0:T(8,128)(2,1)S(1)}, bf16[80,240]{1,0:T(8,128)(2,1)}, u32[]{:S(2)}) copy-start(bf16[80,240]{1,0:T(8,128)(2,1)} %constant.10.clone.refs_6_.table_y.refs_5_.refs_4_.refs_8_) | copy-start | bytes 115204
  2.4 37.8 %copy-start.2 = (bf16[80,240]{1,0:T(8,128)(2,1)S(1)}, bf16[80,240]{1,0:T(8,128)(2,1)}, u32[]{:S(2)}) copy-start(bf16[80,240]{1,0:T(8,128)(2,1)} %constant.11.clone.refs_7_.table_to.refs_6_.refs_5_.refs_9_) | copy-start | bytes 115204
  2.4 37.8 %copy-start.4 = (bf16[80,240]{1,0:T(8,128)(2,1)S(1)}, bf16[80,240]{1,0:T(8,128)(2,1)}, u32[]{:S(2)}) copy-start(bf16[80,240]{1,0:T(8,128)(2,1)} %constant.12.clone.refs_8_.refs_7_.refs_6_.refs_10_) | copy-start | bytes 115204
  2.4 25.1 %collective-permute-start = (f32[25,80,128]{2,1,0:T(8,128)S(1)}, f32[25,80,128]{2,1,0:T(8,128)S(1)}, u32[]{:S(2)}, u32[]{:S(2)}) collective-permute-start(f32[25,80,128]{2,1,0:T(8,128)S(1)} %pack.1.a.refs_0_.refs_2_.refs_1_), channel_id=1, source_target_pairs={{0,1},{1,0},{2,3},{3,2},{4,5},{5,4},{6,7},{7,6},{8,9},{9,8},{10,11... | collective-permute-start | bytes 3072008 | tf_op jit(solution)/shard_map/ppermute | solution.py:440
  6.2 24.4 %collective-permute-start.1 = (f32[25,80,128]{2,1,0:T(8,128)S(1)}, f32[25,80,128]{2,1,0:T(8,128)S(1)}, u32[]{:S(2)}, u32[]{:S(2)}) collective-permute-start(f32[25,80,128]{2,1,0:T(8,128)S(1)} %pack.1.a.refs_0_.refs_2_.refs_1_), channel_id=1, source_target_pairs={{4,0},{126,2},{8,4},{2,6},{12,8},{6,10},{16,12},{10,14},{20,16},{1... | collective-permute-start | bytes 3072008 | tf_op jit(solution)/shard_map/ppermute | solution.py:420
  7.5 27.5 %collective-permute-start.2 = (f32[25,80,128]{2,1,0:T(8,128)S(1)}, f32[25,80,128]{2,1,0:T(8,128)S(1)}, u32[]{:S(2)}, u32[]{:S(2)}) collective-permute-start(f32[25,80,128]{2,1,0:T(8,128)S(1)} %pack.1.a.refs_0_.refs_2_.refs_1_), channel_id=1, source_target_pairs={{124,0},{6,2},{0,4},{10,6},{4,8},{14,10},{8,12},{18,14},{12,16},{2... | collective-permute-start | bytes 3072008 | tf_op jit(solution)/shard_map/ppermute | solution.py:420
  14.0 26.1 %collective-permute-start.4 = (f32[25,80,128]{2,1,0:T(8,128)S(1)}, f32[25,80,128]{2,1,0:T(8,128)S(1)}, u32[]{:S(2)}, u32[]{:S(2)}) collective-permute-start(f32[25,80,128]{2,1,0:T(8,128)S(1)} %pack.1.a.refs_0_.refs_2_.refs_1_), channel_id=1, source_target_pairs={{2,0},{0,2},{6,4},{4,6},{10,8},{8,10},{14,12},{12,14},{18,16},{16,... | collective-permute-start | bytes 3072008 | tf_op jit(solution)/shard_map/ppermute | solution.py:417
  35.0 5.2 %collective-permute-start.5 = (f32[25,80,128]{2,1,0:T(8,128)S(1)}, f32[25,80,128]{2,1,0:T(8,128)S(1)}, u32[]{:S(2)}, u32[]{:S(2)}) collective-permute-start(f32[25,80,128]{2,1,0:T(8,128)S(1)} %collective-permute-done.b.refs_1_.refs_4_.refs_3_), channel_id=1, source_target_pairs={{2,0},{0,2},{6,4},{4,6},{10,8},{8,10},{14,12},{12,14},{18,16},{16,... | collective-permute-start | bytes 3072008 | tf_op jit(solution)/shard_map/ppermute | solution.py:417
  37.6 15.3 %collective-permute-start.6 = (f32[25,80,128]{2,1,0:T(8,128)S(1)}, f32[25,80,128]{2,1,0:T(8,128)S(1)}, u32[]{:S(2)}, u32[]{:S(2)}) collective-permute-start(f32[25,80,128]{2,1,0:T(8,128)S(1)} %collective-permute-done.1.b), channel_id=1, source_target_pairs={{130,2},{252,124},{2,130},{124,252},{131,3},{253,125},{3,131},{125... | collective-permute-start | bytes 3072008 | tf_op jit(solution)/shard_map/ppermute | solution.py:430
  40.1 18.9 %collective-permute-start.3 = (f32[25,80,128]{2,1,0:T(8,128)S(1)}, f32[25,80,128]{2,1,0:T(8,128)S(1)}, u32[]{:S(2)}, u32[]{:S(2)}) collective-permute-start(f32[25,80,128]{2,1,0:T(8,128)S(1)} %choose.2), channel_id=1, source_target_pairs={{4,0},{5,1},{255,2},{254,3},{8,4},{9,5},{2,6},{3,7},{12,8},{13,9},... | collective-permute-start | bytes 3072008 | tf_op jit(solution)/shard_map/ppermute | solution.py:446
  53.7 5.3 %collective-permute-start.7 = (f32[25,80,128]{2,1,0:T(8,128)S(1)}, f32[25,80,128]{2,1,0:T(8,128)S(1)}, u32[]{:S(2)}, u32[]{:S(2)}) collective-permute-start(f32[25,80,128]{2,1,0:T(8,128)S(1)} %choose.3.b.refs_2_.refs_0_.refs_5_), channel_id=1, source_target_pairs={{2,0},{0,2},{6,4},{4,6},{10,8},{8,10},{14,12},{12,14},{18,16},{16,... | collective-permute-start | bytes 3072008 | tf_op jit(solution)/shard_map/ppermute | solution.py:417
  59.0 11.9 %collective-permute-start.8 = (f32[25,80,128]{2,1,0:T(8,128)S(1)}, f32[25,80,128]{2,1,0:T(8,128)S(1)}, u32[]{:S(2)}, u32[]{:S(2)}) collective-permute-start(f32[25,80,128]{2,1,0:T(8,128)S(1)} %collective-permute-done.3.refs_4_.refs_2_.refs_7_), channel_id=1, source_target_pairs={{2,0},{0,2},{6,4},{4,6},{10,8},{8,10},{14,12},{12,14},{18,16},{16,... | collective-permute-start | bytes 3072008 | tf_op jit(solution)/shard_map/ppermute | solution.py:417
  59.0 20.1 %collective-permute-start.9 = (f32[25,80,128]{2,1,0:T(8,128)S(1)}, f32[25,80,128]{2,1,0:T(8,128)S(1)}, u32[]{:S(2)}, u32[]{:S(2)}) collective-permute-start(f32[25,80,128]{2,1,0:T(8,128)S(1)} %get-tuple-element.44), channel_id=1, source_target_pairs={{253,0},{252,1},{6,2},{7,3},{0,4},{1,5},{10,6},{11,7},{4,8},{5,9},... | collective-permute-start | bytes 3072008 | tf_op jit(solution)/shard_map/ppermute | solution.py:450
  65.0 14.0 %collective-permute-start.10 = (f32[25,80,128]{2,1,0:T(8,128)S(1)}, f32[25,80,128]{2,1,0:T(8,128)S(1)}, u32[]{:S(2)}, u32[]{:S(2)}) collective-permute-start(f32[25,80,128]{2,1,0:T(8,128)S(1)} %collective-permute-done.2.refs_3_), channel_id=1, source_target_pairs={{128,0},{254,126},{0,128},{126,254},{129,1},{255,127},{1,129},{127... | collective-permute-start | bytes 3072008 | tf_op jit(solution)/shard_map/ppermute | solution.py:430
  76.4 14.1 %collective-permute-start.11 = (f32[25,80,128]{2,1,0:T(8,128)S(1)}, f32[25,80,128]{2,1,0:T(8,128)S(1)}, u32[]{:S(2)}, u32[]{:S(2)}) collective-permute-start(f32[25,80,128]{2,1,0:T(8,128)S(1)} %get-tuple-element.51), channel_id=1, source_target_pairs={{252,0},{6,2},{0,4},{10,6},{4,8},{14,10},{8,12},{18,14},{12,16},{2... | collective-permute-start | bytes 3072008 | tf_op jit(solution)/shard_map/ppermute | solution.py:417
  89.9 6.2 %collective-permute-start.12 = (f32[25,80,128]{2,1,0:T(8,128)S(1)}, f32[25,80,128]{2,1,0:T(8,128)S(1)}, u32[]{:S(2)}, u32[]{:S(2)}) collective-permute-start(f32[25,80,128]{2,1,0:T(8,128)S(1)} %get-tuple-element.54), channel_id=1, source_target_pairs={{2,0},{0,2},{6,4},{4,6},{10,8},{8,10},{14,12},{12,14},{18,16},{16,... | collective-permute-start | bytes 3072008 | tf_op jit(solution)/shard_map/ppermute | solution.py:417
